TPU v7x, 32 devices: a whole 2x2x4 slice. The times are simulated.
32 devices in a mesh: row: 4 (over y, x), col: 8 (over z, core).
Axes of the slice: x: 2, y: 2, z: 4, core: 2. Of those that a mesh axis runs over, the one named last changes fastest.
Arguments:
- cooc: int32 [8192, 16384], P('row', 'col'), may hold values from 0 to 48
- tile_list: int32 [4, 8, 4], P('row', 'col'), may hold values from -1 to 3, as said below
- marginal: int32 [16384], P(('col', 'row')), may hold values from 8 to 524287
- embed: float32 [16384, 256], P(('col', 'row')), may hold values from -1.5 to 1.5
- accum: float32 [16384, 256], P(('col', 'row')), may hold values from 0.001 to 0.01
Outputs:
- new_embed: float32 [16384, 256], P(('col', 'row'))
- new_accum: float32 [16384, 256], P(('col', 'row'))
Inputs may be any that keep to these rules, and one draw needn't show every extreme that they name: `tile_list`: the first entries of each device's list are distinct local tile numbers, the rest are -1; every device lists at least one tile and some device lists all 4.
All inputs are finite; a program needn't handle non-finite values.
Results may differ from a plain program's by a relative error of at most 0.0003.
Values sent between devices are 32-bit elements; how exact they have to be, the bound alone decides.
No kernel may reach another device: no remote copies, remote signals or barrier semaphores. Data moves between devices by JAX's collectives and lax.ppermute only.
A program may use at most 128 MiB of HBM per device.

v0:
```python
import functools

import jax
import jax.numpy as jnp
from jax import lax
from jax.experimental import pallas as pl
from jax.experimental.pallas import tpu as pltpu
from jax.sharding import PartitionSpec as P

BLOCK = 1024
LEARN_RATE = 0.05
SUB = 512
PAD = 8
VMEM_LIMIT = 42 * 2**20


def split_bf16(values):
    high = values.astype(jnp.bfloat16)
    low = (values - high.astype(jnp.float32)).astype(jnp.bfloat16)
    return high, low


def product(left, right, dims):
    (left_at,), (right_at,) = dims
    left = jnp.concatenate([left[0], left[1], left[0]], axis=left_at)
    right = jnp.concatenate([right[0], right[0], right[1]], axis=right_at)
    return lax.dot_general(left, right, (dims, ((), ())), preferred_element_type=jnp.float32)


def half_kernel(k, groups, share, layout, tiles, first, added, ends, last, extra, *refs):
    rest = list(refs)
    take = lambda count: [rest.pop(0) for _ in range(count)]
    place_ref, listed_ref, cooc_ref, mine_ref, theirs_ref = take(5)
    if first:
        pieces = take(len(layout))
    else:
        high_ref, low_ref, log_ref, sums_in = take(4)
    if added:
        (row_in,) = take(1)
    take(extra)
    if ends:
        mine_out, other_out = take(2)
    else:
        (row_out,) = take(1)
    if first:
        high_ref, low_ref, log_ref = take(3)
    if last:
        outs = take(2 * groups)
    else:
        (sums,) = take(1)
    row_vecs, row_logs, cells, cell_sems = take(4)
    if ends:
        (row_out,) = take(1)
    if last:
        (sums,) = take(1)

    depth = row_vecs.shape[1]
    half = share // 2
    quarter = share // 4
    cols = groups * share
    col_blocks = cols // BLOCK
    per = BLOCK // share
    tall = BLOCK // 2
    g = place_ref[0]
    chip = place_ref[1]
    core = place_ref[2]

    def cell_copies(row, col):
        number = tiles.index((row, col))
        return [
            pltpu.make_async_copy(
                cooc_ref.at[pl.ds((row * per + j) * share + k * half, half), pl.ds(col * BLOCK, BLOCK)],
                cells.at[number, pl.ds(j * half, half), :],
                cell_sems.at[number, j],
            )
            for j in range(per)
        ]

    for row, col in tiles:

        @pl.when(listed_ref[row * col_blocks + col] > 0)
        def _():
            for copy in cell_copies(row, col):
                copy.start()

    if first:
        total = jnp.zeros((1, 128), jnp.float32)
        for ref in (mine_ref, theirs_ref):
            for d in range(groups):
                at = d * (quarter + PAD) + quarter + 1
                total = total + ref[at : at + 1, :128]
        log_total = jnp.concatenate([jnp.log(total)] * (depth // 128), axis=1)
        for piece, (other, start, count) in zip(pieces, layout):
            body = min(count, share - start)
            at = pl.multiple_of((g ^ other) * share + start, 16)
            high, low = split_bf16(piece[:body, :])
            high_ref[pl.ds(at, body), :] = high
            low_ref[pl.ds(at, body), :] = low
            if body < count:
                at = pl.multiple_of((g ^ other) * PAD, PAD)
                log_ref[pl.ds(at, PAD), :] = piece[body:, :] - log_total
        sums[...] = jnp.zeros_like(sums)
    else:
        sums[...] = sums_in[...]

    for ref, side in ((mine_ref, core), (theirs_ref, 1 - core)):
        for d in range(groups):
            start = d * (quarter + PAD)
            at = pl.multiple_of((chip ^ d) * half + side * quarter, quarter)
            row_vecs[pl.ds(at, quarter), :] = ref[start : start + quarter, :]
            log_row = ref[start + quarter : start + quarter + 1, :128]
            row_logs[pl.ds(at, quarter), :] = jnp.transpose(jnp.broadcast_to(log_row, (128, 128)))[:quarter, :]
    row_out[...] = row_in[...] if added else jnp.zeros_like(row_out)

    for row, col in tiles:
        tall_rows = slice(row * tall, (row + 1) * tall)

        @pl.when(listed_ref[row * col_blocks + col] > 0)
        def _():
            for copy in cell_copies(row, col):
                copy.wait()
            rows = row_vecs[tall_rows, :]
            row_pair = split_bf16(rows)
            row_turned = split_bf16(jnp.transpose(rows))
            row_log = jnp.concatenate([row_logs[tall_rows, :]] * (SUB // 128), axis=1)
            strips = BLOCK // SUB

            def col_pair(strip):
                at = col * BLOCK + strip * SUB
                return high_ref[at : at + SUB, :], low_ref[at : at + SUB, :]

            def scores(strip):
                return product(row_pair, col_pair(strip), ((1,), (1,)))

            def slopes(strip, values):
                at = col * BLOCK + strip * SUB
                log_rows = [lane // share * PAD + lane % share // depth for lane in range(at, at + SUB, depth)]
                col_log = jnp.concatenate([log_ref[q : q + 1, :] for q in log_rows], axis=1)
                centred = values + row_log + col_log
                counts = cells[tiles.index((row, col)), :, strip * SUB : (strip + 1) * SUB]
                counts_f = counts.astype(jnp.float32)
                floor = jnp.maximum(counts_f, 1.0)
                weights = 0.1 + 0.25 * (counts_f * lax.rsqrt(floor))
                return split_bf16(
                    jnp.where(
                        counts_f > 0,
                        weights * (centred - jnp.log(floor)),
                        0.5 * jnp.tanh(0.5 * centred) + 0.5,
                    )
                )

            def gradients(strip, pair):
                at = col * BLOCK + strip * SUB
                row_out[tall_rows, :] += product(pair, col_pair(strip), ((1,), (0,)))
                sums[:, at : at + SUB] += product(row_turned, pair, ((1,), (0,)))

            ahead = scores(0)
            behind = None
            for strip in range(strips):
                values = ahead
                if strip + 1 < strips:
                    ahead = scores(strip + 1)
                if strip > 0:
                    gradients(strip - 1, behind)
                behind = slopes(strip, values)
            gradients(strips - 1, behind)

    for out, side in ((mine_out, core), (other_out, 1 - core)) if ends else ():
        for d in range(groups):
            at = pl.multiple_of((chip ^ d) * half + side * quarter, quarter)
            out[d * quarter : (d + 1) * quarter, :] = row_out[pl.ds(at, quarter), :]
    if last:
        for other in range(groups):
            at = pl.multiple_of((g ^ other) * share, share)
            block = jnp.transpose(sums[:, pl.ds(at, share)])
            outs[2 * other][...] = block[:half]
            outs[2 * other + 1][...] = block[half:]


def half_grads(k, groups, share, layout, tiles, place, listed, cooc, mine, theirs, held, row_in, ready):
    depth = mine.shape[1]
    cols = groups * share
    first = k == 0
    added = row_in is not None
    ends = tiles[-1] == (cols // BLOCK - 1,) * 2
    last = ends and k == 1
    per = BLOCK // share
    rows = groups * share // 2
    whole = pl.BlockSpec(memory_space=pltpu.VMEM)
    scalar = pl.BlockSpec(memory_space=pltpu.SMEM)
    remote = pl.BlockSpec(memory_space=pl.ANY)
    row_part = jax.ShapeDtypeStruct((rows // 2, depth), jnp.float32)
    row_all = jax.ShapeDtypeStruct((rows, depth), jnp.float32)
    col_half = jax.ShapeDtypeStruct((share // 2, depth), jnp.float32)
    coded = jax.ShapeDtypeStruct((cols, depth), jnp.bfloat16)
    logs = jax.ShapeDtypeStruct((groups * PAD, depth), jnp.float32)
    turned = jax.ShapeDtypeStruct((depth, cols), jnp.float32)
    out_shape = [row_part] * 2 if ends else [row_all]
    out_shape += [coded, coded, logs] if first else []
    out_shape += [col_half] * (2 * groups) if last else [turned]
    held = [*held, row_in] if added else [*held]
    args = [place, listed, cooc, mine, theirs, *held, *ready]
    in_specs = [scalar] * 2 + [remote] + [whole] * (2 + len(held)) + [remote] * len(ready)
    scratch = [
        pltpu.VMEM((rows, depth), jnp.float32),
        pltpu.VMEM((rows, 128), jnp.float32),
        pltpu.VMEM((len(tiles), BLOCK // 2, BLOCK), jnp.int32),
        pltpu.SemaphoreType.DMA((len(tiles), per)),
    ]
    if ends:
        scratch.append(pltpu.VMEM((rows, depth), jnp.float32))
    if last:
        scratch.append(pltpu.VMEM((depth, cols), jnp.float32))
    cells = len(tiles) * BLOCK * BLOCK // 2
    return pl.pallas_call(
        functools.partial(half_kernel, k, groups, share, layout, tiles, first, added, ends, last, len(ready)),
        out_shape=out_shape,
        in_specs=in_specs,
        out_specs=[whole] * len(out_shape),
        scratch_shapes=scratch,
        compiler_params=pltpu.CompilerParams(vmem_limit_bytes=VMEM_LIMIT),
        cost_estimate=pl.CostEstimate(
            flops=cells * depth * 18, bytes_accessed=4 * cells + 8 * cols * depth, transcendentals=3 * cells
        ),
        name="half_grads",
    )(*args)


def local(groups, col_groups, cooc, tile_list, marginal, embed, accum):
    assert col_groups == 2 * groups and groups & (groups - 1) == 0
    both = ("row", "col")
    g = lax.axis_index("row")
    h = lax.axis_index("col")
    chip = h // 2
    core = h % 2
    share, depth = embed.shape
    half = share // 2
    quarter = share // 4
    rows = range(groups)

    def ident(row, at, core):
        return row * col_groups + at * 2 + core

    def permute(value, pairs):
        return lax.ppermute(value, both, pairs)

    def swapped(value, axis, m):
        return lax.ppermute(value, axis, [(r, r ^ m) for r in range(lax.axis_size(axis))])

    def row_swapped(value, m):
        return swapped(value, "row", m)

    def across(value):
        return swapped(value, "col", 1)

    marg_f = marginal.astype(jnp.float32)
    logs = jnp.log(marg_f)

    plane_total = jnp.broadcast_to(jnp.sum(marg_f), (8, 128))
    step = 1
    while step < groups:
        plane_total = plane_total + row_swapped(plane_total, step)
        step *= 2

    tall = quarter + PAD
    came = []
    for c in (0, 1):
        parts = []
        for at in (c * quarter, half + c * quarter):
            under = jnp.pad(logs[at : at + quarter].reshape(1, quarter), ((0, PAD - 1), (0, depth - quarter)))
            parts += [embed[at : at + quarter], under]
        pairs = [(ident(r, q // 2, q % 2), ident(q, r, c)) for q in rows for r in rows]
        came.append(permute(jnp.concatenate(parts, axis=0), pairs))
    came = jnp.where(core == 0, came[0], came[1])
    part_row = lax.broadcasted_iota(jnp.int32, (tall, depth), 0)
    first_part = jnp.where(part_row == quarter + 1, plane_total[0, 0], came[:tall])
    second_part = came[tall:]

    def along_line(part):
        return [part] + [swapped(part, "col", 2 * d) for d in range(1, groups)]

    mine = jnp.concatenate(along_line(first_part), axis=0)
    theirs = across(mine)

    under = jnp.pad(logs.reshape(share // depth, depth), ((0, PAD - share // depth), (0, 0)))
    under = jnp.where(lax.broadcasted_iota(jnp.int32, under.shape, 0) == PAD - 1, plane_total[:, :1], under)
    coded = jnp.concatenate([embed, under], axis=0)
    pieces = {0: [coded]}
    layout = [(0, 0, share + PAD)]
    for m in range(1, groups):
        if m & (m - 1) == 0 or groups != 4:
            pieces[m] = [row_swapped(coded, m)]
            layout.append((m, 0, share + PAD))
    if groups == 4:
        pieces[3] = [row_swapped(pieces[2][0][:half], 1), row_swapped(pieces[1][0][half:], 2)]
        layout += [(3, 0, half), (3, half, half + PAD)]
    held = [pieces[m][start > 0] for m, start, _ in layout]

    listing = tile_list.reshape(-1)
    listed = jnp.sum((listing[None, :] == jnp.arange(listing.shape[0])[:, None]).astype(jnp.int32), axis=1)
    place = jnp.stack([g, chip, core]).astype(jnp.int32)

    def from_line(outs):
        summed = outs[0] + across(outs[1])
        parts = [summed[d * quarter : (d + 1) * quarter] for d in rows]
        total = parts[0]
        for d in range(1, groups):
            total = total + swapped(parts[d], "col", 2 * d)
        return summed, total

    def to_home(total):
        homes = []
        for c in (0, 1):
            homes.append(permute(total, [(ident(q, r, c), ident(r, q // 2, q % 2)) for q in rows for r in rows]))
        return homes

    tiles = [(row, col) for row in range(groups * share // BLOCK) for col in range(groups * share // BLOCK)]
    grads = functools.partial(half_grads, groups=groups, share=share, layout=layout, place=place, listed=listed, cooc=cooc)
    outs = grads(0, tiles=tiles, mine=mine, theirs=theirs, held=held, row_in=None, ready=[])
    first_summed, first_total = from_line(outs)
    parts = along_line(second_part)
    parts[1] = jnp.where(part_row == quarter + 2, outs[0][:tall], parts[1])
    mine = jnp.concatenate(parts, axis=0)
    theirs = across(mine)
    grads = functools.partial(grads, 1, mine=mine, theirs=theirs)
    columns = outs[2:5]
    outs = grads(tiles=tiles[:-1], held=outs[2:], row_in=None, ready=[first_summed])
    outs = grads(tiles=tiles[-1:], held=[*columns, outs[1]], row_in=outs[0], ready=[first_total])
    second_summed, second_total = from_line(outs)
    first_quarters = to_home(first_total)
    quarters = first_quarters + to_home(second_total)

    halves = outs[2:]
    if groups == 4:
        spare = second_summed[:PAD] + first_quarters[0][:PAD] + first_quarters[1][:PAD]
        first_x = row_swapped(jnp.concatenate([halves[2], halves[6], spare], axis=0), 1)[: 2 * half]
        first_y = row_swapped(jnp.concatenate([halves[5], halves[7], spare], axis=0), 2)[: 2 * half]
        second_x = row_swapped(halves[3] + first_y[half:], 1)
        second_y = row_swapped(halves[4] + first_x[half:], 2)
        top = halves[0] + first_x[:half] + second_y
        bottom = halves[1] + second_x + first_y[:half]
    else:
        top, bottom = halves[:2]
        for m in range(1, groups):
            top = top + row_swapped(halves[2 * m], m)
            bottom = bottom + row_swapped(halves[2 * m + 1], m)
    gradients = (jnp.concatenate([top, bottom], axis=0) + jnp.concatenate(quarters, axis=0)) / BLOCK
    new_accum = accum + gradients * gradients
    new_embed = embed - LEARN_RATE * gradients / jnp.sqrt(new_accum)
    return (new_embed, new_accum)


def solution(mesh):
    placed = (
        P("row", "col"),
        P("row", "col", None),
        P(("col", "row")),
        P(("col", "row"), None),
        P(("col", "row"), None),
    )
    return jax.shard_map(
        functools.partial(local, mesh.shape["row"], mesh.shape["col"]),
        mesh=mesh,
        in_specs=placed,
        out_specs=(P(("col", "row"), None), P(("col", "row"), None)),
        check_vma=False,
    )
```

profile of v0, /device:TPU:2, one launch (start us, length us, event | category | flops | bytes accessed | tf_op | source)
XLA Modules:
  0.0 143.4 jit_solution(9844723499781514708)
XLA Ops:
  0.6 1.3 convert_reduce_fusion
  2.0 1.1 fusion.10
  3.2 2.9 %collective-permute-start.1 = (f32[272,256]{1,0:T(8,128)S(1)}, f32[272,256]{1,0:T(8,128)S(1)}, u32[]{:S(2)}, u32[]{:S(2)}) collective-permute-start(f32[272,256]{1,0:T(8,128)S(1)} %select_maximum_fusion), channel_id=1, source_target_pairs={{0,1},{8,3},{16,5},{24,7},{1,9},{9,11},{17,13},{25,15},{2,17},{10,... | collective-permute-start | bytes 835592 | tf_op jit(solution)/shard_map/ppermute | solution.py:245
  6.1 3.3 %collective-permute-start = (f32[272,256]{1,0:T(8,128)S(1)}, f32[272,256]{1,0:T(8,128)S(1)}, u32[]{:S(2)}, u32[]{:S(2)}) collective-permute-start(f32[272,256]{1,0:T(8,128)S(1)} %select_maximum_fusion.2), channel_id=1, source_target_pairs={{0,0},{8,2},{16,4},{24,6},{1,8},{9,10},{17,12},{25,14},{2,16},{10,... | collective-permute-start | bytes 835592 | tf_op jit(solution)/shard_map/ppermute | solution.py:245
  10.2 6.5 %collective-permute-done.2 = f32[8,128]{0,1:T(8,128)S(1)} collective-permute-done((f32[8,128]{0,1:T(8,128)S(1)}, f32[8,128]{0,1:T(8,128)S(1)}, u32[]{:S(2)}, u32[]{:S(2)}) %collective-permute-start.2) | collective-permute-done | bytes 4128 | tf_op jit(solution)/shard_map/ppermute | solution.py:248
  17.4 4.2 %collective-permute-done.3 = f32[8,128]{0,1:T(8,128)S(1)} collective-permute-done((f32[8,128]{0,1:T(8,128)S(1)}, f32[8,128]{0,1:T(8,128)S(1)}, u32[]{:S(2)}, u32[]{:S(2)}) %collective-permute-start.3) | collective-permute-done | bytes 4128 | tf_op jit(solution)/shard_map/ppermute | solution.py:248
  24.7 7.5 %collective-permute-start.4 = (f32[136,256]{1,0:T(8,128)S(1)}, f32[136,256]{1,0:T(8,128)S(1)}, u32[]{:S(2)}, u32[]{:S(2)}) collective-permute-start(f32[136,256]{1,0:T(8,128)S(1)} %get-tuple-element.50), channel_id=1, source_target_pairs={{0,2},{1,3},{2,0},{3,1},{4,6},{5,7},{6,4},{7,5},{8,10},{9,11},{10,... | collective-permute-start | bytes 417800 | tf_op jit(solution)/shard_map/ppermute | solution.py:248
  32.2 2.4 %collective-permute-start.6 = (f32[136,256]{1,0:T(8,128)S(1)}, f32[136,256]{1,0:T(8,128)S(1)}, u32[]{:S(2)}, u32[]{:S(2)}) collective-permute-start(f32[136,256]{1,0:T(8,128)S(1)} %get-tuple-element.50), channel_id=1, source_target_pairs={{0,6},{1,7},{2,4},{3,5},{4,2},{5,3},{6,0},{7,1},{8,14},{9,15},{10,... | collective-permute-start | bytes 417800 | tf_op jit(solution)/shard_map/ppermute | solution.py:248
  34.7 1.9 %collective-permute-done.4 = f32[136,256]{1,0:T(8,128)S(1)} collective-permute-done((f32[136,256]{1,0:T(8,128)S(1)}, f32[136,256]{1,0:T(8,128)S(1)}, u32[]{:S(2)}, u32[]{:S(2)}) %collective-permute-start.4) | collective-permute-done | bytes 139296 | tf_op jit(solution)/shard_map/ppermute | solution.py:248
  36.5 4.5 %collective-permute-done.5 = f32[136,256]{1,0:T(8,128)S(1)} collective-permute-done((f32[136,256]{1,0:T(8,128)S(1)}, f32[136,256]{1,0:T(8,128)S(1)}, u32[]{:S(2)}, u32[]{:S(2)}) %collective-permute-start.5) | collective-permute-done | bytes 139296 | tf_op jit(solution)/shard_map/ppermute | solution.py:248
  41.9 6.1 %collective-permute-start.11 = (f32[264,256]{1,0:T(8,128)}, f32[264,256]{1,0:T(8,128)S(1)}, u32[]{:S(2)}, u32[]{:S(2)}) collective-permute-start(f32[264,256]{1,0:T(8,128)} %slice.131), channel_id=1, source_target_pairs={{0,16},{8,24},{16,0},{24,8},{1,17},{9,25},{17,1},{25,9},{2,18},{10... | collective-permute-start | bytes 811016 | tf_op jit(solution)/shard_map/ppermute | solution.py:248
  49.7 3.3 %collective-permute-start.12 = (f32[136,256]{1,0:T(8,128)S(1)}, f32[136,256]{1,0:T(8,128)S(1)}, u32[]{:S(2)}, u32[]{:S(2)}) collective-permute-start(f32[136,256]{1,0:T(8,128)S(1)} %get-tuple-element.51), channel_id=1, source_target_pairs={{0,2},{1,3},{2,0},{3,1},{4,6},{5,7},{6,4},{7,5},{8,10},{9,11},{10,... | collective-permute-start | bytes 417800 | tf_op jit(solution)/shard_map/ppermute | solution.py:248
  53.0 4.3 %collective-permute-done.10.refs_8_ = f32[256,256]{1,0:T(8,128)S(1)} collective-permute-done((f32[256,256]{1,0:T(8,128)}, f32[256,256]{1,0:T(8,128)S(1)}, u32[]{:S(2)}, u32[]{:S(2)}) %collective-permute-start.10) | collective-permute-done | bytes 262176 | tf_op jit(solution)/shard_map/ppermute | solution.py:248
  57.3 2.8 %collective-permute-start.14 = (f32[136,256]{1,0:T(8,128)S(1)}, f32[136,256]{1,0:T(8,128)S(1)}, u32[]{:S(2)}, u32[]{:S(2)}) collective-permute-start(f32[136,256]{1,0:T(8,128)S(1)} %get-tuple-element.51), channel_id=1, source_target_pairs={{0,6},{1,7},{2,4},{3,5},{4,2},{5,3},{6,0},{7,1},{8,14},{9,15},{10,... | collective-permute-start | bytes 417800 | tf_op jit(solution)/shard_map/ppermute | solution.py:248
  60.1 16.7 %half_grads.3 = (f32[512,256]{1,0:T(8,128)S(1)}, f32[512,256]{1,0:T(8,128)S(1)}, bf16[2048,256]{1,0:T(8,128)(2,1)S(1)}, bf16[2048,256]{1,0:T(8,128)(2,1)S(1)}, f...) custom-call(s32[3]{0:T(128)S(1)} %pad_add_fusion.refs_0_, s32[4]{0:T(128)S(1)} %convert_reduce_fusion.1.refs_1_, ...), custom_call_target="tpu_custom_call" | custom-call | flops 9663676416 | bytes 12582912 | tf_op jit(solution)/shard_map/half_grads/pallas_call | solution.py:215
  77.6 1.2 collective-permute-done.16
  79.0 4.3 %collective-permute-start.19 = (f32[128,256]{1,0:T(8,128)S(1)}, f32[128,256]{1,0:T(8,128)S(1)}, u32[]{:S(2)}, u32[]{:S(2)}) collective-permute-start(f32[128,256]{1,0:T(8,128)S(1)} %get-tuple-element.44), channel_id=1, source_target_pairs={{0,6},{1,7},{2,4},{3,5},{4,2},{5,3},{6,0},{7,1},{8,14},{9,15},{10,... | collective-permute-start | bytes 393224 | tf_op jit(solution)/shard_map/ppermute | solution.py:248
  83.3 13.1 %half_grads.4 = (f32[1024,256]{1,0:T(8,128)S(1)}, f32[256,2048]{1,0:T(8,128)S(1)}) custom-call(s32[3]{0:T(128)S(1)} %pad_add_fusion.refs_0_, s32[4]{0:T(128)S(1)} %convert_reduce_fusion.1.refs_1_, s32[2048,2048]{1,0:T(8,128)} %refs_2_.5, f32[544,256]{1,0:T(8,128)S(1)} %pad_maximum_fusion.3.refs_3_, f32[544,256]{1,0:T(8,128)S(1)} %collective-permute-done.15.refs_4_, ...), custom_call_target="tpu_custom_call" | custom-call | flops 7247757312 | bytes 10485760 | tf_op jit(solution)/shard_map/half_grads/pallas_call | solution.py:215
  96.5 6.4 %half_grads.5 = (f32[512,256]{1,0:T(8,128)S(1)}, f32[512,256]{1,0:T(8,128)S(1)}, f32[256,256]{1,0:T(8,128)S(1)}, f32[256,256]{1,0:T(8,128)S(1)}, f32[256,256]{1,...) custom-call(s32[3]{0:T(128)S(1)} %pad_add_fusion.refs_0_, ...), custom_call_target="tpu_custom_call" | custom-call | flops 2415919104 | bytes 6291456 | tf_op jit(solution)/shard_map/half_grads/pallas_call | solution.py:215
  103.0 1.9 %collective-permute-start.21 = (f32[128,256]{1,0:T(8,128)S(1)}, f32[128,256]{1,0:T(8,128)S(1)}, u32[]{:S(2)}, u32[]{:S(2)}) collective-permute-start(f32[128,256]{1,0:T(8,128)S(1)} %fusion.7.refs_10_), channel_id=1, source_target_pairs={{0,0},{2,8},{4,16},{6,24},{8,1},{10,9},{12,17},{14,25},{16,2},{18,... | collective-permute-start | bytes 393224 | tf_op jit(solution)/shard_map/ppermute | solution.py:245
  104.9 1.3 collective-permute-start.22
  106.3 4.4 %collective-permute-done.21 = f32[128,256]{1,0:T(8,128)S(1)} collective-permute-done((f32[128,256]{1,0:T(8,128)S(1)}, f32[128,256]{1,0:T(8,128)S(1)}, u32[]{:S(2)}, u32[]{:S(2)}) %collective-permute-start.21) | collective-permute-done | bytes 131104 | tf_op jit(solution)/shard_map/ppermute | solution.py:245
  110.8 1.4 collective-permute-done.22
  112.4 3.4 %collective-permute-start.27 = (f32[128,256]{1,0:T(8,128)S(1)}, f32[128,256]{1,0:T(8,128)S(1)}, u32[]{:S(2)}, u32[]{:S(2)}) collective-permute-start(f32[128,256]{1,0:T(8,128)S(1)} %get-tuple-element.40), channel_id=1, source_target_pairs={{0,2},{1,3},{2,0},{3,1},{4,6},{5,7},{6,4},{7,5},{8,10},{9,11},{10,... | collective-permute-start | bytes 393224 | tf_op jit(solution)/shard_map/ppermute | solution.py:248
  115.8 2.4 %collective-permute-start.29 = (f32[128,256]{1,0:T(8,128)S(1)}, f32[128,256]{1,0:T(8,128)S(1)}, u32[]{:S(2)}, u32[]{:S(2)}) collective-permute-start(f32[128,256]{1,0:T(8,128)S(1)} %get-tuple-element.41), channel_id=1, source_target_pairs={{0,6},{1,7},{2,4},{3,5},{4,2},{5,3},{6,0},{7,1},{8,14},{9,15},{10,... | collective-permute-start | bytes 393224 | tf_op jit(solution)/shard_map/ppermute | solution.py:248
  118.3 7.3 %collective-permute-done.23 = f32[520,256]{1,0:T(8,128)S(1)} collective-permute-done((f32[520,256]{1,0:T(8,128)S(1)}, f32[520,256]{1,0:T(8,128)S(1)}, u32[]{:S(2)}, u32[]{:S(2)}) %collective-permute-start.23) | collective-permute-done | bytes 532512 | tf_op jit(solution)/shard_map/ppermute | solution.py:248
  126.0 1.5 %collective-permute-start.26 = (f32[256,256]{1,0:T(8,128)S(1)}, f32[256,256]{1,0:T(8,128)S(1)}, u32[]{:S(2)}, u32[]{:S(2)}) collective-permute-start(f32[256,256]{1,0:T(8,128)S(1)} %slice_add_fusion.1), channel_id=1, source_target_pairs={{0,8},{8,0},{16,24},{24,16},{1,9},{9,1},{17,25},{25,17},{2,10},{10... | collective-permute-start | bytes 786440 | tf_op jit(solution)/shard_map/ppermute | solution.py:248
  127.5 1.9 %collective-permute-start.30 = (f32[128,256]{1,0:T(8,128)S(1)}, f32[128,256]{1,0:T(8,128)S(1)}, u32[]{:S(2)}, u32[]{:S(2)}) collective-permute-start(f32[128,256]{1,0:T(8,128)S(1)} %fusion.5), channel_id=1, source_target_pairs={{0,0},{2,8},{4,16},{6,24},{8,1},{10,9},{12,17},{14,25},{16,2},{18,... | collective-permute-start | bytes 393224 | tf_op jit(solution)/shard_map/ppermute | solution.py:245
  129.5 1.3 collective-permute-start.31
  130.8 1.5 %collective-permute-done.24 = f32[256,256]{1,0:T(8,128)S(1)} collective-permute-done((f32[256,256]{1,0:T(8,128)S(1)}, f32[256,256]{1,0:T(8,128)S(1)}, u32[]{:S(2)}, u32[]{:S(2)}) %collective-permute-start.24) | collective-permute-done | bytes 262176 | tf_op jit(solution)/shard_map/ppermute | solution.py:248
  133.4 7.3 %collective-permute-done.30 = f32[128,256]{1,0:T(8,128)S(1)} collective-permute-done((f32[128,256]{1,0:T(8,128)S(1)}, f32[128,256]{1,0:T(8,128)S(1)}, u32[]{:S(2)}, u32[]{:S(2)}) %collective-permute-start.30) | collective-permute-done | bytes 131104 | tf_op jit(solution)/shard_map/ppermute | solution.py:245
  140.7 1.6 %collective-permute-done.31 = f32[128,256]{1,0:T(8,128)S(1)} collective-permute-done((f32[128,256]{1,0:T(8,128)S(1)}, f32[128,256]{1,0:T(8,128)S(1)}, u32[]{:S(2)}, u32[]{:S(2)}) %collective-permute-start.31) | collective-permute-done | bytes 131104 | tf_op jit(solution)/shard_map/ppermute | solution.py:245
  (81 shorter events, 11.2 us)
Async XLA Ops:
  3.2 20.8 %collective-permute-start.1 = (f32[272,256]{1,0:T(8,128)S(1)}, f32[272,256]{1,0:T(8,128)S(1)}, u32[]{:S(2)}, u32[]{:S(2)}) collective-permute-start(f32[272,256]{1,0:T(8,128)S(1)} %select_maximum_fusion), channel_id=1, source_target_pairs={{0,1},{8,3},{16,5},{24,7},{1,9},{9,11},{17,13},{25,15},{2,17},{10,... | collective-permute-start | bytes 835592 | tf_op jit(solution)/shard_map/ppermute | solution.py:245
  6.1 17.8 %collective-permute-start = (f32[272,256]{1,0:T(8,128)S(1)}, f32[272,256]{1,0:T(8,128)S(1)}, u32[]{:S(2)}, u32[]{:S(2)}) collective-permute-start(f32[272,256]{1,0:T(8,128)S(1)} %select_maximum_fusion.2), channel_id=1, source_target_pairs={{0,0},{8,2},{16,4},{24,6},{1,8},{9,10},{17,12},{25,14},{2,16},{10,... | collective-permute-start | bytes 835592 | tf_op jit(solution)/shard_map/ppermute | solution.py:245
  10.1 6.6 %collective-permute-start.2 = (f32[8,128]{0,1:T(8,128)S(1)}, f32[8,128]{0,1:T(8,128)S(1)}, u32[]{:S(2)}, u32[]{:S(2)}) collective-permute-start(f32[8,128]{0,1:T(8,128)S(1)} %broadcast_in_dim.18), channel_id=1, source_target_pairs={{0,8},{8,0},{16,24},{24,16},{1,9},{9,1},{17,25},{25,17},{2,10},{10... | collective-permute-start | bytes 12296 | tf_op jit(solution)/shard_map/ppermute | solution.py:248
  17.3 4.3 %collective-permute-start.3 = (f32[8,128]{0,1:T(8,128)S(1)}, f32[8,128]{0,1:T(8,128)S(1)}, u32[]{:S(2)}, u32[]{:S(2)}) collective-permute-start(f32[8,128]{0,1:T(8,128)S(1)} %broadcast_add_fusion), channel_id=1, source_target_pairs={{0,16},{8,24},{16,0},{24,8},{1,17},{9,25},{17,1},{25,9},{2,18},{10... | collective-permute-start | bytes 12296 | tf_op jit(solution)/shard_map/ppermute | solution.py:248
  22.9 18.2 %collective-permute-start.8 = (f32[520,256]{1,0:T(8,128)S(1)}, f32[520,256]{1,0:T(8,128)S(1)}, u32[]{:S(2)}, u32[]{:S(2)}) collective-permute-start(f32[520,256]{1,0:T(8,128)S(1)} %pad_maximum_fusion.4.refs_5_), channel_id=1, source_target_pairs={{0,8},{8,0},{16,24},{24,16},{1,9},{9,1},{17,25},{25,17},{2,10},{10... | collective-permute-start | bytes 1597448 | tf_op jit(solution)/shard_map/ppermute | solution.py:248
  23.0 25.0 %collective-permute-start.9 = (f32[520,256]{1,0:T(8,128)S(1)}, f32[520,256]{1,0:T(8,128)S(1)}, u32[]{:S(2)}, u32[]{:S(2)}) collective-permute-start(f32[520,256]{1,0:T(8,128)S(1)} %pad_maximum_fusion.4.refs_5_), channel_id=1, source_target_pairs={{0,16},{8,24},{16,0},{24,8},{1,17},{9,25},{17,1},{25,9},{2,18},{10... | collective-permute-start | bytes 1597448 | tf_op jit(solution)/shard_map/ppermute | solution.py:248
  24.7 11.8 %collective-permute-start.4 = (f32[136,256]{1,0:T(8,128)S(1)}, f32[136,256]{1,0:T(8,128)S(1)}, u32[]{:S(2)}, u32[]{:S(2)}) collective-permute-start(f32[136,256]{1,0:T(8,128)S(1)} %get-tuple-element.50), channel_id=1, source_target_pairs={{0,2},{1,3},{2,0},{3,1},{4,6},{5,7},{6,4},{7,5},{8,10},{9,11},{10,... | collective-permute-start | bytes 417800 | tf_op jit(solution)/shard_map/ppermute | solution.py:248
  32.2 8.8 %collective-permute-start.5 = (f32[136,256]{1,0:T(8,128)S(1)}, f32[136,256]{1,0:T(8,128)S(1)}, u32[]{:S(2)}, u32[]{:S(2)}) collective-permute-start(f32[136,256]{1,0:T(8,128)S(1)} %get-tuple-element.50), channel_id=1, source_target_pairs={{0,4},{1,5},{2,6},{3,7},{4,0},{5,1},{6,2},{7,3},{8,12},{9,13},{10,... | collective-permute-start | bytes 417800 | tf_op jit(solution)/shard_map/ppermute | solution.py:248
  32.2 8.8 %collective-permute-start.6 = (f32[136,256]{1,0:T(8,128)S(1)}, f32[136,256]{1,0:T(8,128)S(1)}, u32[]{:S(2)}, u32[]{:S(2)}) collective-permute-start(f32[136,256]{1,0:T(8,128)S(1)} %get-tuple-element.50), channel_id=1, source_target_pairs={{0,6},{1,7},{2,4},{3,5},{4,2},{5,3},{6,0},{7,1},{8,14},{9,15},{10,... | collective-permute-start | bytes 417800 | tf_op jit(solution)/shard_map/ppermute | solution.py:248
  41.1 19.1 %collective-permute-start.7 = (f32[544,256]{1,0:T(8,128)S(1)}, f32[544,256]{1,0:T(8,128)S(1)}, u32[]{:S(2)}, u32[]{:S(2)}) collective-permute-start(f32[544,256]{1,0:T(8,128)S(1)} %pad_maximum_fusion.2.refs_3_), channel_id=1, source_target_pairs={{0,1},{1,0},{2,3},{3,2},{4,5},{5,4},{6,7},{7,6},{8,9},{9,8},{10,11... | collective-permute-start | bytes 1671176 | tf_op jit(solution)/shard_map/ppermute | solution.py:248
  41.9 18.2 %collective-permute-start.11 = (f32[264,256]{1,0:T(8,128)}, f32[264,256]{1,0:T(8,128)S(1)}, u32[]{:S(2)}, u32[]{:S(2)}) collective-permute-start(f32[264,256]{1,0:T(8,128)} %slice.131), channel_id=1, source_target_pairs={{0,16},{8,24},{16,0},{24,8},{1,17},{9,25},{17,1},{25,9},{2,18},{10... | collective-permute-start | bytes 811016 | tf_op jit(solution)/shard_map/ppermute | solution.py:248
  48.7 8.6 %collective-permute-start.10 = (f32[256,256]{1,0:T(8,128)}, f32[256,256]{1,0:T(8,128)S(1)}, u32[]{:S(2)}, u32[]{:S(2)}) collective-permute-start(f32[256,256]{1,0:T(8,128)} %slice.130), channel_id=1, source_target_pairs={{0,8},{8,0},{16,24},{24,16},{1,9},{9,1},{17,25},{25,17},{2,10},{10... | collective-permute-start | bytes 786440 | tf_op jit(solution)/shard_map/ppermute | solution.py:248
  49.7 27.2 %collective-permute-start.12 = (f32[136,256]{1,0:T(8,128)S(1)}, f32[136,256]{1,0:T(8,128)S(1)}, u32[]{:S(2)}, u32[]{:S(2)}) collective-permute-start(f32[136,256]{1,0:T(8,128)S(1)} %get-tuple-element.51), channel_id=1, source_target_pairs={{0,2},{1,3},{2,0},{3,1},{4,6},{5,7},{6,4},{7,5},{8,10},{9,11},{10,... | collective-permute-start | bytes 417800 | tf_op jit(solution)/shard_map/ppermute | solution.py:248
  53.0 24.0 %collective-permute-start.13 = (f32[136,256]{1,0:T(8,128)S(1)}, f32[136,256]{1,0:T(8,128)S(1)}, u32[]{:S(2)}, u32[]{:S(2)}) collective-permute-start(f32[136,256]{1,0:T(8,128)S(1)} %get-tuple-element.51), channel_id=1, source_target_pairs={{0,4},{1,5},{2,6},{3,7},{4,0},{5,1},{6,2},{7,3},{8,12},{9,13},{10,... | collective-permute-start | bytes 417800 | tf_op jit(solution)/shard_map/ppermute | solution.py:248
  57.3 19.7 %collective-permute-start.14 = (f32[136,256]{1,0:T(8,128)S(1)}, f32[136,256]{1,0:T(8,128)S(1)}, u32[]{:S(2)}, u32[]{:S(2)}) collective-permute-start(f32[136,256]{1,0:T(8,128)S(1)} %get-tuple-element.51), channel_id=1, source_target_pairs={{0,6},{1,7},{2,4},{3,5},{4,2},{5,3},{6,0},{7,1},{8,14},{9,15},{10,... | collective-permute-start | bytes 417800 | tf_op jit(solution)/shard_map/ppermute | solution.py:248
  76.8 2.0 %collective-permute-start.16 = (f32[512,256]{1,0:T(8,128)S(1)}, f32[512,256]{1,0:T(8,128)S(1)}, u32[]{:S(2)}, u32[]{:S(2)}) collective-permute-start(f32[512,256]{1,0:T(8,128)S(1)} %get-tuple-element.25), channel_id=1, source_target_pairs={{0,1},{1,0},{2,3},{3,2},{4,5},{5,4},{6,7},{7,6},{8,9},{9,8},{10,11... | collective-permute-start | bytes 1572872 | tf_op jit(solution)/shard_map/ppermute | solution.py:248
  77.1 6.3 %collective-permute-start.15 = (f32[544,256]{1,0:T(8,128)S(1)}, f32[544,256]{1,0:T(8,128)S(1)}, u32[]{:S(2)}, u32[]{:S(2)}) collective-permute-start(f32[544,256]{1,0:T(8,128)S(1)} %pad_maximum_fusion.3.refs_3_), channel_id=1, source_target_pairs={{0,1},{1,0},{2,3},{3,2},{4,5},{5,4},{6,7},{7,6},{8,9},{9,8},{10,11... | collective-permute-start | bytes 1671176 | tf_op jit(solution)/shard_map/ppermute | solution.py:248
  78.9 17.5 %collective-permute-start.17 = (f32[128,256]{1,0:T(8,128)S(1)}, f32[128,256]{1,0:T(8,128)S(1)}, u32[]{:S(2)}, u32[]{:S(2)}) collective-permute-start(f32[128,256]{1,0:T(8,128)S(1)} %get-tuple-element.43), channel_id=1, source_target_pairs={{0,2},{1,3},{2,0},{3,1},{4,6},{5,7},{6,4},{7,5},{8,10},{9,11},{10,... | collective-permute-start | bytes 393224 | tf_op jit(solution)/shard_map/ppermute | solution.py:248
  79.0 17.5 %collective-permute-start.18 = (f32[128,256]{1,0:T(8,128)S(1)}, f32[128,256]{1,0:T(8,128)S(1)}, u32[]{:S(2)}, u32[]{:S(2)}) collective-permute-start(f32[128,256]{1,0:T(8,128)S(1)} %get-tuple-element.45), channel_id=1, source_target_pairs={{0,4},{1,5},{2,6},{3,7},{4,0},{5,1},{6,2},{7,3},{8,12},{9,13},{10,... | collective-permute-start | bytes 393224 | tf_op jit(solution)/shard_map/ppermute | solution.py:248
  79.0 17.4 %collective-permute-start.19 = (f32[128,256]{1,0:T(8,128)S(1)}, f32[128,256]{1,0:T(8,128)S(1)}, u32[]{:S(2)}, u32[]{:S(2)}) collective-permute-start(f32[128,256]{1,0:T(8,128)S(1)} %get-tuple-element.44), channel_id=1, source_target_pairs={{0,6},{1,7},{2,4},{3,5},{4,2},{5,3},{6,0},{7,1},{8,14},{9,15},{10,... | collective-permute-start | bytes 393224 | tf_op jit(solution)/shard_map/ppermute | solution.py:248
  102.9 3.3 %collective-permute-start.20 = (f32[512,256]{1,0:T(8,128)S(1)}, f32[512,256]{1,0:T(8,128)S(1)}, u32[]{:S(2)}, u32[]{:S(2)}) collective-permute-start(f32[512,256]{1,0:T(8,128)S(1)} %get-tuple-element.32), channel_id=1, source_target_pairs={{0,1},{1,0},{2,3},{3,2},{4,5},{5,4},{6,7},{7,6},{8,9},{9,8},{10,11... | collective-permute-start | bytes 1572872 | tf_op jit(solution)/shard_map/ppermute | solution.py:248
  103.0 7.8 %collective-permute-start.21 = (f32[128,256]{1,0:T(8,128)S(1)}, f32[128,256]{1,0:T(8,128)S(1)}, u32[]{:S(2)}, u32[]{:S(2)}) collective-permute-start(f32[128,256]{1,0:T(8,128)S(1)} %fusion.7.refs_10_), channel_id=1, source_target_pairs={{0,0},{2,8},{4,16},{6,24},{8,1},{10,9},{12,17},{14,25},{16,2},{18,... | collective-permute-start | bytes 393224 | tf_op jit(solution)/shard_map/ppermute | solution.py:245
  104.9 7.2 %collective-permute-start.22 = (f32[128,256]{1,0:T(8,128)S(1)}, f32[128,256]{1,0:T(8,128)S(1)}, u32[]{:S(2)}, u32[]{:S(2)}) collective-permute-start(f32[128,256]{1,0:T(8,128)S(1)} %fusion.7.refs_10_), channel_id=1, source_target_pairs={{1,0},{3,8},{5,16},{7,24},{9,1},{11,9},{13,17},{15,25},{17,2},{19,... | collective-permute-start | bytes 393224 | tf_op jit(solution)/shard_map/ppermute | solution.py:245
  112.2 13.4 %collective-permute-start.23 = (f32[520,256]{1,0:T(8,128)S(1)}, f32[520,256]{1,0:T(8,128)S(1)}, u32[]{:S(2)}, u32[]{:S(2)}) collective-permute-start(f32[520,256]{1,0:T(8,128)S(1)} %get-tuple-element.52), channel_id=1, source_target_pairs={{0,8},{8,0},{16,24},{24,16},{1,9},{9,1},{17,25},{25,17},{2,10},{10... | collective-permute-start | bytes 1597448 | tf_op jit(solution)/shard_map/ppermute | solution.py:248
  112.3 13.6 %collective-permute-start.25 = (f32[520,256]{1,0:T(8,128)S(1)}, f32[520,256]{1,0:T(8,128)S(1)}, u32[]{:S(2)}, u32[]{:S(2)}) collective-permute-start(f32[520,256]{1,0:T(8,128)S(1)} %get-tuple-element.53), channel_id=1, source_target_pairs={{0,16},{8,24},{16,0},{24,8},{1,17},{9,25},{17,1},{25,9},{2,18},{10... | collective-permute-start | bytes 1597448 | tf_op jit(solution)/shard_map/ppermute | solution.py:248
  112.4 15.1 %collective-permute-start.27 = (f32[128,256]{1,0:T(8,128)S(1)}, f32[128,256]{1,0:T(8,128)S(1)}, u32[]{:S(2)}, u32[]{:S(2)}) collective-permute-start(f32[128,256]{1,0:T(8,128)S(1)} %get-tuple-element.40), channel_id=1, source_target_pairs={{0,2},{1,3},{2,0},{3,1},{4,6},{5,7},{6,4},{7,5},{8,10},{9,11},{10,... | collective-permute-start | bytes 393224 | tf_op jit(solution)/shard_map/ppermute | solution.py:248
  115.8 11.7 %collective-permute-start.28 = (f32[128,256]{1,0:T(8,128)S(1)}, f32[128,256]{1,0:T(8,128)S(1)}, u32[]{:S(2)}, u32[]{:S(2)}) collective-permute-start(f32[128,256]{1,0:T(8,128)S(1)} %get-tuple-element.42), channel_id=1, source_target_pairs={{0,4},{1,5},{2,6},{3,7},{4,0},{5,1},{6,2},{7,3},{8,12},{9,13},{10,... | collective-permute-start | bytes 393224 | tf_op jit(solution)/shard_map/ppermute | solution.py:248
  115.8 11.7 %collective-permute-start.29 = (f32[128,256]{1,0:T(8,128)S(1)}, f32[128,256]{1,0:T(8,128)S(1)}, u32[]{:S(2)}, u32[]{:S(2)}) collective-permute-start(f32[128,256]{1,0:T(8,128)S(1)} %get-tuple-element.41), channel_id=1, source_target_pairs={{0,6},{1,7},{2,4},{3,5},{4,2},{5,3},{6,0},{7,1},{8,14},{9,15},{10,... | collective-permute-start | bytes 393224 | tf_op jit(solution)/shard_map/ppermute | solution.py:248
  125.7 6.7 %collective-permute-start.24 = (f32[256,256]{1,0:T(8,128)S(1)}, f32[256,256]{1,0:T(8,128)S(1)}, u32[]{:S(2)}, u32[]{:S(2)}) collective-permute-start(f32[256,256]{1,0:T(8,128)S(1)} %slice_add_fusion.2), channel_id=1, source_target_pairs={{0,16},{8,24},{16,0},{24,8},{1,17},{9,25},{17,1},{25,9},{2,18},{10... | collective-permute-start | bytes 786440 | tf_op jit(solution)/shard_map/ppermute | solution.py:248
  126.0 7.3 %collective-permute-start.26 = (f32[256,256]{1,0:T(8,128)S(1)}, f32[256,256]{1,0:T(8,128)S(1)}, u32[]{:S(2)}, u32[]{:S(2)}) collective-permute-start(f32[256,256]{1,0:T(8,128)S(1)} %slice_add_fusion.1), channel_id=1, source_target_pairs={{0,8},{8,0},{16,24},{24,16},{1,9},{9,1},{17,25},{25,17},{2,10},{10... | collective-permute-start | bytes 786440 | tf_op jit(solution)/shard_map/ppermute | solution.py:248
  127.5 13.2 %collective-permute-start.30 = (f32[128,256]{1,0:T(8,128)S(1)}, f32[128,256]{1,0:T(8,128)S(1)}, u32[]{:S(2)}, u32[]{:S(2)}) collective-permute-start(f32[128,256]{1,0:T(8,128)S(1)} %fusion.5), channel_id=1, source_target_pairs={{0,0},{2,8},{4,16},{6,24},{8,1},{10,9},{12,17},{14,25},{16,2},{18,... | collective-permute-start | bytes 393224 | tf_op jit(solution)/shard_map/ppermute | solution.py:245
  129.5 12.9 %collective-permute-start.31 = (f32[128,256]{1,0:T(8,128)S(1)}, f32[128,256]{1,0:T(8,128)S(1)}, u32[]{:S(2)}, u32[]{:S(2)}) collective-permute-start(f32[128,256]{1,0:T(8,128)S(1)} %fusion.5), channel_id=1, source_target_pairs={{1,0},{3,8},{5,16},{7,24},{9,1},{11,9},{13,17},{15,25},{17,2},{19,... | collective-permute-start | bytes 393224 | tf_op jit(solution)/shard_map/ppermute | solution.py:245
  (4 other events, 82.4 us)
where the time goes:
time: 144 us; the launch traced here: 143 us
  starting transfers between devices  49.4 us (34%)
  waiting for transfers between devices  47.4 us (33%)
  Pallas kernels  36.2 us (25%)
  other arithmetic  5.54 us (4%)
  local copies, waits for them, and re-layouts  3.83 us (3%)
    ppermute x26, starting transfers between devices, swapped(): lax.ppermute(value, axis, [(r, r ^ m) for r in range(lax.axis_size(axis))])  36.8 us
    pallas_call x3, Pallas kernels, half_grads(): pl.pallas_call(functools.partial(half_kernel, k, groups, share, layout, t...  36.2 us
    ppermute x26, waiting for transfers between devices, swapped(): lax.ppermute(value, axis, [(r, r ^ m) for r in range(lax.axis_size(axis))])  32.6 us
    ppermute x6, waiting for transfers between devices, permute(): return lax.ppermute(value, both, pairs)  14.8 us
    ppermute x6, starting transfers between devices, permute(): return lax.ppermute(value, both, pairs)  12.6 us
  transfers between devices with their start and end apart: 32, of which 14 were waited for; matrix products, arithmetic and copies ran while one was open for 4% of the time, Pallas kernels for 21%

commit v1 on v0

--- a/solution.py
+++ b/solution.py
@@ -27,10 +27,21 @@
     return lax.dot_general(left, right, (dims, ((), ())), preferred_element_type=jnp.float32)
 
 
+def order_of(count):
+    order = [0]
+    step = count // 2
+    while step:
+        order += [d + step for d in order]
+        step //= 2
+    return order
+
+
 def half_kernel(k, groups, share, layout, tiles, first, added, ends, last, extra, *refs):
     rest = list(refs)
     take = lambda count: [rest.pop(0) for _ in range(count)]
-    place_ref, listed_ref, cooc_ref, mine_ref, theirs_ref = take(5)
+    place_ref, listed_ref, cooc_ref = take(3)
+    row_refs = take(4)
+    order = order_of(groups)
     if first:
         pieces = take(len(layout))
     else:
@@ -85,9 +96,9 @@
 
     if first:
         total = jnp.zeros((1, 128), jnp.float32)
-        for ref in (mine_ref, theirs_ref):
-            for d in range(groups):
-                at = d * (quarter + PAD) + quarter + 1
+        for ref in row_refs:
+            for j in range(groups // 2):
+                at = j * (quarter + PAD) + quarter + 1
                 total = total + ref[at : at + 1, :128]
         log_total = jnp.concatenate([jnp.log(total)] * (depth // 128), axis=1)
         for piece, (other, start, count) in zip(pieces, layout):
@@ -103,9 +114,11 @@
     else:
         sums[...] = sums_in[...]
 
-    for ref, side in ((mine_ref, core), (theirs_ref, 1 - core)):
-        for d in range(groups):
-            start = d * (quarter + PAD)
+    for number, ref in enumerate(row_refs):
+        side = core if number < 2 else 1 - core
+        for j in range(groups // 2):
+            d = order[number % 2 * (groups // 2) + j]
+            start = j * (quarter + PAD)
             at = pl.multiple_of((chip ^ d) * half + side * quarter, quarter)
             row_vecs[pl.ds(at, quarter), :] = ref[start : start + quarter, :]
             log_row = ref[start + quarter : start + quarter + 1, :128]
@@ -166,9 +179,9 @@
             gradients(strips - 1, behind)
 
     for out, side in ((mine_out, core), (other_out, 1 - core)) if ends else ():
-        for d in range(groups):
+        for j, d in enumerate(order):
             at = pl.multiple_of((chip ^ d) * half + side * quarter, quarter)
-            out[d * quarter : (d + 1) * quarter, :] = row_out[pl.ds(at, quarter), :]
+            out[j * quarter : (j + 1) * quarter, :] = row_out[pl.ds(at, quarter), :]
     if last:
         for other in range(groups):
             at = pl.multiple_of((g ^ other) * share, share)
@@ -177,10 +190,10 @@
             outs[2 * other + 1][...] = block[half:]
 
 
-def half_grads(k, groups, share, layout, tiles, place, listed, cooc, mine, theirs, held, row_in, ready):
-    depth = mine.shape[1]
+def half_grads(k, groups, share, layout, tiles, place, listed, cooc, vectors, held, row_in, ready):
+    depth = vectors[0].shape[1]
     cols = groups * share
-    first = k == 0
+    first = k == 0 and tiles[0] == (0, 0)
     added = row_in is not None
     ends = tiles[-1] == (cols // BLOCK - 1,) * 2
     last = ends and k == 1
@@ -199,8 +212,8 @@
     out_shape += [coded, coded, logs] if first else []
     out_shape += [col_half] * (2 * groups) if last else [turned]
     held = [*held, row_in] if added else [*held]
-    args = [place, listed, cooc, mine, theirs, *held, *ready]
-    in_specs = [scalar] * 2 + [remote] + [whole] * (2 + len(held)) + [remote] * len(ready)
+    args = [place, listed, cooc, *vectors, *held, *ready]
+    in_specs = [scalar] * 2 + [remote] + [whole] * (4 + len(held)) + [remote] * len(ready)
     scratch = [
         pltpu.VMEM((rows, depth), jnp.float32),
         pltpu.VMEM((rows, 128), jnp.float32),
@@ -262,28 +275,26 @@
         plane_total = plane_total + row_swapped(plane_total, step)
         step *= 2
 
-    tall = quarter + PAD
-    came = []
-    for c in (0, 1):
-        parts = []
-        for at in (c * quarter, half + c * quarter):
+    def to_line(k):
+        came = []
+        for c in (0, 1):
+            at = k * half + c * quarter
             under = jnp.pad(logs[at : at + quarter].reshape(1, quarter), ((0, PAD - 1), (0, depth - quarter)))
-            parts += [embed[at : at + quarter], under]
-        pairs = [(ident(r, q // 2, q % 2), ident(q, r, c)) for q in rows for r in rows]
-        came.append(permute(jnp.concatenate(parts, axis=0), pairs))
-    came = jnp.where(core == 0, came[0], came[1])
-    part_row = lax.broadcasted_iota(jnp.int32, (tall, depth), 0)
-    first_part = jnp.where(part_row == quarter + 1, plane_total[0, 0], came[:tall])
-    second_part = came[tall:]
-
-    def along_line(part):
-        return [part] + [swapped(part, "col", 2 * d) for d in range(1, groups)]
-
-    mine = jnp.concatenate(along_line(first_part), axis=0)
-    theirs = across(mine)
+            part = jnp.concatenate([embed[at : at + quarter], under], axis=0)
+            came.append(permute(part, [(ident(r, q // 2, q % 2), ident(q, r, c)) for q in rows for r in rows]))
+        return jnp.where(core == 0, came[0], came[1])
+
+    def along_line(part, after=()):
+        step = groups // 2
+        while step > 1:
+            came = swapped(part, "col", 2 * step)
+            part = part[: part.shape[0] - 2 * len(after)]
+            part = jnp.concatenate([part, *[array[:2] for array in after], came], axis=0)
+            after = ()
+            step //= 2
+        return part, swapped(part, "col", 2)
 
     under = jnp.pad(logs.reshape(share // depth, depth), ((0, PAD - share // depth), (0, 0)))
-    under = jnp.where(lax.broadcasted_iota(jnp.int32, under.shape, 0) == PAD - 1, plane_total[:, :1], under)
     coded = jnp.concatenate([embed, under], axis=0)
     pieces = {0: [coded]}
     layout = [(0, 0, share + PAD)]
@@ -296,16 +307,25 @@
         layout += [(3, 0, half), (3, half, half + PAD)]
     held = [pieces[m][start > 0] for m, start, _ in layout]
 
+    part = to_line(0)
+    part_row = lax.broadcasted_iota(jnp.int32, part.shape, 0)
+    part = jnp.where(part_row == quarter + 1, plane_total[0, 0], part)
+    for number, m in enumerate([1 << q for q in range(groups.bit_length() - 1)]):
+        part = jnp.where(part_row == quarter + 2 + number, pieces[m][0][: quarter + PAD], part)
+    lower, upper = along_line(part, pieces[3] if groups == 4 else ())
+    vectors = [lower, upper, across(lower), across(upper)]
+
     listing = tile_list.reshape(-1)
     listed = jnp.sum((listing[None, :] == jnp.arange(listing.shape[0])[:, None]).astype(jnp.int32), axis=1)
     place = jnp.stack([g, chip, core]).astype(jnp.int32)
 
     def from_line(outs):
-        summed = outs[0] + across(outs[1])
-        parts = [summed[d * quarter : (d + 1) * quarter] for d in rows]
-        total = parts[0]
-        for d in range(1, groups):
-            total = total + swapped(parts[d], "col", 2 * d)
+        summed = total = outs[0] + across(outs[1])
+        step = 1
+        while step < groups:
+            kept = total.shape[0] // 2
+            total = total[:kept] + swapped(total[kept:], "col", 2 * step)
+            step *= 2
         return summed, total
 
     def to_home(total):
@@ -316,23 +336,21 @@
 
     tiles = [(row, col) for row in range(groups * share // BLOCK) for col in range(groups * share // BLOCK)]
     grads = functools.partial(half_grads, groups=groups, share=share, layout=layout, place=place, listed=listed, cooc=cooc)
-    outs = grads(0, tiles=tiles, mine=mine, theirs=theirs, held=held, row_in=None, ready=[])
+    lower, upper = along_line(to_line(1))
+    outs = grads(0, tiles=tiles[:-1], vectors=vectors, held=held, row_in=None, ready=[lower])
+    columns = outs[1:4]
+    outs = grads(0, tiles=tiles[-1:], vectors=vectors, held=outs[1:], row_in=outs[0], ready=[upper])
     first_summed, first_total = from_line(outs)
-    parts = along_line(second_part)
-    parts[1] = jnp.where(part_row == quarter + 2, outs[0][:tall], parts[1])
-    mine = jnp.concatenate(parts, axis=0)
-    theirs = across(mine)
-    grads = functools.partial(grads, 1, mine=mine, theirs=theirs)
-    columns = outs[2:5]
-    outs = grads(tiles=tiles[:-1], held=outs[2:], row_in=None, ready=[first_summed])
-    outs = grads(tiles=tiles[-1:], held=[*columns, outs[1]], row_in=outs[0], ready=[first_total])
+    vectors = [lower, upper, across(lower), across(upper)]
+    outs = grads(1, tiles=tiles[:-1], vectors=vectors, held=[*columns, outs[2]], row_in=None, ready=[first_summed])
+    outs = grads(1, tiles=tiles[-1:], vectors=vectors, held=[*columns, outs[1]], row_in=outs[0], ready=[first_total])
     second_summed, second_total = from_line(outs)
     first_quarters = to_home(first_total)
     quarters = first_quarters + to_home(second_total)
 
     halves = outs[2:]
     if groups == 4:
-        spare = second_summed[:PAD] + first_quarters[0][:PAD] + first_quarters[1][:PAD]
+        spare = second_summed[:PAD]
         first_x = row_swapped(jnp.concatenate([halves[2], halves[6], spare], axis=0), 1)[: 2 * half]
         first_y = row_swapped(jnp.concatenate([halves[5], halves[7], spare], axis=0), 2)[: 2 * half]
         second_x = row_swapped(halves[3] + first_y[half:], 1)

time: 144 us -> 144 us (level); the launches traced: 143 us -> 142 us
  starting transfers between devices: 49.4 us -> 37 us
  waiting for transfers between devices: 47.4 us -> 56.3 us
  Pallas kernels: 36.2 us -> 38.5 us
    ppermute x26 -> x24, starting transfers between devices: 36.8 us -> 15.1 us  [swapped(): lax.ppermute(value, axis, [(r, r ^ m) for r in range(lax.axis_size(axis))])]
    ppermute x26 -> x24, waiting for transfers between devices: 32.6 us -> 44.5 us  [swapped(): lax.ppermute(value, axis, [(r, r ^ m) for r in range(lax.axis_size(axis))])]
    ppermute x6 -> x8, starting transfers between devices: 12.6 us -> 22 us  [permute(): return lax.ppermute(value, both, pairs)]
    ppermute x6 -> x8, waiting for transfers between devices: 14.8 us -> 11.9 us  [permute(): return lax.ppermute(value, both, pairs)]
    pallas_call x3 -> x4, Pallas kernels: 36.2 us -> 38.5 us  [half_grads(): pl.pallas_call(functools.partial(half_kernel, k, groups, share, layout, t...]
  transfers between devices with their start and end apart: 32 -> 32, of which waited for: 14 -> 15; matrix products, arithmetic and copies ran while one was open for 4% -> 4% of each run, Pallas kernels for 21% -> 18%
where the time goes in v1:
time: 144 us; the launch traced here: 142 us
  waiting for transfers between devices  56.3 us (39%)
  Pallas kernels  38.5 us (27%)
  starting transfers between devices  37 us (26%)
  other arithmetic  6.35 us (4%)
  local copies, waits for them, and re-layouts  2.43 us (2%)
    ppermute x24, waiting for transfers between devices, swapped(): lax.ppermute(value, axis, [(r, r ^ m) for r in range(lax.axis_size(axis))])  44.5 us
    pallas_call x4, Pallas kernels, half_grads(): pl.pallas_call(functools.partial(half_kernel, k, groups, share, layout, t...  38.5 us
    ppermute x8, starting transfers between devices, permute(): return lax.ppermute(value, both, pairs)  22 us
    ppermute x24, starting transfers between devices, swapped(): lax.ppermute(value, axis, [(r, r ^ m) for r in range(lax.axis_size(axis))])  15.1 us
    ppermute x8, waiting for transfers between devices, permute(): return lax.ppermute(value, both, pairs)  11.9 us
  transfers between devices with their start and end apart: 32, of which 15 were waited for; matrix products, arithmetic and copies ran while one was open for 4% of the time, Pallas kernels for 18%

profile of v1, /device:TPU:2, one launch (start us, length us, event | category | flops | bytes accessed | tf_op | source)
XLA Modules:
  0.0 141.8 jit_solution(1237840668963467352)
XLA Ops:
  0.6 1.3 convert_reduce_fusion
  3.0 1.6 %collective-permute-start.6 = (f32[520,256]{1,0:T(8,128)S(1)}, f32[520,256]{1,0:T(8,128)S(1)}, u32[]{:S(2)}, u32[]{:S(2)}) collective-permute-start(f32[520,256]{1,0:T(8,128)S(1)} %select_maximum_fusion.refs_7_), channel_id=1, source_target_pairs={{0,16},{8,24},{16,0},{24,8},{1,17},{9,25},{17,1},{25,9},{2,18},{10... | collective-permute-start | bytes 1597448 | tf_op jit(solution)/shard_map/ppermute | solution.py:261
  5.8 1.6 %collective-permute-start.8 = (f32[8,128]{1,0:T(8,128)S(1)}, f32[8,128]{1,0:T(8,128)S(1)}, u32[]{:S(2)}, u32[]{:S(2)}) collective-permute-start(f32[8,128]{1,0:T(8,128)S(1)} %broadcast_in_dim.8), channel_id=1, source_target_pairs={{0,8},{8,0},{16,24},{24,16},{1,9},{9,1},{17,25},{25,17},{2,10},{10... | collective-permute-start | bytes 12296 | tf_op jit(solution)/shard_map/ppermute | solution.py:261
  7.3 1.1 fusion.2
  8.5 3.5 %collective-permute-start.10 = (f32[136,256]{1,0:T(8,128)S(1)}, f32[136,256]{1,0:T(8,128)S(1)}, u32[]{:S(2)}, u32[]{:S(2)}) collective-permute-start(f32[136,256]{1,0:T(8,128)S(1)} %select_maximum_fusion.2), channel_id=1, source_target_pairs={{0,0},{8,2},{16,4},{24,6},{1,8},{9,10},{17,12},{25,14},{2,16},{10,... | collective-permute-start | bytes 417800 | tf_op jit(solution)/shard_map/ppermute | solution.py:258
  12.0 3.0 %collective-permute-start.11 = (f32[136,256]{1,0:T(8,128)S(1)}, f32[136,256]{1,0:T(8,128)S(1)}, u32[]{:S(2)}, u32[]{:S(2)}) collective-permute-start(f32[136,256]{1,0:T(8,128)S(1)} %select_maximum_fusion.1), channel_id=1, source_target_pairs={{0,1},{8,3},{16,5},{24,7},{1,9},{9,11},{17,13},{25,15},{2,17},{10,... | collective-permute-start | bytes 417800 | tf_op jit(solution)/shard_map/ppermute | solution.py:258
  15.0 7.0 %collective-permute-done.8 = f32[8,128]{1,0:T(8,128)S(1)} collective-permute-done((f32[8,128]{1,0:T(8,128)S(1)}, f32[8,128]{1,0:T(8,128)S(1)}, u32[]{:S(2)}, u32[]{:S(2)}) %collective-permute-start.8) | collective-permute-done | bytes 4128 | tf_op jit(solution)/shard_map/ppermute | solution.py:261
  22.8 3.6 %collective-permute-done.9 = f32[8,128]{1,0:T(8,128)S(1)} collective-permute-done((f32[8,128]{1,0:T(8,128)S(1)}, f32[8,128]{1,0:T(8,128)S(1)}, u32[]{:S(2)}, u32[]{:S(2)}) %collective-permute-start.9) | collective-permute-done | bytes 4128 | tf_op jit(solution)/shard_map/ppermute | solution.py:261
  28.6 3.4 %collective-permute-start.14 = (f32[136,256]{1,0:T(8,128)S(1)}, f32[136,256]{1,0:T(8,128)S(1)}, u32[]{:S(2)}, u32[]{:S(2)}) collective-permute-start(f32[136,256]{1,0:T(8,128)S(1)} %fusion.1), channel_id=1, source_target_pairs={{0,4},{1,5},{2,6},{3,7},{4,0},{5,1},{6,2},{7,3},{8,12},{9,13},{10,... | collective-permute-start | bytes 417800 | tf_op jit(solution)/shard_map/ppermute | solution.py:261
  32.0 1.9 %collective-permute-start = (f32[136,256]{1,0:T(8,128)S(1)}, f32[136,256]{1,0:T(8,128)S(1)}, u32[]{:S(2)}, u32[]{:S(2)}) collective-permute-start(f32[136,256]{1,0:T(8,128)S(1)} %select_maximum_fusion.4), channel_id=1, source_target_pairs={{0,0},{8,2},{16,4},{24,6},{1,8},{9,10},{17,12},{25,14},{2,16},{10,... | collective-permute-start | bytes 417800 | tf_op jit(solution)/shard_map/ppermute | solution.py:258
  33.9 4.0 %collective-permute-start.1 = (f32[136,256]{1,0:T(8,128)S(1)}, f32[136,256]{1,0:T(8,128)S(1)}, u32[]{:S(2)}, u32[]{:S(2)}) collective-permute-start(f32[136,256]{1,0:T(8,128)S(1)} %select_maximum_fusion.3), channel_id=1, source_target_pairs={{0,1},{8,3},{16,5},{24,7},{1,9},{9,11},{17,13},{25,15},{2,17},{10,... | collective-permute-start | bytes 417800 | tf_op jit(solution)/shard_map/ppermute | solution.py:258
  39.9 2.2 %collective-permute-done.1 = f32[136,256]{1,0:T(8,128)S(1)} collective-permute-done((f32[136,256]{1,0:T(8,128)S(1)}, f32[136,256]{1,0:T(8,128)S(1)}, u32[]{:S(2)}, u32[]{:S(2)}) %collective-permute-start.1) | collective-permute-done | bytes 139296 | tf_op jit(solution)/shard_map/ppermute | solution.py:258
  42.2 2.0 %collective-permute-start.16 = (f32[272,256]{1,0:T(8,128)S(1)}, f32[272,256]{1,0:T(8,128)S(1)}, u32[]{:S(2)}, u32[]{:S(2)}) collective-permute-start(f32[272,256]{1,0:T(8,128)S(1)} %pad_maximum_fusion.3.refs_3_), channel_id=1, source_target_pairs={{0,1},{1,0},{2,3},{3,2},{4,5},{5,4},{6,7},{7,6},{8,9},{9,8},{10,11... | collective-permute-start | bytes 835592 | tf_op jit(solution)/shard_map/ppermute | solution.py:261
  44.2 3.8 %collective-permute-done.15.refs_4_ = f32[272,256]{1,0:T(8,128)S(1)} collective-permute-done((f32[272,256]{1,0:T(8,128)S(1)}, f32[272,256]{1,0:T(8,128)S(1)}, u32[]{:S(2)}, u32[]{:S(2)}) %collective-permute-start.15) | collective-permute-done | bytes 278560 | tf_op jit(solution)/shard_map/ppermute | solution.py:261
  48.2 3.3 %collective-permute-done.2 = f32[136,256]{1,0:T(8,128)S(1)} collective-permute-done((f32[136,256]{1,0:T(8,128)S(1)}, f32[136,256]{1,0:T(8,128)S(1)}, u32[]{:S(2)}, u32[]{:S(2)}) %collective-permute-start.2) | collective-permute-done | bytes 139296 | tf_op jit(solution)/shard_map/ppermute | solution.py:261
  51.7 13.1 %half_grads.4 = (f32[1024,256]{1,0:T(8,128)S(1)}, bf16[2048,256]{1,0:T(8,128)(2,1)S(1)}, bf16[2048,256]{1,0:T(8,128)(2,1)S(1)}, f32[32,256]{1,0:T(8,128)S(1)}, f32[256,2048]{1,0:T(8,128)S(1)}) custom-call(s32[3]{0:T(128)S(1)} %pad_add_fusion.refs_0_, s32[4]{0:T(128)S(1)} %convert_reduce_fusion.1.refs_1_, s32[2048,2048]{1,0:T(8,128)} %refs_2_.7, ...), custom_call_target="tpu_custom_call" | custom-call | flops 7247757312 | bytes 10485760 | tf_op jit(solution)/shard_map/half_grads/pallas_call | solution.py:228
  64.8 5.9 %half_grads.5 = (f32[512,256]{1,0:T(8,128)S(1)}, f32[512,256]{1,0:T(8,128)S(1)}, f32[256,2048]{1,0:T(8,128)S(1)}) custom-call(s32[3]{0:T(128)S(1)} %pad_add_fusion.refs_0_, s32[4]{0:T(128)S(1)} %convert_reduce_fusion.1.refs_1_, s32[2048,2048]{1,0:T(8,128)} %refs_2_.7, f32[272,256]{1,0:T(8,128)S(1)} %pad_maximum_fusion.3.refs_3_, ...), custom_call_target="tpu_custom_call" | custom-call | flops 2415919104 | bytes 6291456 | tf_op jit(solution)/shard_map/half_grads/pallas_call | solution.py:228
  70.8 1.9 %collective-permute-done.18 = f32[512,256]{1,0:T(8,128)S(1)} collective-permute-done((f32[512,256]{1,0:T(8,128)S(1)}, f32[512,256]{1,0:T(8,128)S(1)}, u32[]{:S(2)}, u32[]{:S(2)}) %collective-permute-start.18) | collective-permute-done | bytes 524320 | tf_op jit(solution)/shard_map/ppermute | solution.py:261
  72.8 2.0 %collective-permute-start.19 = (f32[256,256]{1,0:T(8,128)S(1)}, f32[256,256]{1,0:T(8,128)S(1)}, u32[]{:S(2)}, u32[]{:S(2)}) collective-permute-start(f32[256,256]{1,0:T(8,128)S(1)} %slice.130), channel_id=1, source_target_pairs={{0,2},{1,3},{2,0},{3,1},{4,6},{5,7},{6,4},{7,5},{8,10},{9,11},{10,... | collective-permute-start | bytes 786440 | tf_op jit(solution)/shard_map/ppermute | solution.py:261
  75.3 6.1 %collective-permute-done.19 = f32[256,256]{1,0:T(8,128)S(1)} collective-permute-done((f32[256,256]{1,0:T(8,128)S(1)}, f32[256,256]{1,0:T(8,128)S(1)}, u32[]{:S(2)}, u32[]{:S(2)}) %collective-permute-start.19) | collective-permute-done | bytes 262176 | tf_op jit(solution)/shard_map/ppermute | solution.py:261
  81.6 13.1 %half_grads.6 = (f32[1024,256]{1,0:T(8,128)S(1)}, f32[256,2048]{1,0:T(8,128)S(1)}) custom-call(s32[3]{0:T(128)S(1)} %pad_add_fusion.refs_0_, s32[4]{0:T(128)S(1)} %convert_reduce_fusion.1.refs_1_, s32[2048,2048]{1,0:T(8,128)} %refs_2_.7, f32[272,256]{1,0:T(8,128)S(1)} %pad_maximum_fusion.2.refs_12_.refs_3_, ...), custom_call_target="tpu_custom_call" | custom-call | flops 7247757312 | bytes 10485760 | tf_op jit(solution)/shard_map/half_grads/pallas_call | solution.py:228
  94.7 6.4 %half_grads.7 = (f32[512,256]{1,0:T(8,128)S(1)}, f32[512,256]{1,0:T(8,128)S(1)}, f32[256,256]{1,0:T(8,128)S(1)}, f32[256,256]{1,0:T(8,128)S(1)}, f32[256,256]{1,...) custom-call(s32[3]{0:T(128)S(1)} %pad_add_fusion.refs_0_, ...), custom_call_target="tpu_custom_call" | custom-call | flops 2415919104 | bytes 6291456 | tf_op jit(solution)/shard_map/half_grads/pallas_call | solution.py:228
  101.2 1.9 %collective-permute-done.21 = f32[512,256]{1,0:T(8,128)S(1)} collective-permute-done((f32[512,256]{1,0:T(8,128)S(1)}, f32[512,256]{1,0:T(8,128)S(1)}, u32[]{:S(2)}, u32[]{:S(2)}) %collective-permute-start.21) | collective-permute-done | bytes 524320 | tf_op jit(solution)/shard_map/ppermute | solution.py:261
  103.4 1.8 %collective-permute-start.28 = (f32[256,256]{1,0:T(8,128)S(1)}, f32[256,256]{1,0:T(8,128)S(1)}, u32[]{:S(2)}, u32[]{:S(2)}) collective-permute-start(f32[256,256]{1,0:T(8,128)S(1)} %slice.139), channel_id=1, source_target_pairs={{0,2},{1,3},{2,0},{3,1},{4,6},{5,7},{6,4},{7,5},{8,10},{9,11},{10,... | collective-permute-start | bytes 786440 | tf_op jit(solution)/shard_map/ppermute | solution.py:261
  105.2 3.1 %collective-permute-start.26 = (f32[128,256]{1,0:T(8,128)S(1)}, f32[128,256]{1,0:T(8,128)S(1)}, u32[]{:S(2)}, u32[]{:S(2)}) collective-permute-start(f32[128,256]{1,0:T(8,128)S(1)} %slice_add_fusion.7.refs_12_), channel_id=1, source_target_pairs={{0,0},{2,8},{4,16},{6,24},{8,1},{10,9},{12,17},{14,25},{16,2},{18,... | collective-permute-start | bytes 393224 | tf_op jit(solution)/shard_map/ppermute | solution.py:258
  108.3 1.3 collective-permute-start.27
  109.6 3.0 %collective-permute-done.28 = f32[256,256]{1,0:T(8,128)S(1)} collective-permute-done((f32[256,256]{1,0:T(8,128)S(1)}, f32[256,256]{1,0:T(8,128)S(1)}, u32[]{:S(2)}, u32[]{:S(2)}) %collective-permute-start.28) | collective-permute-done | bytes 262176 | tf_op jit(solution)/shard_map/ppermute | solution.py:261
  112.7 10.3 %collective-permute-done.22 = f32[520,256]{1,0:T(8,128)S(1)} collective-permute-done((f32[520,256]{1,0:T(8,128)S(1)}, f32[520,256]{1,0:T(8,128)S(1)}, u32[]{:S(2)}, u32[]{:S(2)}) %collective-permute-start.22) | collective-permute-done | bytes 532512 | tf_op jit(solution)/shard_map/ppermute | solution.py:261
  124.3 4.0 %collective-permute-start.30 = (f32[128,256]{1,0:T(8,128)S(1)}, f32[128,256]{1,0:T(8,128)S(1)}, u32[]{:S(2)}, u32[]{:S(2)}) collective-permute-start(f32[128,256]{1,0:T(8,128)S(1)} %slice_add_fusion.6), channel_id=1, source_target_pairs={{0,0},{2,8},{4,16},{6,24},{8,1},{10,9},{12,17},{14,25},{16,2},{18,... | collective-permute-start | bytes 393224 | tf_op jit(solution)/shard_map/ppermute | solution.py:258
  128.3 2.4 %collective-permute-done.23 = f32[256,256]{1,0:T(8,128)S(1)} collective-permute-done((f32[256,256]{1,0:T(8,128)S(1)}, f32[256,256]{1,0:T(8,128)S(1)}, u32[]{:S(2)}, u32[]{:S(2)}) %collective-permute-start.23) | collective-permute-done | bytes 262176 | tf_op jit(solution)/shard_map/ppermute | solution.py:261
  130.7 1.3 collective-permute-start.31
  132.5 8.2 %collective-permute-done.31 = f32[128,256]{1,0:T(8,128)S(1)} collective-permute-done((f32[128,256]{1,0:T(8,128)S(1)}, f32[128,256]{1,0:T(8,128)S(1)}, u32[]{:S(2)}, u32[]{:S(2)}) %collective-permute-start.31) | collective-permute-done | bytes 131104 | tf_op jit(solution)/shard_map/ppermute | solution.py:258
  (84 shorter events, 11.5 us)
Async XLA Ops:
  3.0 24.6 %collective-permute-start.6 = (f32[520,256]{1,0:T(8,128)S(1)}, f32[520,256]{1,0:T(8,128)S(1)}, u32[]{:S(2)}, u32[]{:S(2)}) collective-permute-start(f32[520,256]{1,0:T(8,128)S(1)} %select_maximum_fusion.refs_7_), channel_id=1, source_target_pairs={{0,16},{8,24},{16,0},{24,8},{1,17},{9,25},{17,1},{25,9},{2,18},{10... | collective-permute-start | bytes 1597448 | tf_op jit(solution)/shard_map/ppermute | solution.py:261
  4.6 22.9 %collective-permute-start.7 = (f32[520,256]{1,0:T(8,128)S(1)}, f32[520,256]{1,0:T(8,128)S(1)}, u32[]{:S(2)}, u32[]{:S(2)}) collective-permute-start(f32[520,256]{1,0:T(8,128)S(1)} %select_maximum_fusion.refs_7_), channel_id=1, source_target_pairs={{0,8},{8,0},{16,24},{24,16},{1,9},{9,1},{17,25},{25,17},{2,10},{10... | collective-permute-start | bytes 1597448 | tf_op jit(solution)/shard_map/ppermute | solution.py:261
  5.8 16.2 %collective-permute-start.8 = (f32[8,128]{1,0:T(8,128)S(1)}, f32[8,128]{1,0:T(8,128)S(1)}, u32[]{:S(2)}, u32[]{:S(2)}) collective-permute-start(f32[8,128]{1,0:T(8,128)S(1)} %broadcast_in_dim.8), channel_id=1, source_target_pairs={{0,8},{8,0},{16,24},{24,16},{1,9},{9,1},{17,25},{25,17},{2,10},{10... | collective-permute-start | bytes 12296 | tf_op jit(solution)/shard_map/ppermute | solution.py:261
  8.5 19.2 %collective-permute-start.10 = (f32[136,256]{1,0:T(8,128)S(1)}, f32[136,256]{1,0:T(8,128)S(1)}, u32[]{:S(2)}, u32[]{:S(2)}) collective-permute-start(f32[136,256]{1,0:T(8,128)S(1)} %select_maximum_fusion.2), channel_id=1, source_target_pairs={{0,0},{8,2},{16,4},{24,6},{1,8},{9,10},{17,12},{25,14},{2,16},{10,... | collective-permute-start | bytes 417800 | tf_op jit(solution)/shard_map/ppermute | solution.py:258
  12.0 15.8 %collective-permute-start.11 = (f32[136,256]{1,0:T(8,128)S(1)}, f32[136,256]{1,0:T(8,128)S(1)}, u32[]{:S(2)}, u32[]{:S(2)}) collective-permute-start(f32[136,256]{1,0:T(8,128)S(1)} %select_maximum_fusion.1), channel_id=1, source_target_pairs={{0,1},{8,3},{16,5},{24,7},{1,9},{9,11},{17,13},{25,15},{2,17},{10,... | collective-permute-start | bytes 417800 | tf_op jit(solution)/shard_map/ppermute | solution.py:258
  22.7 3.7 %collective-permute-start.9 = (f32[8,128]{1,0:T(8,128)S(1)}, f32[8,128]{1,0:T(8,128)S(1)}, u32[]{:S(2)}, u32[]{:S(2)}) collective-permute-start(f32[8,128]{1,0:T(8,128)S(1)} %broadcast_add_fusion), channel_id=1, source_target_pairs={{0,16},{8,24},{16,0},{24,8},{1,17},{9,25},{17,1},{25,9},{2,18},{10... | collective-permute-start | bytes 12296 | tf_op jit(solution)/shard_map/ppermute | solution.py:261
  27.6 10.4 %collective-permute-start.13 = (f32[264,256]{1,0:T(8,128)S(1)}, f32[264,256]{1,0:T(8,128)S(1)}, u32[]{:S(2)}, u32[]{:S(2)}) collective-permute-start(f32[264,256]{1,0:T(8,128)S(1)} %slice.127), channel_id=1, source_target_pairs={{0,16},{8,24},{16,0},{24,8},{1,17},{9,25},{17,1},{25,9},{2,18},{10... | collective-permute-start | bytes 811016 | tf_op jit(solution)/shard_map/ppermute | solution.py:261
  27.7 10.3 %collective-permute-start.12 = (f32[256,256]{1,0:T(8,128)S(1)}, f32[256,256]{1,0:T(8,128)S(1)}, u32[]{:S(2)}, u32[]{:S(2)}) collective-permute-start(f32[256,256]{1,0:T(8,128)S(1)} %slice.125), channel_id=1, source_target_pairs={{0,8},{8,0},{16,24},{24,16},{1,9},{9,1},{17,25},{25,17},{2,10},{10... | collective-permute-start | bytes 786440 | tf_op jit(solution)/shard_map/ppermute | solution.py:261
  28.6 9.4 %collective-permute-start.14 = (f32[136,256]{1,0:T(8,128)S(1)}, f32[136,256]{1,0:T(8,128)S(1)}, u32[]{:S(2)}, u32[]{:S(2)}) collective-permute-start(f32[136,256]{1,0:T(8,128)S(1)} %fusion.1), channel_id=1, source_target_pairs={{0,4},{1,5},{2,6},{3,7},{4,0},{5,1},{6,2},{7,3},{8,12},{9,13},{10,... | collective-permute-start | bytes 417800 | tf_op jit(solution)/shard_map/ppermute | solution.py:261
  32.0 7.9 %collective-permute-start = (f32[136,256]{1,0:T(8,128)S(1)}, f32[136,256]{1,0:T(8,128)S(1)}, u32[]{:S(2)}, u32[]{:S(2)}) collective-permute-start(f32[136,256]{1,0:T(8,128)S(1)} %select_maximum_fusion.4), channel_id=1, source_target_pairs={{0,0},{8,2},{16,4},{24,6},{1,8},{9,10},{17,12},{25,14},{2,16},{10,... | collective-permute-start | bytes 417800 | tf_op jit(solution)/shard_map/ppermute | solution.py:258
  33.9 8.1 %collective-permute-start.1 = (f32[136,256]{1,0:T(8,128)S(1)}, f32[136,256]{1,0:T(8,128)S(1)}, u32[]{:S(2)}, u32[]{:S(2)}) collective-permute-start(f32[136,256]{1,0:T(8,128)S(1)} %select_maximum_fusion.3), channel_id=1, source_target_pairs={{0,1},{8,3},{16,5},{24,7},{1,9},{9,11},{17,13},{25,15},{2,17},{10,... | collective-permute-start | bytes 417800 | tf_op jit(solution)/shard_map/ppermute | solution.py:258
  38.0 10.0 %collective-permute-start.15 = (f32[272,256]{1,0:T(8,128)S(1)}, f32[272,256]{1,0:T(8,128)S(1)}, u32[]{:S(2)}, u32[]{:S(2)}) collective-permute-start(f32[272,256]{1,0:T(8,128)S(1)} %pad_maximum_fusion.3.refs_3_), channel_id=1, source_target_pairs={{0,2},{1,3},{2,0},{3,1},{4,6},{5,7},{6,4},{7,5},{8,10},{9,11},{10,... | collective-permute-start | bytes 835592 | tf_op jit(solution)/shard_map/ppermute | solution.py:261
  42.1 9.5 %collective-permute-start.2 = (f32[136,256]{1,0:T(8,128)S(1)}, f32[136,256]{1,0:T(8,128)S(1)}, u32[]{:S(2)}, u32[]{:S(2)}) collective-permute-start(f32[136,256]{1,0:T(8,128)S(1)} %broadcast_select_fusion), channel_id=1, source_target_pairs={{0,4},{1,5},{2,6},{3,7},{4,0},{5,1},{6,2},{7,3},{8,12},{9,13},{10,... | collective-permute-start | bytes 417800 | tf_op jit(solution)/shard_map/ppermute | solution.py:261
  42.2 9.5 %collective-permute-start.16 = (f32[272,256]{1,0:T(8,128)S(1)}, f32[272,256]{1,0:T(8,128)S(1)}, u32[]{:S(2)}, u32[]{:S(2)}) collective-permute-start(f32[272,256]{1,0:T(8,128)S(1)} %pad_maximum_fusion.3.refs_3_), channel_id=1, source_target_pairs={{0,1},{1,0},{2,3},{3,2},{4,5},{5,4},{6,7},{7,6},{8,9},{9,8},{10,11... | collective-permute-start | bytes 835592 | tf_op jit(solution)/shard_map/ppermute | solution.py:261
  48.0 3.7 %collective-permute-start.17 = (f32[272,256]{1,0:T(8,128)S(1)}, f32[272,256]{1,0:T(8,128)S(1)}, u32[]{:S(2)}, u32[]{:S(2)}) collective-permute-start(f32[272,256]{1,0:T(8,128)S(1)} %collective-permute-done.15.refs_4_), channel_id=1, source_target_pairs={{0,1},{1,0},{2,3},{3,2},{4,5},{5,4},{6,7},{7,6},{8,9},{9,8},{10,11... | collective-permute-start | bytes 835592 | tf_op jit(solution)/shard_map/ppermute | solution.py:261
  51.6 13.2 %collective-permute-start.3 = (f32[272,256]{1,0:T(8,128)S(1)}, f32[272,256]{1,0:T(8,128)S(1)}, u32[]{:S(2)}, u32[]{:S(2)}) collective-permute-start(f32[272,256]{1,0:T(8,128)S(1)} %pad_maximum_fusion.2.refs_12_.refs_3_), channel_id=1, source_target_pairs={{0,2},{1,3},{2,0},{3,1},{4,6},{5,7},{6,4},{7,5},{8,10},{9,11},{10,... | collective-permute-start | bytes 835592 | tf_op jit(solution)/shard_map/ppermute | solution.py:261
  70.7 2.0 %collective-permute-start.18 = (f32[512,256]{1,0:T(8,128)S(1)}, f32[512,256]{1,0:T(8,128)S(1)}, u32[]{:S(2)}, u32[]{:S(2)}) collective-permute-start(f32[512,256]{1,0:T(8,128)S(1)} %get-tuple-element.29), channel_id=1, source_target_pairs={{0,1},{1,0},{2,3},{3,2},{4,5},{5,4},{6,7},{7,6},{8,9},{9,8},{10,11... | collective-permute-start | bytes 1572872 | tf_op jit(solution)/shard_map/ppermute | solution.py:261
  72.8 8.7 %collective-permute-start.19 = (f32[256,256]{1,0:T(8,128)S(1)}, f32[256,256]{1,0:T(8,128)S(1)}, u32[]{:S(2)}, u32[]{:S(2)}) collective-permute-start(f32[256,256]{1,0:T(8,128)S(1)} %slice.130), channel_id=1, source_target_pairs={{0,2},{1,3},{2,0},{3,1},{4,6},{5,7},{6,4},{7,5},{8,10},{9,11},{10,... | collective-permute-start | bytes 786440 | tf_op jit(solution)/shard_map/ppermute | solution.py:261
  74.8 6.7 %collective-permute-start.4 = (f32[272,256]{1,0:T(8,128)S(1)}, f32[272,256]{1,0:T(8,128)S(1)}, u32[]{:S(2)}, u32[]{:S(2)}) collective-permute-start(f32[272,256]{1,0:T(8,128)S(1)} %pad_maximum_fusion.2.refs_12_.refs_3_), channel_id=1, source_target_pairs={{0,1},{1,0},{2,3},{3,2},{4,5},{5,4},{6,7},{7,6},{8,9},{9,8},{10,11... | collective-permute-start | bytes 835592 | tf_op jit(solution)/shard_map/ppermute | solution.py:261
  74.8 6.8 %collective-permute-start.5 = (f32[272,256]{1,0:T(8,128)S(1)}, f32[272,256]{1,0:T(8,128)S(1)}, u32[]{:S(2)}, u32[]{:S(2)}) collective-permute-start(f32[272,256]{1,0:T(8,128)S(1)} %collective-permute-done.3.refs_12_.refs_4_), channel_id=1, source_target_pairs={{0,1},{1,0},{2,3},{3,2},{4,5},{5,4},{6,7},{7,6},{8,9},{9,8},{10,11... | collective-permute-start | bytes 835592 | tf_op jit(solution)/shard_map/ppermute | solution.py:261
  81.5 13.2 %collective-permute-start.20 = (f32[128,256]{1,0:T(8,128)S(1)}, f32[128,256]{1,0:T(8,128)S(1)}, u32[]{:S(2)}, u32[]{:S(2)}) collective-permute-start(f32[128,256]{1,0:T(8,128)S(1)} %slice.132), channel_id=1, source_target_pairs={{0,4},{1,5},{2,6},{3,7},{4,0},{5,1},{6,2},{7,3},{8,12},{9,13},{10,... | collective-permute-start | bytes 393224 | tf_op jit(solution)/shard_map/ppermute | solution.py:261
  101.1 2.0 %collective-permute-start.21 = (f32[512,256]{1,0:T(8,128)S(1)}, f32[512,256]{1,0:T(8,128)S(1)}, u32[]{:S(2)}, u32[]{:S(2)}) collective-permute-start(f32[512,256]{1,0:T(8,128)S(1)} %get-tuple-element.36), channel_id=1, source_target_pairs={{0,1},{1,0},{2,3},{3,2},{4,5},{5,4},{6,7},{7,6},{8,9},{9,8},{10,11... | collective-permute-start | bytes 1572872 | tf_op jit(solution)/shard_map/ppermute | solution.py:261
  103.2 19.8 %collective-permute-start.22 = (f32[520,256]{1,0:T(8,128)S(1)}, f32[520,256]{1,0:T(8,128)S(1)}, u32[]{:S(2)}, u32[]{:S(2)}) collective-permute-start(f32[520,256]{1,0:T(8,128)S(1)} %get-tuple-element.48), channel_id=1, source_target_pairs={{0,8},{8,0},{16,24},{24,16},{1,9},{9,1},{17,25},{25,17},{2,10},{10... | collective-permute-start | bytes 1597448 | tf_op jit(solution)/shard_map/ppermute | solution.py:261
  103.4 9.2 %collective-permute-start.28 = (f32[256,256]{1,0:T(8,128)S(1)}, f32[256,256]{1,0:T(8,128)S(1)}, u32[]{:S(2)}, u32[]{:S(2)}) collective-permute-start(f32[256,256]{1,0:T(8,128)S(1)} %slice.139), channel_id=1, source_target_pairs={{0,2},{1,3},{2,0},{3,1},{4,6},{5,7},{6,4},{7,5},{8,10},{9,11},{10,... | collective-permute-start | bytes 786440 | tf_op jit(solution)/shard_map/ppermute | solution.py:261
  105.2 18.0 %collective-permute-start.24 = (f32[520,256]{1,0:T(8,128)S(1)}, f32[520,256]{1,0:T(8,128)S(1)}, u32[]{:S(2)}, u32[]{:S(2)}) collective-permute-start(f32[520,256]{1,0:T(8,128)S(1)} %get-tuple-element.49), channel_id=1, source_target_pairs={{0,16},{8,24},{16,0},{24,8},{1,17},{9,25},{17,1},{25,9},{2,18},{10... | collective-permute-start | bytes 1597448 | tf_op jit(solution)/shard_map/ppermute | solution.py:261
  105.2 27.0 %collective-permute-start.26 = (f32[128,256]{1,0:T(8,128)S(1)}, f32[128,256]{1,0:T(8,128)S(1)}, u32[]{:S(2)}, u32[]{:S(2)}) collective-permute-start(f32[128,256]{1,0:T(8,128)S(1)} %slice_add_fusion.7.refs_12_), channel_id=1, source_target_pairs={{0,0},{2,8},{4,16},{6,24},{8,1},{10,9},{12,17},{14,25},{16,2},{18,... | collective-permute-start | bytes 393224 | tf_op jit(solution)/shard_map/ppermute | solution.py:258
  108.3 23.9 %collective-permute-start.27 = (f32[128,256]{1,0:T(8,128)S(1)}, f32[128,256]{1,0:T(8,128)S(1)}, u32[]{:S(2)}, u32[]{:S(2)}) collective-permute-start(f32[128,256]{1,0:T(8,128)S(1)} %slice_add_fusion.7.refs_12_), channel_id=1, source_target_pairs={{1,0},{3,8},{5,16},{7,24},{9,1},{11,9},{13,17},{15,25},{17,2},{19,... | collective-permute-start | bytes 393224 | tf_op jit(solution)/shard_map/ppermute | solution.py:258
  112.6 11.7 %collective-permute-start.29 = (f32[128,256]{1,0:T(8,128)S(1)}, f32[128,256]{1,0:T(8,128)S(1)}, u32[]{:S(2)}, u32[]{:S(2)}) collective-permute-start(f32[128,256]{1,0:T(8,128)S(1)} %slice.141), channel_id=1, source_target_pairs={{0,4},{1,5},{2,6},{3,7},{4,0},{5,1},{6,2},{7,3},{8,12},{9,13},{10,... | collective-permute-start | bytes 393224 | tf_op jit(solution)/shard_map/ppermute | solution.py:261
  123.1 7.6 %collective-permute-start.23 = (f32[256,256]{1,0:T(8,128)S(1)}, f32[256,256]{1,0:T(8,128)S(1)}, u32[]{:S(2)}, u32[]{:S(2)}) collective-permute-start(f32[256,256]{1,0:T(8,128)S(1)} %slice_add_fusion.3), channel_id=1, source_target_pairs={{0,16},{8,24},{16,0},{24,8},{1,17},{9,25},{17,1},{25,9},{2,18},{10... | collective-permute-start | bytes 786440 | tf_op jit(solution)/shard_map/ppermute | solution.py:261
  123.2 8.8 %collective-permute-start.25 = (f32[256,256]{1,0:T(8,128)S(1)}, f32[256,256]{1,0:T(8,128)S(1)}, u32[]{:S(2)}, u32[]{:S(2)}) collective-permute-start(f32[256,256]{1,0:T(8,128)S(1)} %slice_add_fusion.2), channel_id=1, source_target_pairs={{0,8},{8,0},{16,24},{24,16},{1,9},{9,1},{17,25},{25,17},{2,10},{10... | collective-permute-start | bytes 786440 | tf_op jit(solution)/shard_map/ppermute | solution.py:261
  124.3 8.2 %collective-permute-start.30 = (f32[128,256]{1,0:T(8,128)S(1)}, f32[128,256]{1,0:T(8,128)S(1)}, u32[]{:S(2)}, u32[]{:S(2)}) collective-permute-start(f32[128,256]{1,0:T(8,128)S(1)} %slice_add_fusion.6), channel_id=1, source_target_pairs={{0,0},{2,8},{4,16},{6,24},{8,1},{10,9},{12,17},{14,25},{16,2},{18,... | collective-permute-start | bytes 393224 | tf_op jit(solution)/shard_map/ppermute | solution.py:258
  130.7 10.0 %collective-permute-start.31 = (f32[128,256]{1,0:T(8,128)S(1)}, f32[128,256]{1,0:T(8,128)S(1)}, u32[]{:S(2)}, u32[]{:S(2)}) collective-permute-start(f32[128,256]{1,0:T(8,128)S(1)} %slice_add_fusion.6), channel_id=1, source_target_pairs={{1,0},{3,8},{5,16},{7,24},{9,1},{11,9},{13,17},{15,25},{17,2},{19,... | collective-permute-start | bytes 393224 | tf_op jit(solution)/shard_map/ppermute | solution.py:258
  (3 other events, 95.7 us)

commit v2 on v1

--- a/solution.py
+++ b/solution.py
@@ -275,26 +275,37 @@
         plane_total = plane_total + row_swapped(plane_total, step)
         step *= 2
 
-    def to_line(k):
+    last_spare = lax.broadcasted_iota(jnp.int32, (PAD, depth), 0) == PAD - 1
+
+    def to_line(k, after):
         came = []
         for c in (0, 1):
             at = k * half + c * quarter
             under = jnp.pad(logs[at : at + quarter].reshape(1, quarter), ((0, PAD - 1), (0, depth - quarter)))
+            under = jnp.where(last_spare, after, under)
             part = jnp.concatenate([embed[at : at + quarter], under], axis=0)
             came.append(permute(part, [(ident(r, q // 2, q % 2), ident(q, r, c)) for q in rows for r in rows]))
         return jnp.where(core == 0, came[0], came[1])
 
-    def along_line(part, after=()):
+    def along_line_at_once(part):
+        came = [swapped(part, "col", 2 * d) for d in range(1, groups)]
+        parts = [([part] + came)[d] for d in order_of(groups)]
+        return [jnp.concatenate(few, axis=0) for few in (parts[: groups // 2], parts[groups // 2 :])] + [came]
+
+    def along_line(part, after):
         step = groups // 2
+        first_came = None
         while step > 1:
             came = swapped(part, "col", 2 * step)
+            first_came = came if first_came is None else first_came
             part = part[: part.shape[0] - 2 * len(after)]
             part = jnp.concatenate([part, *[array[:2] for array in after], came], axis=0)
             after = ()
             step //= 2
-        return part, swapped(part, "col", 2)
+        return part, swapped(part, "col", 2), first_came
 
     under = jnp.pad(logs.reshape(share // depth, depth), ((0, PAD - share // depth), (0, 0)))
+    under = jnp.where(lax.broadcasted_iota(jnp.int32, (PAD, depth), 0) == PAD - 1, plane_total[:, :1], under)
     coded = jnp.concatenate([embed, under], axis=0)
     pieces = {0: [coded]}
     layout = [(0, 0, share + PAD)]
@@ -307,45 +318,56 @@
         layout += [(3, 0, half), (3, half, half + PAD)]
     held = [pieces[m][start > 0] for m, start, _ in layout]
 
-    part = to_line(0)
+    part = to_line(0, plane_total[:, :1])
     part_row = lax.broadcasted_iota(jnp.int32, part.shape, 0)
     part = jnp.where(part_row == quarter + 1, plane_total[0, 0], part)
     for number, m in enumerate([1 << q for q in range(groups.bit_length() - 1)]):
         part = jnp.where(part_row == quarter + 2 + number, pieces[m][0][: quarter + PAD], part)
-    lower, upper = along_line(part, pieces[3] if groups == 4 else ())
+    lower, upper, first_came = along_line(part, pieces[3] if groups == 4 else ())
     vectors = [lower, upper, across(lower), across(upper)]
 
     listing = tile_list.reshape(-1)
     listed = jnp.sum((listing[None, :] == jnp.arange(listing.shape[0])[:, None]).astype(jnp.int32), axis=1)
     place = jnp.stack([g, chip, core]).astype(jnp.int32)
+
+    def from_line_at_once(outs):
+        summed = outs[0] + across(outs[1])
+        parts = {d: summed[j * quarter : (j + 1) * quarter] for j, d in enumerate(order_of(groups))}
+        total = parts[0]
+        for d in range(1, groups):
+            total = total + swapped(parts[d], "col", 2 * d)
+        return summed, total
 
     def from_line(outs):
         summed = total = outs[0] + across(outs[1])
         step = 1
         while step < groups:
             kept = total.shape[0] // 2
-            total = total[:kept] + swapped(total[kept:], "col", 2 * step)
+            came = swapped(total[kept:], "col", 2 * step)
+            first_came = came if step == 1 else first_came
+            total = total[:kept] + came
             step *= 2
-        return summed, total
-
-    def to_home(total):
+        return summed, total, first_came
+
+    def to_home(total, after=None):
         homes = []
         for c in (0, 1):
-            homes.append(permute(total, [(ident(q, r, c), ident(r, q // 2, q % 2)) for q in rows for r in rows]))
+            value = total if after is None else jnp.where(core == c, total, after)
+            homes.append(permute(value, [(ident(q, r, c), ident(r, q // 2, q % 2)) for q in rows for r in rows]))
         return homes
 
     tiles = [(row, col) for row in range(groups * share // BLOCK) for col in range(groups * share // BLOCK)]
     grads = functools.partial(half_grads, groups=groups, share=share, layout=layout, place=place, listed=listed, cooc=cooc)
-    lower, upper = along_line(to_line(1))
-    outs = grads(0, tiles=tiles[:-1], vectors=vectors, held=held, row_in=None, ready=[lower])
+    lower, upper, came = along_line_at_once(to_line(1, first_came[:PAD]))
+    outs = grads(0, tiles=tiles[:-1], vectors=vectors, held=held, row_in=None, ready=[])
     columns = outs[1:4]
-    outs = grads(0, tiles=tiles[-1:], vectors=vectors, held=outs[1:], row_in=outs[0], ready=[upper])
-    first_summed, first_total = from_line(outs)
+    outs = grads(0, tiles=tiles[-1:], vectors=vectors, held=outs[1:], row_in=outs[0], ready=came)
+    first_summed, first_total = from_line_at_once(outs)
     vectors = [lower, upper, across(lower), across(upper)]
     outs = grads(1, tiles=tiles[:-1], vectors=vectors, held=[*columns, outs[2]], row_in=None, ready=[first_summed])
     outs = grads(1, tiles=tiles[-1:], vectors=vectors, held=[*columns, outs[1]], row_in=outs[0], ready=[first_total])
-    second_summed, second_total = from_line(outs)
-    first_quarters = to_home(first_total)
+    second_summed, second_total, second_came = from_line(outs)
+    first_quarters = to_home(first_total, second_came[:quarter])
     quarters = first_quarters + to_home(second_total)
 
     halves = outs[2:]

time: 144 us -> 150 us (1.042)
  the two profiles are of different devices: /device:TPU:2 before, /device:TPU:6 now
where the time goes in v2:
time: 150 us; the launch traced here: 148 us
  waiting for transfers between devices  68.5 us (46%)
  starting transfers between devices  52.1 us (35%)
  Pallas kernels  15.1 us (10%)
  other arithmetic  8.42 us (6%)
  local copies, waits for them, and re-layouts  2.45 us (2%)
    ppermute x26, waiting for transfers between devices, swapped(): lax.ppermute(value, axis, [(r, r ^ m) for r in range(lax.axis_size(axis))])  48.7 us
    ppermute x26, starting transfers between devices, swapped(): lax.ppermute(value, axis, [(r, r ^ m) for r in range(lax.axis_size(axis))])  29.7 us
    ppermute x8, starting transfers between devices, permute(): return lax.ppermute(value, both, pairs)  22.4 us
    ppermute x8, waiting for transfers between devices, permute(): return lax.ppermute(value, both, pairs)  19.8 us
    pallas_call x4, Pallas kernels, half_grads(): pl.pallas_call(functools.partial(half_kernel, k, groups, share, layout, t...  15.1 us
  transfers between devices with their start and end apart: 34, of which 21 were waited for; matrix products, arithmetic and copies ran while one was open for 3% of the time, Pallas kernels for 2%

profile of v2, /device:TPU:6, one launch (start us, length us, event | category | flops | bytes accessed | tf_op | source)
XLA Modules:
  0.0 147.7 jit_solution(2200230708244253845)
XLA Ops:
  3.2 3.7 %collective-permute-done = f32[8,128]{0,1:T(8,128)S(1)} collective-permute-done((f32[8,128]{0,1:T(8,128)S(1)}, f32[8,128]{0,1:T(8,128)S(1)}, u32[]{:S(2)}, u32[]{:S(2)}) %collective-permute-start) | collective-permute-done | bytes 4128 | tf_op jit(solution)/shard_map/ppermute | solution.py:261
  8.2 3.7 %collective-permute-done.1 = f32[8,128]{0,1:T(8,128)S(1)} collective-permute-done((f32[8,128]{0,1:T(8,128)S(1)}, f32[8,128]{0,1:T(8,128)S(1)}, u32[]{:S(2)}, u32[]{:S(2)}) %collective-permute-start.1) | collective-permute-done | bytes 4128 | tf_op jit(solution)/shard_map/ppermute | solution.py:261
  15.6 7.8 %collective-permute-start.4 = (f32[136,256]{1,0:T(8,128)S(1)}, f32[136,256]{1,0:T(8,128)S(1)}, u32[]{:S(2)}, u32[]{:S(2)}) collective-permute-start(f32[136,256]{1,0:T(8,128)S(1)} %pad_maximum_fusion.5), channel_id=1, source_target_pairs={{0,0},{8,2},{16,4},{24,6},{1,8},{9,10},{17,12},{25,14},{2,16},{10,... | collective-permute-start | bytes 417800 | tf_op jit(solution)/shard_map/ppermute | solution.py:258
  23.4 1.3 collective-permute-start.5
  25.3 1.9 %collective-permute-done.4 = f32[136,256]{1,0:T(8,128)S(1)} collective-permute-done((f32[136,256]{1,0:T(8,128)S(1)}, f32[136,256]{1,0:T(8,128)S(1)}, u32[]{:S(2)}, u32[]{:S(2)}) %collective-permute-start.4) | collective-permute-done | bytes 139296 | tf_op jit(solution)/shard_map/ppermute | solution.py:258
  27.1 1.8 %collective-permute-done.5 = f32[136,256]{1,0:T(8,128)S(1)} collective-permute-done((f32[136,256]{1,0:T(8,128)S(1)}, f32[136,256]{1,0:T(8,128)S(1)}, u32[]{:S(2)}, u32[]{:S(2)}) %collective-permute-start.5) | collective-permute-done | bytes 139296 | tf_op jit(solution)/shard_map/ppermute | solution.py:258
  29.8 3.9 %collective-permute-start.6 = (f32[136,256]{1,0:T(8,128)S(1)}, f32[136,256]{1,0:T(8,128)S(1)}, u32[]{:S(2)}, u32[]{:S(2)}) collective-permute-start(f32[136,256]{1,0:T(8,128)S(1)} %fusion.1), channel_id=1, source_target_pairs={{0,4},{1,5},{2,6},{3,7},{4,0},{5,1},{6,2},{7,3},{8,12},{9,13},{10,... | collective-permute-start | bytes 417800 | tf_op jit(solution)/shard_map/ppermute | solution.py:261
  34.0 1.4 collective-permute-start.14
  36.7 5.2 %collective-permute-done.14.refs_10_ = f32[256,256]{1,0:T(8,128)S(1)} collective-permute-done((f32[256,256]{1,0:T(8,128)S(1)}, f32[256,256]{1,0:T(8,128)S(1)}, u32[]{:S(2)}, u32[]{:S(2)}) %collective-permute-start.14) | collective-permute-done | bytes 262176 | tf_op jit(solution)/shard_map/ppermute | solution.py:261
  42.0 3.2 %collective-permute-start.16 = (f32[272,256]{1,0:T(8,128)S(1)}, f32[272,256]{1,0:T(8,128)S(1)}, u32[]{:S(2)}, u32[]{:S(2)}) collective-permute-start(f32[272,256]{1,0:T(8,128)S(1)} %pad_maximum_fusion.4.refs_3_), channel_id=1, source_target_pairs={{0,2},{1,3},{2,0},{3,1},{4,6},{5,7},{6,4},{7,5},{8,10},{9,11},{10,... | collective-permute-start | bytes 835592 | tf_op jit(solution)/shard_map/ppermute | solution.py:261
  45.2 4.9 %collective-permute-start.8 = (f32[136,256]{1,0:T(8,128)S(1)}, f32[136,256]{1,0:T(8,128)S(1)}, u32[]{:S(2)}, u32[]{:S(2)}) collective-permute-start(f32[136,256]{1,0:T(8,128)S(1)} %pad_maximum_fusion.8), channel_id=1, source_target_pairs={{0,1},{8,3},{16,5},{24,7},{1,9},{9,11},{17,13},{25,15},{2,17},{10,... | collective-permute-start | bytes 417800 | tf_op jit(solution)/shard_map/ppermute | solution.py:258
  50.1 1.9 %collective-permute-start.7 = (f32[136,256]{1,0:T(8,128)S(1)}, f32[136,256]{1,0:T(8,128)S(1)}, u32[]{:S(2)}, u32[]{:S(2)}) collective-permute-start(f32[136,256]{1,0:T(8,128)S(1)} %pad_maximum_fusion.7), channel_id=1, source_target_pairs={{0,0},{8,2},{16,4},{24,6},{1,8},{9,10},{17,12},{25,14},{2,16},{10,... | collective-permute-start | bytes 417800 | tf_op jit(solution)/shard_map/ppermute | solution.py:258
  52.9 2.3 %collective-permute-done.8 = f32[136,256]{1,0:T(8,128)S(1)} collective-permute-done((f32[136,256]{1,0:T(8,128)S(1)}, f32[136,256]{1,0:T(8,128)S(1)}, u32[]{:S(2)}, u32[]{:S(2)}) %collective-permute-start.8) | collective-permute-done | bytes 139296 | tf_op jit(solution)/shard_map/ppermute | solution.py:258
  55.2 5.8 %collective-permute-done.7 = f32[136,256]{1,0:T(8,128)S(1)} collective-permute-done((f32[136,256]{1,0:T(8,128)S(1)}, f32[136,256]{1,0:T(8,128)S(1)}, u32[]{:S(2)}, u32[]{:S(2)}) %collective-permute-start.7) | collective-permute-done | bytes 139296 | tf_op jit(solution)/shard_map/ppermute | solution.py:258
  61.1 5.1 %collective-permute-start.11 = (f32[136,256]{1,0:T(8,128)S(1)}, f32[136,256]{1,0:T(8,128)S(1)}, u32[]{:S(2)}, u32[]{:S(2)}) collective-permute-start(f32[136,256]{1,0:T(8,128)S(1)} %broadcast_select_fusion), channel_id=1, source_target_pairs={{0,6},{1,7},{2,4},{3,5},{4,2},{5,3},{6,0},{7,1},{8,14},{9,15},{10,... | collective-permute-start | bytes 417800 | tf_op jit(solution)/shard_map/ppermute | solution.py:261
  66.7 1.7 %half_grads.4 = (f32[1024,256]{1,0:T(8,128)S(1)}, bf16[2048,256]{1,0:T(8,128)(2,1)S(1)}, bf16[2048,256]{1,0:T(8,128)(2,1)S(1)}, f32[32,256]{1,0:T(8,128)S(1)}, f32[256,2048]{1,0:T(8,128)S(1)}) custom-call(s32[3]{0:T(128)S(1)} %pad_add_fusion.refs_0_, s32[4]{0:T(128)S(1)} %convert_reduce_fusion.1.refs_1_, s32[2048,2048]{1,0:T(8,128)} %refs_2_.7, ...), custom_call_target="tpu_custom_call" | custom-call | flops 7247757312 | bytes 10485760 | tf_op jit(solution)/shard_map/half_grads/pallas_call | solution.py:228
  68.4 5.3 %collective-permute-done.11.refs_14_ = f32[136,256]{1,0:T(8,128)S(1)} collective-permute-done((f32[136,256]{1,0:T(8,128)S(1)}, f32[136,256]{1,0:T(8,128)S(1)}, u32[]{:S(2)}, u32[]{:S(2)}) %collective-permute-start.11) | collective-permute-done | bytes 139296 | tf_op jit(solution)/shard_map/ppermute | solution.py:261
  73.7 6.0 %collective-permute-done.9.refs_13_ = f32[136,256]{1,0:T(8,128)S(1)} collective-permute-done((f32[136,256]{1,0:T(8,128)S(1)}, f32[136,256]{1,0:T(8,128)S(1)}, u32[]{:S(2)}, u32[]{:S(2)}) %collective-permute-start.9) | collective-permute-done | bytes 139296 | tf_op jit(solution)/shard_map/ppermute | solution.py:261
  79.7 5.9 %half_grads.5 = (f32[512,256]{1,0:T(8,128)S(1)}, f32[512,256]{1,0:T(8,128)S(1)}, f32[256,2048]{1,0:T(8,128)S(1)}) custom-call(s32[3]{0:T(128)S(1)} %pad_add_fusion.refs_0_, s32[4]{0:T(128)S(1)} %convert_reduce_fusion.1.refs_1_, s32[2048,2048]{1,0:T(8,128)} %refs_2_.7, f32[272,256]{1,0:T(8,128)S(1)} %pad_maximum_fusion.4.refs_3_, ...), custom_call_target="tpu_custom_call" | custom-call | flops 2415919104 | bytes 6291456 | tf_op jit(solution)/shard_map/half_grads/pallas_call | solution.py:228
  87.7 3.2 %collective-permute-start.21 = (f32[128,256]{1,0:T(8,128)S(1)}, f32[128,256]{1,0:T(8,128)S(1)}, u32[]{:S(2)}, u32[]{:S(2)}) collective-permute-start(f32[128,256]{1,0:T(8,128)S(1)} %get-tuple-element.46), channel_id=1, source_target_pairs={{0,4},{1,5},{2,6},{3,7},{4,0},{5,1},{6,2},{7,3},{8,12},{9,13},{10,... | collective-permute-start | bytes 393224 | tf_op jit(solution)/shard_map/ppermute | solution.py:261
  93.3 2.2 %collective-permute-done.20 = f32[128,256]{1,0:T(8,128)S(1)} collective-permute-done((f32[128,256]{1,0:T(8,128)S(1)}, f32[128,256]{1,0:T(8,128)S(1)}, u32[]{:S(2)}, u32[]{:S(2)}) %collective-permute-start.20) | collective-permute-done | bytes 131104 | tf_op jit(solution)/shard_map/ppermute | solution.py:261
  95.5 5.4 %collective-permute-done.21 = f32[128,256]{1,0:T(8,128)S(1)} collective-permute-done((f32[128,256]{1,0:T(8,128)S(1)}, f32[128,256]{1,0:T(8,128)S(1)}, u32[]{:S(2)}, u32[]{:S(2)}) %collective-permute-start.21) | collective-permute-done | bytes 131104 | tf_op jit(solution)/shard_map/ppermute | solution.py:261
  100.9 6.4 %half_grads.7 = (f32[512,256]{1,0:T(8,128)S(1)}, f32[512,256]{1,0:T(8,128)S(1)}, f32[256,256]{1,0:T(8,128)S(1)}, f32[256,256]{1,0:T(8,128)S(1)}, f32[256,256]{1,...) custom-call(s32[3]{0:T(128)S(1)} %pad_add_fusion.refs_0_, ...), custom_call_target="tpu_custom_call" | custom-call | flops 2415919104 | bytes 6291456 | tf_op jit(solution)/shard_map/half_grads/pallas_call | solution.py:228
  107.4 1.9 %collective-permute-done.23 = f32[512,256]{1,0:T(8,128)S(1)} collective-permute-done((f32[512,256]{1,0:T(8,128)S(1)}, f32[512,256]{1,0:T(8,128)S(1)}, u32[]{:S(2)}, u32[]{:S(2)}) %collective-permute-start.23) | collective-permute-done | bytes 524320 | tf_op jit(solution)/shard_map/ppermute | solution.py:261
  109.7 8.1 %collective-permute-done.28 = f32[256,256]{1,0:T(8,128)S(1)} collective-permute-done((f32[256,256]{1,0:T(8,128)S(1)}, f32[256,256]{1,0:T(8,128)S(1)}, u32[]{:S(2)}, u32[]{:S(2)}) %collective-permute-start.28) | collective-permute-done | bytes 262176 | tf_op jit(solution)/shard_map/ppermute | solution.py:261
  117.8 1.9 %collective-permute-start.29 = (f32[128,256]{1,0:T(8,128)S(1)}, f32[128,256]{1,0:T(8,128)S(1)}, u32[]{:S(2)}, u32[]{:S(2)}) collective-permute-start(f32[128,256]{1,0:T(8,128)S(1)} %get-tuple-element.51), channel_id=1, source_target_pairs={{0,0},{2,8},{4,16},{6,24},{8,1},{10,9},{12,17},{14,25},{16,2},{18,... | collective-permute-start | bytes 393224 | tf_op jit(solution)/shard_map/ppermute | solution.py:258
  121.2 2.7 %collective-permute-done.24 = f32[520,256]{1,0:T(8,128)} collective-permute-done((f32[520,256]{1,0:T(8,128)S(1)}, f32[520,256]{1,0:T(8,128)}, u32[]{:S(2)}, u32[]{:S(2)}) %collective-permute-start.24) | collective-permute-done | bytes 532512 | tf_op jit(solution)/shard_map/ppermute | solution.py:261
  125.0 7.4 %collective-permute-start.27 = (f32[256,256]{1,0:T(8,128)S(1)}, f32[256,256]{1,0:T(8,128)S(1)}, u32[]{:S(2)}, u32[]{:S(2)}) collective-permute-start(f32[256,256]{1,0:T(8,128)S(1)} %slice_add_fusion.2), channel_id=1, source_target_pairs={{0,8},{8,0},{16,24},{24,16},{1,9},{9,1},{17,25},{25,17},{2,10},{10... | collective-permute-start | bytes 786440 | tf_op jit(solution)/shard_map/ppermute | solution.py:261
  132.9 1.9 %collective-permute-start.32 = (f32[128,256]{1,0:T(8,128)S(1)}, f32[128,256]{1,0:T(8,128)S(1)}, u32[]{:S(2)}, u32[]{:S(2)}) collective-permute-start(f32[128,256]{1,0:T(8,128)S(1)} %slice_add_fusion.5), channel_id=1, source_target_pairs={{0,0},{2,8},{4,16},{6,24},{8,1},{10,9},{12,17},{14,25},{16,2},{18,... | collective-permute-start | bytes 393224 | tf_op jit(solution)/shard_map/ppermute | solution.py:258
  134.8 1.4 collective-permute-done.25
  138.6 4.9 %collective-permute-done.32 = f32[128,256]{1,0:T(8,128)S(1)} collective-permute-done((f32[128,256]{1,0:T(8,128)S(1)}, f32[128,256]{1,0:T(8,128)S(1)}, u32[]{:S(2)}, u32[]{:S(2)}) %collective-permute-start.32) | collective-permute-done | bytes 131104 | tf_op jit(solution)/shard_map/ppermute | solution.py:258
  143.5 3.1 %collective-permute-done.33 = f32[128,256]{1,0:T(8,128)S(1)} collective-permute-done((f32[128,256]{1,0:T(8,128)S(1)}, f32[128,256]{1,0:T(8,128)S(1)}, u32[]{:S(2)}, u32[]{:S(2)}) %collective-permute-start.33) | collective-permute-done | bytes 131104 | tf_op jit(solution)/shard_map/ppermute | solution.py:258
  (93 shorter events, 23.3 us)
Async XLA Ops:
  2.6 4.3 %collective-permute-start = (f32[8,128]{0,1:T(8,128)S(1)}, f32[8,128]{0,1:T(8,128)S(1)}, u32[]{:S(2)}, u32[]{:S(2)}) collective-permute-start(f32[8,128]{0,1:T(8,128)S(1)} %broadcast_in_dim.24), channel_id=1, source_target_pairs={{0,8},{8,0},{16,24},{24,16},{1,9},{9,1},{17,25},{25,17},{2,10},{10... | collective-permute-start | bytes 12296 | tf_op jit(solution)/shard_map/ppermute | solution.py:261
  7.6 4.3 %collective-permute-start.1 = (f32[8,128]{0,1:T(8,128)S(1)}, f32[8,128]{0,1:T(8,128)S(1)}, u32[]{:S(2)}, u32[]{:S(2)}) collective-permute-start(f32[8,128]{0,1:T(8,128)S(1)} %broadcast_add_fusion), channel_id=1, source_target_pairs={{0,16},{8,24},{16,0},{24,8},{1,17},{9,25},{17,1},{25,9},{2,18},{10... | collective-permute-start | bytes 12296 | tf_op jit(solution)/shard_map/ppermute | solution.py:261
  13.7 15.2 %collective-permute-start.2 = (f32[520,256]{1,0:T(8,128)S(1)}, f32[520,256]{1,0:T(8,128)S(1)}, u32[]{:S(2)}, u32[]{:S(2)}) collective-permute-start(f32[520,256]{1,0:T(8,128)S(1)} %pad_maximum_fusion.2.refs_7_), channel_id=1, source_target_pairs={{0,16},{8,24},{16,0},{24,8},{1,17},{9,25},{17,1},{25,9},{2,18},{10... | collective-permute-start | bytes 1597448 | tf_op jit(solution)/shard_map/ppermute | solution.py:261
  14.3 14.7 %collective-permute-start.3 = (f32[520,256]{1,0:T(8,128)S(1)}, f32[520,256]{1,0:T(8,128)S(1)}, u32[]{:S(2)}, u32[]{:S(2)}) collective-permute-start(f32[520,256]{1,0:T(8,128)S(1)} %pad_maximum_fusion.2.refs_7_), channel_id=1, source_target_pairs={{0,8},{8,0},{16,24},{24,16},{1,9},{9,1},{17,25},{25,17},{2,10},{10... | collective-permute-start | bytes 1597448 | tf_op jit(solution)/shard_map/ppermute | solution.py:261
  15.6 11.6 %collective-permute-start.4 = (f32[136,256]{1,0:T(8,128)S(1)}, f32[136,256]{1,0:T(8,128)S(1)}, u32[]{:S(2)}, u32[]{:S(2)}) collective-permute-start(f32[136,256]{1,0:T(8,128)S(1)} %pad_maximum_fusion.5), channel_id=1, source_target_pairs={{0,0},{8,2},{16,4},{24,6},{1,8},{9,10},{17,12},{25,14},{2,16},{10,... | collective-permute-start | bytes 417800 | tf_op jit(solution)/shard_map/ppermute | solution.py:258
  23.4 5.6 %collective-permute-start.5 = (f32[136,256]{1,0:T(8,128)S(1)}, f32[136,256]{1,0:T(8,128)S(1)}, u32[]{:S(2)}, u32[]{:S(2)}) collective-permute-start(f32[136,256]{1,0:T(8,128)S(1)} %pad_maximum_fusion.6), channel_id=1, source_target_pairs={{0,1},{8,3},{16,5},{24,7},{1,9},{9,11},{17,13},{25,15},{2,17},{10,... | collective-permute-start | bytes 417800 | tf_op jit(solution)/shard_map/ppermute | solution.py:258
  29.8 6.9 %collective-permute-start.6 = (f32[136,256]{1,0:T(8,128)S(1)}, f32[136,256]{1,0:T(8,128)S(1)}, u32[]{:S(2)}, u32[]{:S(2)}) collective-permute-start(f32[136,256]{1,0:T(8,128)S(1)} %fusion.1), channel_id=1, source_target_pairs={{0,4},{1,5},{2,6},{3,7},{4,0},{5,1},{6,2},{7,3},{8,12},{9,13},{10,... | collective-permute-start | bytes 417800 | tf_op jit(solution)/shard_map/ppermute | solution.py:261
  33.7 8.3 %collective-permute-start.15 = (f32[264,256]{1,0:T(8,128)S(1)}, f32[264,256]{1,0:T(8,128)S(1)}, u32[]{:S(2)}, u32[]{:S(2)}) collective-permute-start(f32[264,256]{1,0:T(8,128)S(1)} %slice.143), channel_id=1, source_target_pairs={{0,16},{8,24},{16,0},{24,8},{1,17},{9,25},{17,1},{25,9},{2,18},{10... | collective-permute-start | bytes 811016 | tf_op jit(solution)/shard_map/ppermute | solution.py:261
  34.0 7.9 %collective-permute-start.14 = (f32[256,256]{1,0:T(8,128)S(1)}, f32[256,256]{1,0:T(8,128)S(1)}, u32[]{:S(2)}, u32[]{:S(2)}) collective-permute-start(f32[256,256]{1,0:T(8,128)S(1)} %slice.141), channel_id=1, source_target_pairs={{0,8},{8,0},{16,24},{24,16},{1,9},{9,1},{17,25},{25,17},{2,10},{10... | collective-permute-start | bytes 786440 | tf_op jit(solution)/shard_map/ppermute | solution.py:261
  42.0 10.5 %collective-permute-start.16 = (f32[272,256]{1,0:T(8,128)S(1)}, f32[272,256]{1,0:T(8,128)S(1)}, u32[]{:S(2)}, u32[]{:S(2)}) collective-permute-start(f32[272,256]{1,0:T(8,128)S(1)} %pad_maximum_fusion.4.refs_3_), channel_id=1, source_target_pairs={{0,2},{1,3},{2,0},{3,1},{4,6},{5,7},{6,4},{7,5},{8,10},{9,11},{10,... | collective-permute-start | bytes 835592 | tf_op jit(solution)/shard_map/ppermute | solution.py:261
  45.2 10.0 %collective-permute-start.8 = (f32[136,256]{1,0:T(8,128)S(1)}, f32[136,256]{1,0:T(8,128)S(1)}, u32[]{:S(2)}, u32[]{:S(2)}) collective-permute-start(f32[136,256]{1,0:T(8,128)S(1)} %pad_maximum_fusion.8), channel_id=1, source_target_pairs={{0,1},{8,3},{16,5},{24,7},{1,9},{9,11},{17,13},{25,15},{2,17},{10,... | collective-permute-start | bytes 417800 | tf_op jit(solution)/shard_map/ppermute | solution.py:258
  50.1 10.8 %collective-permute-start.7 = (f32[136,256]{1,0:T(8,128)S(1)}, f32[136,256]{1,0:T(8,128)S(1)}, u32[]{:S(2)}, u32[]{:S(2)}) collective-permute-start(f32[136,256]{1,0:T(8,128)S(1)} %pad_maximum_fusion.7), channel_id=1, source_target_pairs={{0,0},{8,2},{16,4},{24,6},{1,8},{9,10},{17,12},{25,14},{2,16},{10,... | collective-permute-start | bytes 417800 | tf_op jit(solution)/shard_map/ppermute | solution.py:258
  52.2 14.5 %collective-permute-start.17 = (f32[272,256]{1,0:T(8,128)S(1)}, f32[272,256]{1,0:T(8,128)S(1)}, u32[]{:S(2)}, u32[]{:S(2)}) collective-permute-start(f32[272,256]{1,0:T(8,128)S(1)} %pad_maximum_fusion.4.refs_3_), channel_id=1, source_target_pairs={{0,1},{1,0},{2,3},{3,2},{4,5},{5,4},{6,7},{7,6},{8,9},{9,8},{10,11... | collective-permute-start | bytes 835592 | tf_op jit(solution)/shard_map/ppermute | solution.py:261
  52.5 14.2 %collective-permute-start.18 = (f32[272,256]{1,0:T(8,128)S(1)}, f32[272,256]{1,0:T(8,128)S(1)}, u32[]{:S(2)}, u32[]{:S(2)}) collective-permute-start(f32[272,256]{1,0:T(8,128)S(1)} %collective-permute-done.16.refs_4_), channel_id=1, source_target_pairs={{0,1},{1,0},{2,3},{3,2},{4,5},{5,4},{6,7},{7,6},{8,9},{9,8},{10,11... | collective-permute-start | bytes 835592 | tf_op jit(solution)/shard_map/ppermute | solution.py:261
  61.0 7.4 %collective-permute-start.10 = (f32[136,256]{1,0:T(8,128)S(1)}, f32[136,256]{1,0:T(8,128)S(1)}, u32[]{:S(2)}, u32[]{:S(2)}) collective-permute-start(f32[136,256]{1,0:T(8,128)S(1)} %broadcast_select_fusion), channel_id=1, source_target_pairs={{0,2},{1,3},{2,0},{3,1},{4,6},{5,7},{6,4},{7,5},{8,10},{9,11},{10,... | collective-permute-start | bytes 417800 | tf_op jit(solution)/shard_map/ppermute | solution.py:261
  61.1 12.6 %collective-permute-start.11 = (f32[136,256]{1,0:T(8,128)S(1)}, f32[136,256]{1,0:T(8,128)S(1)}, u32[]{:S(2)}, u32[]{:S(2)}) collective-permute-start(f32[136,256]{1,0:T(8,128)S(1)} %broadcast_select_fusion), channel_id=1, source_target_pairs={{0,6},{1,7},{2,4},{3,5},{4,2},{5,3},{6,0},{7,1},{8,14},{9,15},{10,... | collective-permute-start | bytes 417800 | tf_op jit(solution)/shard_map/ppermute | solution.py:261
  66.2 13.5 %collective-permute-start.9 = (f32[136,256]{1,0:T(8,128)S(1)}, f32[136,256]{1,0:T(8,128)S(1)}, u32[]{:S(2)}, u32[]{:S(2)}) collective-permute-start(f32[136,256]{1,0:T(8,128)S(1)} %broadcast_select_fusion), channel_id=1, source_target_pairs={{0,4},{1,5},{2,6},{3,7},{4,0},{5,1},{6,2},{7,3},{8,12},{9,13},{10,... | collective-permute-start | bytes 417800 | tf_op jit(solution)/shard_map/ppermute | solution.py:261
  85.7 6.4 %collective-permute-start.13 = (f32[272,256]{1,0:T(8,128)S(1)}, f32[272,256]{1,0:T(8,128)S(1)}, u32[]{:S(2)}, u32[]{:S(2)}) collective-permute-start(f32[272,256]{1,0:T(8,128)S(1)} %constant_dynamic-update-slice_fusion.refs_4_), channel_id=1, source_target_pairs={{0,1},{1,0},{2,3},{3,2},{4,5},{5,4},{6,7},{7,6},{8,9},{9,8},{10,11... | collective-permute-start | bytes 835592 | tf_op jit(solution)/shard_map/ppermute | solution.py:261
  86.2 5.8 %collective-permute-start.12 = (f32[272,256]{1,0:T(8,128)S(1)}, f32[272,256]{1,0:T(8,128)S(1)}, u32[]{:S(2)}, u32[]{:S(2)}) collective-permute-start(f32[272,256]{1,0:T(8,128)S(1)} %pad_maximum_fusion.3.refs_3_), channel_id=1, source_target_pairs={{0,1},{1,0},{2,3},{3,2},{4,5},{5,4},{6,7},{7,6},{8,9},{9,8},{10,11... | collective-permute-start | bytes 835592 | tf_op jit(solution)/shard_map/ppermute | solution.py:261
  87.6 7.9 %collective-permute-start.20 = (f32[128,256]{1,0:T(8,128)S(1)}, f32[128,256]{1,0:T(8,128)S(1)}, u32[]{:S(2)}, u32[]{:S(2)}) collective-permute-start(f32[128,256]{1,0:T(8,128)S(1)} %get-tuple-element.44), channel_id=1, source_target_pairs={{0,2},{1,3},{2,0},{3,1},{4,6},{5,7},{6,4},{7,5},{8,10},{9,11},{10,... | collective-permute-start | bytes 393224 | tf_op jit(solution)/shard_map/ppermute | solution.py:261
  87.7 13.2 %collective-permute-start.21 = (f32[128,256]{1,0:T(8,128)S(1)}, f32[128,256]{1,0:T(8,128)S(1)}, u32[]{:S(2)}, u32[]{:S(2)}) collective-permute-start(f32[128,256]{1,0:T(8,128)S(1)} %get-tuple-element.46), channel_id=1, source_target_pairs={{0,4},{1,5},{2,6},{3,7},{4,0},{5,1},{6,2},{7,3},{8,12},{9,13},{10,... | collective-permute-start | bytes 393224 | tf_op jit(solution)/shard_map/ppermute | solution.py:261
  90.9 10.0 %collective-permute-start.22 = (f32[128,256]{1,0:T(8,128)S(1)}, f32[128,256]{1,0:T(8,128)S(1)}, u32[]{:S(2)}, u32[]{:S(2)}) collective-permute-start(f32[128,256]{1,0:T(8,128)S(1)} %get-tuple-element.45), channel_id=1, source_target_pairs={{0,6},{1,7},{2,4},{3,5},{4,2},{5,3},{6,0},{7,1},{8,14},{9,15},{10,... | collective-permute-start | bytes 393224 | tf_op jit(solution)/shard_map/ppermute | solution.py:261
  109.4 8.4 %collective-permute-start.28 = (f32[256,256]{1,0:T(8,128)S(1)}, f32[256,256]{1,0:T(8,128)S(1)}, u32[]{:S(2)}, u32[]{:S(2)}) collective-permute-start(f32[256,256]{1,0:T(8,128)S(1)} %slice.154), channel_id=1, source_target_pairs={{0,2},{1,3},{2,0},{3,1},{4,6},{5,7},{6,4},{7,5},{8,10},{9,11},{10,... | collective-permute-start | bytes 786440 | tf_op jit(solution)/shard_map/ppermute | solution.py:261
  109.5 14.3 %collective-permute-start.24 = (f32[520,256]{1,0:T(8,128)S(1)}, f32[520,256]{1,0:T(8,128)}, u32[]{:S(2)}, u32[]{:S(2)}) collective-permute-start(f32[520,256]{1,0:T(8,128)S(1)} %get-tuple-element.55), channel_id=1, source_target_pairs={{0,8},{8,0},{16,24},{24,16},{1,9},{9,1},{17,25},{25,17},{2,10},{10... | collective-permute-start | bytes 1597448 | tf_op jit(solution)/shard_map/ppermute | solution.py:261
  109.6 15.3 %collective-permute-start.26 = (f32[520,256]{1,0:T(8,128)S(1)}, f32[520,256]{1,0:T(8,128)S(1)}, u32[]{:S(2)}, u32[]{:S(2)}) collective-permute-start(f32[520,256]{1,0:T(8,128)S(1)} %get-tuple-element.56), channel_id=1, source_target_pairs={{0,16},{8,24},{16,0},{24,8},{1,17},{9,25},{17,1},{25,9},{2,18},{10... | collective-permute-start | bytes 1597448 | tf_op jit(solution)/shard_map/ppermute | solution.py:261
  117.8 20.8 %collective-permute-start.29 = (f32[128,256]{1,0:T(8,128)S(1)}, f32[128,256]{1,0:T(8,128)S(1)}, u32[]{:S(2)}, u32[]{:S(2)}) collective-permute-start(f32[128,256]{1,0:T(8,128)S(1)} %get-tuple-element.51), channel_id=1, source_target_pairs={{0,0},{2,8},{4,16},{6,24},{8,1},{10,9},{12,17},{14,25},{16,2},{18,... | collective-permute-start | bytes 393224 | tf_op jit(solution)/shard_map/ppermute | solution.py:258
  119.7 18.9 %collective-permute-start.30 = (f32[128,256]{1,0:T(8,128)S(1)}, f32[128,256]{1,0:T(8,128)S(1)}, u32[]{:S(2)}, u32[]{:S(2)}) collective-permute-start(f32[128,256]{1,0:T(8,128)S(1)} %get-tuple-element.52), channel_id=1, source_target_pairs={{1,0},{3,8},{5,16},{7,24},{9,1},{11,9},{13,17},{15,25},{17,2},{19,... | collective-permute-start | bytes 393224 | tf_op jit(solution)/shard_map/ppermute | solution.py:258
  121.1 11.8 %collective-permute-start.31 = (f32[128,256]{1,0:T(8,128)S(1)}, f32[128,256]{1,0:T(8,128)S(1)}, u32[]{:S(2)}, u32[]{:S(2)}) collective-permute-start(f32[128,256]{1,0:T(8,128)S(1)} %slice.158), channel_id=1, source_target_pairs={{0,4},{1,5},{2,6},{3,7},{4,0},{5,1},{6,2},{7,3},{8,12},{9,13},{10,... | collective-permute-start | bytes 393224 | tf_op jit(solution)/shard_map/ppermute | solution.py:261
  124.8 11.4 %collective-permute-start.25 = (f32[256,256]{1,0:T(8,128)S(1)}, f32[256,256]{1,0:T(8,128)S(1)}, u32[]{:S(2)}, u32[]{:S(2)}) collective-permute-start(f32[256,256]{1,0:T(8,128)S(1)} %slice_add_fusion.3), channel_id=1, source_target_pairs={{0,16},{8,24},{16,0},{24,8},{1,17},{9,25},{17,1},{25,9},{2,18},{10... | collective-permute-start | bytes 786440 | tf_op jit(solution)/shard_map/ppermute | solution.py:261
  125.0 13.6 %collective-permute-start.27 = (f32[256,256]{1,0:T(8,128)S(1)}, f32[256,256]{1,0:T(8,128)S(1)}, u32[]{:S(2)}, u32[]{:S(2)}) collective-permute-start(f32[256,256]{1,0:T(8,128)S(1)} %slice_add_fusion.2), channel_id=1, source_target_pairs={{0,8},{8,0},{16,24},{24,16},{1,9},{9,1},{17,25},{25,17},{2,10},{10... | collective-permute-start | bytes 786440 | tf_op jit(solution)/shard_map/ppermute | solution.py:261
  132.9 10.6 %collective-permute-start.32 = (f32[128,256]{1,0:T(8,128)S(1)}, f32[128,256]{1,0:T(8,128)S(1)}, u32[]{:S(2)}, u32[]{:S(2)}) collective-permute-start(f32[128,256]{1,0:T(8,128)S(1)} %slice_add_fusion.5), channel_id=1, source_target_pairs={{0,0},{2,8},{4,16},{6,24},{8,1},{10,9},{12,17},{14,25},{16,2},{18,... | collective-permute-start | bytes 393224 | tf_op jit(solution)/shard_map/ppermute | solution.py:258
  136.3 10.4 %collective-permute-start.33 = (f32[128,256]{1,0:T(8,128)S(1)}, f32[128,256]{1,0:T(8,128)S(1)}, u32[]{:S(2)}, u32[]{:S(2)}) collective-permute-start(f32[128,256]{1,0:T(8,128)S(1)} %slice_add_fusion.5), channel_id=1, source_target_pairs={{1,0},{3,8},{5,16},{7,24},{9,1},{11,9},{13,17},{15,25},{17,2},{19,... | collective-permute-start | bytes 393224 | tf_op jit(solution)/shard_map/ppermute | solution.py:258
  (5 other events, 93.4 us)

commit v3 on v1

--- a/solution.py
+++ b/solution.py
@@ -9,7 +9,7 @@
 
 BLOCK = 1024
 LEARN_RATE = 0.05
-SUB = 512
+SUB = 1024
 PAD = 8
 VMEM_LIMIT = 42 * 2**20
 
@@ -319,6 +319,14 @@
     listed = jnp.sum((listing[None, :] == jnp.arange(listing.shape[0])[:, None]).astype(jnp.int32), axis=1)
     place = jnp.stack([g, chip, core]).astype(jnp.int32)
 
+    def from_line_at_once(outs):
+        summed = outs[0] + across(outs[1])
+        parts = {d: summed[j * quarter : (j + 1) * quarter] for j, d in enumerate(order_of(groups))}
+        total = parts[0]
+        for d in range(1, groups):
+            total = total + swapped(parts[d], "col", 2 * d)
+        return summed, total
+
     def from_line(outs):
         summed = total = outs[0] + across(outs[1])
         step = 1
@@ -340,13 +348,13 @@
     outs = grads(0, tiles=tiles[:-1], vectors=vectors, held=held, row_in=None, ready=[lower])
     columns = outs[1:4]
     outs = grads(0, tiles=tiles[-1:], vectors=vectors, held=outs[1:], row_in=outs[0], ready=[upper])
-    first_summed, first_total = from_line(outs)
+    first_summed, first_total = from_line_at_once(outs)
     vectors = [lower, upper, across(lower), across(upper)]
     outs = grads(1, tiles=tiles[:-1], vectors=vectors, held=[*columns, outs[2]], row_in=None, ready=[first_summed])
     outs = grads(1, tiles=tiles[-1:], vectors=vectors, held=[*columns, outs[1]], row_in=outs[0], ready=[first_total])
     second_summed, second_total = from_line(outs)
-    first_quarters = to_home(first_total)
-    quarters = first_quarters + to_home(second_total)
+    homes = to_home(jnp.concatenate([first_total, second_total], axis=0))
+    quarters = [home[at : at + quarter] for at in (0, quarter) for home in homes]
 
     halves = outs[2:]
     if groups == 4:

time: 144 us -> 145 us (level)
  the two profiles are of different devices: /device:TPU:2 before, /device:TPU:4 now
where the time goes in v3:
time: 145 us; the launch traced here: 147 us
  starting transfers between devices  65.2 us (45%)
  waiting for transfers between devices  57.6 us (40%)
  Pallas kernels  14.3 us (10%)
  other arithmetic  6.35 us (4%)
  local copies, waits for them, and re-layouts  2.46 us (2%)
    ppermute x25, starting transfers between devices, swapped(): lax.ppermute(value, axis, [(r, r ^ m) for r in range(lax.axis_size(axis))])  50.1 us
    ppermute x25, waiting for transfers between devices, swapped(): lax.ppermute(value, axis, [(r, r ^ m) for r in range(lax.axis_size(axis))])  31.2 us
    ppermute x6, waiting for transfers between devices, permute(): return lax.ppermute(value, both, pairs)  26.4 us
    ppermute x6, starting transfers between devices, permute(): return lax.ppermute(value, both, pairs)  15.1 us
    pallas_call x4, Pallas kernels, half_grads(): pl.pallas_call(functools.partial(half_kernel, k, groups, share, layout, t...  14.3 us
  transfers between devices with their start and end apart: 31, of which 15 were waited for; matrix products, arithmetic and copies ran while one was open for 3% of the time, Pallas kernels for 8%

profile of v3, /device:TPU:4, one launch (start us, length us, event | category | flops | bytes accessed | tf_op | source)
XLA Modules:
  0.0 146.9 jit_solution(6554884972302984776)
XLA Ops:
  3.1 2.0 %collective-permute-start.7 = (f32[520,256]{1,0:T(8,128)S(1)}, f32[520,256]{1,0:T(8,128)S(1)}, u32[]{:S(2)}, u32[]{:S(2)}) collective-permute-start(f32[520,256]{1,0:T(8,128)S(1)} %select_maximum_fusion.refs_7_), channel_id=1, source_target_pairs={{0,8},{8,0},{16,24},{24,16},{1,9},{9,1},{17,25},{25,17},{2,10},{10... | collective-permute-start | bytes 1597448 | tf_op jit(solution)/shard_map/ppermute | solution.py:261
  7.1 5.9 %collective-permute-start.10 = (f32[136,256]{1,0:T(8,128)S(1)}, f32[136,256]{1,0:T(8,128)S(1)}, u32[]{:S(2)}, u32[]{:S(2)}) collective-permute-start(f32[136,256]{1,0:T(8,128)S(1)} %select_maximum_fusion.2), channel_id=1, source_target_pairs={{0,0},{8,2},{16,4},{24,6},{1,8},{9,10},{17,12},{25,14},{2,16},{10,... | collective-permute-start | bytes 417800 | tf_op jit(solution)/shard_map/ppermute | solution.py:258
  13.0 1.3 collective-permute-start.11
  14.3 2.8 %collective-permute-done.8 = f32[8,128]{1,0:T(8,128)S(1)} collective-permute-done((f32[8,128]{1,0:T(8,128)S(1)}, f32[8,128]{1,0:T(8,128)S(1)}, u32[]{:S(2)}, u32[]{:S(2)}) %collective-permute-start.8) | collective-permute-done | bytes 4128 | tf_op jit(solution)/shard_map/ppermute | solution.py:261
  17.7 4.0 %collective-permute-start.9 = (f32[8,128]{1,0:T(8,128)S(1)}, f32[8,128]{1,0:T(8,128)S(1)}, u32[]{:S(2)}, u32[]{:S(2)}) collective-permute-start(f32[8,128]{1,0:T(8,128)S(1)} %broadcast_add_fusion), channel_id=1, source_target_pairs={{0,16},{8,24},{16,0},{24,8},{1,17},{9,25},{17,1},{25,9},{2,18},{10... | collective-permute-start | bytes 12296 | tf_op jit(solution)/shard_map/ppermute | solution.py:261
  21.8 1.6 %collective-permute-done.9 = f32[8,128]{1,0:T(8,128)S(1)} collective-permute-done((f32[8,128]{1,0:T(8,128)S(1)}, f32[8,128]{1,0:T(8,128)S(1)}, u32[]{:S(2)}, u32[]{:S(2)}) %collective-permute-start.9) | collective-permute-done | bytes 4128 | tf_op jit(solution)/shard_map/ppermute | solution.py:261
  24.6 2.0 %collective-permute-start.13 = (f32[264,256]{1,0:T(8,128)S(1)}, f32[264,256]{1,0:T(8,128)S(1)}, u32[]{:S(2)}, u32[]{:S(2)}) collective-permute-start(f32[264,256]{1,0:T(8,128)S(1)} %slice.143), channel_id=1, source_target_pairs={{0,16},{8,24},{16,0},{24,8},{1,17},{9,25},{17,1},{25,9},{2,18},{10... | collective-permute-start | bytes 811016 | tf_op jit(solution)/shard_map/ppermute | solution.py:261
  26.7 3.1 %collective-permute-start.12 = (f32[256,256]{1,0:T(8,128)S(1)}, f32[256,256]{1,0:T(8,128)S(1)}, u32[]{:S(2)}, u32[]{:S(2)}) collective-permute-start(f32[256,256]{1,0:T(8,128)S(1)} %slice.141), channel_id=1, source_target_pairs={{0,8},{8,0},{16,24},{24,16},{1,9},{9,1},{17,25},{25,17},{2,10},{10... | collective-permute-start | bytes 786440 | tf_op jit(solution)/shard_map/ppermute | solution.py:261
  30.5 1.4 collective-permute-start.14
  32.0 3.4 %collective-permute-start = (f32[136,256]{1,0:T(8,128)S(1)}, f32[136,256]{1,0:T(8,128)S(1)}, u32[]{:S(2)}, u32[]{:S(2)}) collective-permute-start(f32[136,256]{1,0:T(8,128)S(1)} %select_maximum_fusion.4), channel_id=1, source_target_pairs={{0,0},{8,2},{16,4},{24,6},{1,8},{9,10},{17,12},{25,14},{2,16},{10,... | collective-permute-start | bytes 417800 | tf_op jit(solution)/shard_map/ppermute | solution.py:258
  35.4 1.3 collective-permute-start.1
  37.5 2.8 %collective-permute-done = f32[136,256]{1,0:T(8,128)S(1)} collective-permute-done((f32[136,256]{1,0:T(8,128)S(1)}, f32[136,256]{1,0:T(8,128)S(1)}, u32[]{:S(2)}, u32[]{:S(2)}) %collective-permute-start) | collective-permute-done | bytes 139296 | tf_op jit(solution)/shard_map/ppermute | solution.py:258
  40.2 2.2 %collective-permute-done.1 = f32[136,256]{1,0:T(8,128)S(1)} collective-permute-done((f32[136,256]{1,0:T(8,128)S(1)}, f32[136,256]{1,0:T(8,128)S(1)}, u32[]{:S(2)}, u32[]{:S(2)}) %collective-permute-start.1) | collective-permute-done | bytes 139296 | tf_op jit(solution)/shard_map/ppermute | solution.py:258
  42.4 5.4 %collective-permute-start.2 = (f32[136,256]{1,0:T(8,128)S(1)}, f32[136,256]{1,0:T(8,128)S(1)}, u32[]{:S(2)}, u32[]{:S(2)}) collective-permute-start(f32[136,256]{1,0:T(8,128)S(1)} %broadcast_select_fusion), channel_id=1, source_target_pairs={{0,4},{1,5},{2,6},{3,7},{4,0},{5,1},{6,2},{7,3},{8,12},{9,13},{10,... | collective-permute-start | bytes 417800 | tf_op jit(solution)/shard_map/ppermute | solution.py:261
  47.8 1.7 %collective-permute-start.16 = (f32[272,256]{1,0:T(8,128)S(1)}, f32[272,256]{1,0:T(8,128)S(1)}, u32[]{:S(2)}, u32[]{:S(2)}) collective-permute-start(f32[272,256]{1,0:T(8,128)S(1)} %pad_maximum_fusion.3.refs_3_), channel_id=1, source_target_pairs={{0,1},{1,0},{2,3},{3,2},{4,5},{5,4},{6,7},{7,6},{8,9},{9,8},{10,11... | collective-permute-start | bytes 835592 | tf_op jit(solution)/shard_map/ppermute | solution.py:261
  49.7 1.4 collective-permute-done.2
  51.1 5.1 %collective-permute-start.3 = (f32[272,256]{1,0:T(8,128)S(1)}, f32[272,256]{1,0:T(8,128)S(1)}, u32[]{:S(2)}, u32[]{:S(2)}) collective-permute-start(f32[272,256]{1,0:T(8,128)S(1)} %pad_maximum_fusion.2.refs_12_.refs_3_), channel_id=1, source_target_pairs={{0,2},{1,3},{2,0},{3,1},{4,6},{5,7},{6,4},{7,5},{8,10},{9,11},{10,... | collective-permute-start | bytes 835592 | tf_op jit(solution)/shard_map/ppermute | solution.py:261
  56.2 5.9 %half_grads.4 = (f32[1024,256]{1,0:T(8,128)S(1)}, bf16[2048,256]{1,0:T(8,128)(2,1)S(1)}, bf16[2048,256]{1,0:T(8,128)(2,1)S(1)}, f32[32,256]{1,0:T(8,128)S(1)}, f32[256,2048]{1,0:T(8,128)S(1)}) custom-call(s32[3]{0:T(128)S(1)} %pad_add_fusion.refs_0_, s32[4]{0:T(128)S(1)} %convert_reduce_fusion.1.refs_1_, s32[2048,2048]{1,0:T(8,128)} %refs_2_.7, ...), custom_call_target="tpu_custom_call" | custom-call | flops 7247757312 | bytes 10485760 | tf_op jit(solution)/shard_map/half_grads/pallas_call | solution.py:228
  62.1 1.5 %collective-permute-done.3.refs_12_.refs_4_ = f32[272,256]{1,0:T(8,128)S(1)} collective-permute-done((f32[272,256]{1,0:T(8,128)S(1)}, f32[272,256]{1,0:T(8,128)S(1)}, u32[]{:S(2)}, u32[]{:S(2)}) %collective-permute-start.3) | collective-permute-done | bytes 278560 | tf_op jit(solution)/shard_map/ppermute | solution.py:261
  64.6 10.2 %collective-permute-start.18 = (f32[512,256]{1,0:T(8,128)S(1)}, f32[512,256]{1,0:T(8,128)S(1)}, u32[]{:S(2)}, u32[]{:S(2)}) collective-permute-start(f32[512,256]{1,0:T(8,128)S(1)} %get-tuple-element.29), channel_id=1, source_target_pairs={{0,1},{1,0},{2,3},{3,2},{4,5},{5,4},{6,7},{7,6},{8,9},{9,8},{10,11... | collective-permute-start | bytes 1572872 | tf_op jit(solution)/shard_map/ppermute | solution.py:261
  76.5 4.3 %collective-permute-start.21 = (f32[128,256]{1,0:T(8,128)S(1)}, f32[128,256]{1,0:T(8,128)S(1)}, u32[]{:S(2)}, u32[]{:S(2)}) collective-permute-start(f32[128,256]{1,0:T(8,128)S(1)} %get-tuple-element.45), channel_id=1, source_target_pairs={{0,6},{1,7},{2,4},{3,5},{4,2},{5,3},{6,0},{7,1},{8,14},{9,15},{10,... | collective-permute-start | bytes 393224 | tf_op jit(solution)/shard_map/ppermute | solution.py:261
  80.9 5.9 %half_grads.6 = (f32[1024,256]{1,0:T(8,128)S(1)}, f32[256,2048]{1,0:T(8,128)S(1)}) custom-call(s32[3]{0:T(128)S(1)} %pad_add_fusion.refs_0_, s32[4]{0:T(128)S(1)} %convert_reduce_fusion.1.refs_1_, s32[2048,2048]{1,0:T(8,128)} %refs_2_.7, f32[272,256]{1,0:T(8,128)S(1)} %pad_maximum_fusion.2.refs_12_.refs_3_, ...), custom_call_target="tpu_custom_call" | custom-call | flops 7247757312 | bytes 10485760 | tf_op jit(solution)/shard_map/half_grads/pallas_call | solution.py:228
  86.8 2.7 %collective-permute-done.20 = f32[128,256]{1,0:T(8,128)S(1)} collective-permute-done((f32[128,256]{1,0:T(8,128)S(1)}, f32[128,256]{1,0:T(8,128)S(1)}, u32[]{:S(2)}, u32[]{:S(2)}) %collective-permute-start.20) | collective-permute-done | bytes 131104 | tf_op jit(solution)/shard_map/ppermute | solution.py:261
  89.5 1.5 %half_grads.7 = (f32[512,256]{1,0:T(8,128)S(1)}, f32[512,256]{1,0:T(8,128)S(1)}, f32[256,256]{1,0:T(8,128)S(1)}, f32[256,256]{1,0:T(8,128)S(1)}, f32[256,256]{1,...) custom-call(s32[3]{0:T(128)S(1)} %pad_add_fusion.refs_0_, ...), custom_call_target="tpu_custom_call" | custom-call | flops 2415919104 | bytes 6291456 | tf_op jit(solution)/shard_map/half_grads/pallas_call | solution.py:228
  91.0 8.5 %collective-permute-start.22 = (f32[512,256]{1,0:T(8,128)S(1)}, f32[512,256]{1,0:T(8,128)S(1)}, u32[]{:S(2)}, u32[]{:S(2)}) collective-permute-start(f32[512,256]{1,0:T(8,128)S(1)} %get-tuple-element.36), channel_id=1, source_target_pairs={{0,1},{1,0},{2,3},{3,2},{4,5},{5,4},{6,7},{7,6},{8,9},{9,8},{10,11... | collective-permute-start | bytes 1572872 | tf_op jit(solution)/shard_map/ppermute | solution.py:261
  99.5 1.5 %collective-permute-done.22 = f32[512,256]{1,0:T(8,128)S(1)} collective-permute-done((f32[512,256]{1,0:T(8,128)S(1)}, f32[512,256]{1,0:T(8,128)S(1)}, u32[]{:S(2)}, u32[]{:S(2)}) %collective-permute-start.22) | collective-permute-done | bytes 524320 | tf_op jit(solution)/shard_map/ppermute | solution.py:261
  101.4 8.4 %collective-permute-done.27 = f32[256,256]{1,0:T(8,128)S(1)} collective-permute-done((f32[256,256]{1,0:T(8,128)S(1)}, f32[256,256]{1,0:T(8,128)S(1)}, u32[]{:S(2)}, u32[]{:S(2)}) %collective-permute-start.27) | collective-permute-done | bytes 262176 | tf_op jit(solution)/shard_map/ppermute | solution.py:261
  110.0 8.5 %collective-permute-done.28 = f32[128,256]{1,0:T(8,128)S(1)} collective-permute-done((f32[128,256]{1,0:T(8,128)S(1)}, f32[128,256]{1,0:T(8,128)S(1)}, u32[]{:S(2)}, u32[]{:S(2)}) %collective-permute-start.28) | collective-permute-done | bytes 131104 | tf_op jit(solution)/shard_map/ppermute | solution.py:261
  118.6 1.9 %collective-permute-start.29 = (f32[256,256]{1,0:T(8,128)S(1)}, f32[256,256]{1,0:T(8,128)S(1)}, u32[]{:S(2)}, u32[]{:S(2)}) collective-permute-start(f32[256,256]{1,0:T(8,128)S(1)} %pad_maximum_fusion.4), channel_id=1, source_target_pairs={{0,0},{2,8},{4,16},{6,24},{8,1},{10,9},{12,17},{14,25},{16,2},{18,... | collective-permute-start | bytes 786440 | tf_op jit(solution)/shard_map/ppermute | solution.py:258
  120.5 1.3 collective-permute-start.30
  122.0 1.6 %collective-permute-done.25 = f32[520,256]{1,0:T(8,128)S(1)} collective-permute-done((f32[520,256]{1,0:T(8,128)S(1)}, f32[520,256]{1,0:T(8,128)S(1)}, u32[]{:S(2)}, u32[]{:S(2)}) %collective-permute-start.25) | collective-permute-done | bytes 532512 | tf_op jit(solution)/shard_map/ppermute | solution.py:261
  124.1 21.3 %collective-permute-done.29 = f32[256,256]{1,0:T(8,128)S(1)} collective-permute-done((f32[256,256]{1,0:T(8,128)S(1)}, f32[256,256]{1,0:T(8,128)S(1)}, u32[]{:S(2)}, u32[]{:S(2)}) %collective-permute-start.29) | collective-permute-done | bytes 262176 | tf_op jit(solution)/shard_map/ppermute | solution.py:258
  (83 shorter events, 13.6 us)
Async XLA Ops:
  3.0 23.6 %collective-permute-start.6 = (f32[520,256]{1,0:T(8,128)S(1)}, f32[520,256]{1,0:T(8,128)S(1)}, u32[]{:S(2)}, u32[]{:S(2)}) collective-permute-start(f32[520,256]{1,0:T(8,128)S(1)} %select_maximum_fusion.refs_7_), channel_id=1, source_target_pairs={{0,16},{8,24},{16,0},{24,8},{1,17},{9,25},{17,1},{25,9},{2,18},{10... | collective-permute-start | bytes 1597448 | tf_op jit(solution)/shard_map/ppermute | solution.py:261
  3.1 21.5 %collective-permute-start.7 = (f32[520,256]{1,0:T(8,128)S(1)}, f32[520,256]{1,0:T(8,128)S(1)}, u32[]{:S(2)}, u32[]{:S(2)}) collective-permute-start(f32[520,256]{1,0:T(8,128)S(1)} %select_maximum_fusion.refs_7_), channel_id=1, source_target_pairs={{0,8},{8,0},{16,24},{24,16},{1,9},{9,1},{17,25},{25,17},{2,10},{10... | collective-permute-start | bytes 1597448 | tf_op jit(solution)/shard_map/ppermute | solution.py:261
  5.7 11.3 %collective-permute-start.8 = (f32[8,128]{1,0:T(8,128)S(1)}, f32[8,128]{1,0:T(8,128)S(1)}, u32[]{:S(2)}, u32[]{:S(2)}) collective-permute-start(f32[8,128]{1,0:T(8,128)S(1)} %broadcast_in_dim.8), channel_id=1, source_target_pairs={{0,8},{8,0},{16,24},{24,16},{1,9},{9,1},{17,25},{25,17},{2,10},{10... | collective-permute-start | bytes 12296 | tf_op jit(solution)/shard_map/ppermute | solution.py:261
  7.0 42.5 %copy-start.2 = (s32[1,1,4]{2,1,0:T(1,128)S(1)}, s32[1,1,4]{2,1,0:T(1,128)}, u32[]{:S(2)}) copy-start(s32[1,1,4]{2,1,0:T(1,128)} %param.6) | copy-start | bytes 52
  7.1 22.6 %collective-permute-start.10 = (f32[136,256]{1,0:T(8,128)S(1)}, f32[136,256]{1,0:T(8,128)S(1)}, u32[]{:S(2)}, u32[]{:S(2)}) collective-permute-start(f32[136,256]{1,0:T(8,128)S(1)} %select_maximum_fusion.2), channel_id=1, source_target_pairs={{0,0},{8,2},{16,4},{24,6},{1,8},{9,10},{17,12},{25,14},{2,16},{10,... | collective-permute-start | bytes 417800 | tf_op jit(solution)/shard_map/ppermute | solution.py:258
  13.0 16.7 %collective-permute-start.11 = (f32[136,256]{1,0:T(8,128)S(1)}, f32[136,256]{1,0:T(8,128)S(1)}, u32[]{:S(2)}, u32[]{:S(2)}) collective-permute-start(f32[136,256]{1,0:T(8,128)S(1)} %select_maximum_fusion.1), channel_id=1, source_target_pairs={{0,1},{8,3},{16,5},{24,7},{1,9},{9,11},{17,13},{25,15},{2,17},{10,... | collective-permute-start | bytes 417800 | tf_op jit(solution)/shard_map/ppermute | solution.py:258
  17.7 5.7 %collective-permute-start.9 = (f32[8,128]{1,0:T(8,128)S(1)}, f32[8,128]{1,0:T(8,128)S(1)}, u32[]{:S(2)}, u32[]{:S(2)}) collective-permute-start(f32[8,128]{1,0:T(8,128)S(1)} %broadcast_add_fusion), channel_id=1, source_target_pairs={{0,16},{8,24},{16,0},{24,8},{1,17},{9,25},{17,1},{25,9},{2,18},{10... | collective-permute-start | bytes 12296 | tf_op jit(solution)/shard_map/ppermute | solution.py:261
  24.6 12.1 %collective-permute-start.13 = (f32[264,256]{1,0:T(8,128)S(1)}, f32[264,256]{1,0:T(8,128)S(1)}, u32[]{:S(2)}, u32[]{:S(2)}) collective-permute-start(f32[264,256]{1,0:T(8,128)S(1)} %slice.143), channel_id=1, source_target_pairs={{0,16},{8,24},{16,0},{24,8},{1,17},{9,25},{17,1},{25,9},{2,18},{10... | collective-permute-start | bytes 811016 | tf_op jit(solution)/shard_map/ppermute | solution.py:261
  26.7 10.0 %collective-permute-start.12 = (f32[256,256]{1,0:T(8,128)S(1)}, f32[256,256]{1,0:T(8,128)S(1)}, u32[]{:S(2)}, u32[]{:S(2)}) collective-permute-start(f32[256,256]{1,0:T(8,128)S(1)} %slice.141), channel_id=1, source_target_pairs={{0,8},{8,0},{16,24},{24,16},{1,9},{9,1},{17,25},{25,17},{2,10},{10... | collective-permute-start | bytes 786440 | tf_op jit(solution)/shard_map/ppermute | solution.py:261
  30.5 6.3 %collective-permute-start.14 = (f32[136,256]{1,0:T(8,128)S(1)}, f32[136,256]{1,0:T(8,128)S(1)}, u32[]{:S(2)}, u32[]{:S(2)}) collective-permute-start(f32[136,256]{1,0:T(8,128)S(1)} %fusion.1), channel_id=1, source_target_pairs={{0,4},{1,5},{2,6},{3,7},{4,0},{5,1},{6,2},{7,3},{8,12},{9,13},{10,... | collective-permute-start | bytes 417800 | tf_op jit(solution)/shard_map/ppermute | solution.py:261
  32.0 8.3 %collective-permute-start = (f32[136,256]{1,0:T(8,128)S(1)}, f32[136,256]{1,0:T(8,128)S(1)}, u32[]{:S(2)}, u32[]{:S(2)}) collective-permute-start(f32[136,256]{1,0:T(8,128)S(1)} %select_maximum_fusion.4), channel_id=1, source_target_pairs={{0,0},{8,2},{16,4},{24,6},{1,8},{9,10},{17,12},{25,14},{2,16},{10,... | collective-permute-start | bytes 417800 | tf_op jit(solution)/shard_map/ppermute | solution.py:258
  35.4 7.0 %collective-permute-start.1 = (f32[136,256]{1,0:T(8,128)S(1)}, f32[136,256]{1,0:T(8,128)S(1)}, u32[]{:S(2)}, u32[]{:S(2)}) collective-permute-start(f32[136,256]{1,0:T(8,128)S(1)} %select_maximum_fusion.3), channel_id=1, source_target_pairs={{0,1},{8,3},{16,5},{24,7},{1,9},{9,11},{17,13},{25,15},{2,17},{10,... | collective-permute-start | bytes 417800 | tf_op jit(solution)/shard_map/ppermute | solution.py:258
  36.8 12.7 %collective-permute-start.15 = (f32[272,256]{1,0:T(8,128)S(1)}, f32[272,256]{1,0:T(8,128)S(1)}, u32[]{:S(2)}, u32[]{:S(2)}) collective-permute-start(f32[272,256]{1,0:T(8,128)S(1)} %pad_maximum_fusion.3.refs_3_), channel_id=1, source_target_pairs={{0,2},{1,3},{2,0},{3,1},{4,6},{5,7},{6,4},{7,5},{8,10},{9,11},{10,... | collective-permute-start | bytes 835592 | tf_op jit(solution)/shard_map/ppermute | solution.py:261
  42.4 8.6 %collective-permute-start.2 = (f32[136,256]{1,0:T(8,128)S(1)}, f32[136,256]{1,0:T(8,128)S(1)}, u32[]{:S(2)}, u32[]{:S(2)}) collective-permute-start(f32[136,256]{1,0:T(8,128)S(1)} %broadcast_select_fusion), channel_id=1, source_target_pairs={{0,4},{1,5},{2,6},{3,7},{4,0},{5,1},{6,2},{7,3},{8,12},{9,13},{10,... | collective-permute-start | bytes 417800 | tf_op jit(solution)/shard_map/ppermute | solution.py:261
  47.8 8.4 %collective-permute-start.16 = (f32[272,256]{1,0:T(8,128)S(1)}, f32[272,256]{1,0:T(8,128)S(1)}, u32[]{:S(2)}, u32[]{:S(2)}) collective-permute-start(f32[272,256]{1,0:T(8,128)S(1)} %pad_maximum_fusion.3.refs_3_), channel_id=1, source_target_pairs={{0,1},{1,0},{2,3},{3,2},{4,5},{5,4},{6,7},{7,6},{8,9},{9,8},{10,11... | collective-permute-start | bytes 835592 | tf_op jit(solution)/shard_map/ppermute | solution.py:261
  49.5 6.7 %collective-permute-start.17 = (f32[272,256]{1,0:T(8,128)S(1)}, f32[272,256]{1,0:T(8,128)S(1)}, u32[]{:S(2)}, u32[]{:S(2)}) collective-permute-start(f32[272,256]{1,0:T(8,128)S(1)} %collective-permute-done.15.refs_4_), channel_id=1, source_target_pairs={{0,1},{1,0},{2,3},{3,2},{4,5},{5,4},{6,7},{7,6},{8,9},{9,8},{10,11... | collective-permute-start | bytes 835592 | tf_op jit(solution)/shard_map/ppermute | solution.py:261
  51.1 12.5 %collective-permute-start.3 = (f32[272,256]{1,0:T(8,128)S(1)}, f32[272,256]{1,0:T(8,128)S(1)}, u32[]{:S(2)}, u32[]{:S(2)}) collective-permute-start(f32[272,256]{1,0:T(8,128)S(1)} %pad_maximum_fusion.2.refs_12_.refs_3_), channel_id=1, source_target_pairs={{0,2},{1,3},{2,0},{3,1},{4,6},{5,7},{6,4},{7,5},{8,10},{9,11},{10,... | collective-permute-start | bytes 835592 | tf_op jit(solution)/shard_map/ppermute | solution.py:261
  64.6 11.7 %collective-permute-start.18 = (f32[512,256]{1,0:T(8,128)S(1)}, f32[512,256]{1,0:T(8,128)S(1)}, u32[]{:S(2)}, u32[]{:S(2)}) collective-permute-start(f32[512,256]{1,0:T(8,128)S(1)} %get-tuple-element.29), channel_id=1, source_target_pairs={{0,1},{1,0},{2,3},{3,2},{4,5},{5,4},{6,7},{7,6},{8,9},{9,8},{10,11... | collective-permute-start | bytes 1572872 | tf_op jit(solution)/shard_map/ppermute | solution.py:261
  74.7 6.1 %collective-permute-start.4 = (f32[272,256]{1,0:T(8,128)S(1)}, f32[272,256]{1,0:T(8,128)S(1)}, u32[]{:S(2)}, u32[]{:S(2)}) collective-permute-start(f32[272,256]{1,0:T(8,128)S(1)} %pad_maximum_fusion.2.refs_12_.refs_3_), channel_id=1, source_target_pairs={{0,1},{1,0},{2,3},{3,2},{4,5},{5,4},{6,7},{7,6},{8,9},{9,8},{10,11... | collective-permute-start | bytes 835592 | tf_op jit(solution)/shard_map/ppermute | solution.py:261
  74.8 6.0 %collective-permute-start.5 = (f32[272,256]{1,0:T(8,128)S(1)}, f32[272,256]{1,0:T(8,128)S(1)}, u32[]{:S(2)}, u32[]{:S(2)}) collective-permute-start(f32[272,256]{1,0:T(8,128)S(1)} %collective-permute-done.3.refs_12_.refs_4_), channel_id=1, source_target_pairs={{0,1},{1,0},{2,3},{3,2},{4,5},{5,4},{6,7},{7,6},{8,9},{9,8},{10,11... | collective-permute-start | bytes 835592 | tf_op jit(solution)/shard_map/ppermute | solution.py:261
  76.4 10.4 %collective-permute-start.19 = (f32[128,256]{1,0:T(8,128)S(1)}, f32[128,256]{1,0:T(8,128)S(1)}, u32[]{:S(2)}, u32[]{:S(2)}) collective-permute-start(f32[128,256]{1,0:T(8,128)S(1)} %get-tuple-element.44), channel_id=1, source_target_pairs={{0,2},{1,3},{2,0},{3,1},{4,6},{5,7},{6,4},{7,5},{8,10},{9,11},{10,... | collective-permute-start | bytes 393224 | tf_op jit(solution)/shard_map/ppermute | solution.py:261
  76.5 13.0 %collective-permute-start.20 = (f32[128,256]{1,0:T(8,128)S(1)}, f32[128,256]{1,0:T(8,128)S(1)}, u32[]{:S(2)}, u32[]{:S(2)}) collective-permute-start(f32[128,256]{1,0:T(8,128)S(1)} %get-tuple-element.46), channel_id=1, source_target_pairs={{0,4},{1,5},{2,6},{3,7},{4,0},{5,1},{6,2},{7,3},{8,12},{9,13},{10,... | collective-permute-start | bytes 393224 | tf_op jit(solution)/shard_map/ppermute | solution.py:261
  76.5 12.9 %collective-permute-start.21 = (f32[128,256]{1,0:T(8,128)S(1)}, f32[128,256]{1,0:T(8,128)S(1)}, u32[]{:S(2)}, u32[]{:S(2)}) collective-permute-start(f32[128,256]{1,0:T(8,128)S(1)} %get-tuple-element.45), channel_id=1, source_target_pairs={{0,6},{1,7},{2,4},{3,5},{4,2},{5,3},{6,0},{7,1},{8,14},{9,15},{10,... | collective-permute-start | bytes 393224 | tf_op jit(solution)/shard_map/ppermute | solution.py:261
  91.0 10.0 %collective-permute-start.22 = (f32[512,256]{1,0:T(8,128)S(1)}, f32[512,256]{1,0:T(8,128)S(1)}, u32[]{:S(2)}, u32[]{:S(2)}) collective-permute-start(f32[512,256]{1,0:T(8,128)S(1)} %get-tuple-element.36), channel_id=1, source_target_pairs={{0,1},{1,0},{2,3},{3,2},{4,5},{5,4},{6,7},{7,6},{8,9},{9,8},{10,11... | collective-permute-start | bytes 1572872 | tf_op jit(solution)/shard_map/ppermute | solution.py:261
  101.1 8.7 %collective-permute-start.27 = (f32[256,256]{1,0:T(8,128)S(1)}, f32[256,256]{1,0:T(8,128)S(1)}, u32[]{:S(2)}, u32[]{:S(2)}) collective-permute-start(f32[256,256]{1,0:T(8,128)S(1)} %slice.155), channel_id=1, source_target_pairs={{0,2},{1,3},{2,0},{3,1},{4,6},{5,7},{6,4},{7,5},{8,10},{9,11},{10,... | collective-permute-start | bytes 786440 | tf_op jit(solution)/shard_map/ppermute | solution.py:261
  101.3 20.5 %collective-permute-start.23 = (f32[520,256]{1,0:T(8,128)S(1)}, f32[520,256]{1,0:T(8,128)S(1)}, u32[]{:S(2)}, u32[]{:S(2)}) collective-permute-start(f32[520,256]{1,0:T(8,128)S(1)} %get-tuple-element.55), channel_id=1, source_target_pairs={{0,8},{8,0},{16,24},{24,16},{1,9},{9,1},{17,25},{25,17},{2,10},{10... | collective-permute-start | bytes 1597448 | tf_op jit(solution)/shard_map/ppermute | solution.py:261
  109.8 8.7 %collective-permute-start.28 = (f32[128,256]{1,0:T(8,128)S(1)}, f32[128,256]{1,0:T(8,128)S(1)}, u32[]{:S(2)}, u32[]{:S(2)}) collective-permute-start(f32[128,256]{1,0:T(8,128)S(1)} %slice.157), channel_id=1, source_target_pairs={{0,4},{1,5},{2,6},{3,7},{4,0},{5,1},{6,2},{7,3},{8,12},{9,13},{10,... | collective-permute-start | bytes 393224 | tf_op jit(solution)/shard_map/ppermute | solution.py:261
  109.9 13.6 %collective-permute-start.25 = (f32[520,256]{1,0:T(8,128)S(1)}, f32[520,256]{1,0:T(8,128)S(1)}, u32[]{:S(2)}, u32[]{:S(2)}) collective-permute-start(f32[520,256]{1,0:T(8,128)S(1)} %get-tuple-element.56), channel_id=1, source_target_pairs={{0,16},{8,24},{16,0},{24,8},{1,17},{9,25},{17,1},{25,9},{2,18},{10... | collective-permute-start | bytes 1597448 | tf_op jit(solution)/shard_map/ppermute | solution.py:261
  118.6 26.8 %collective-permute-start.29 = (f32[256,256]{1,0:T(8,128)S(1)}, f32[256,256]{1,0:T(8,128)S(1)}, u32[]{:S(2)}, u32[]{:S(2)}) collective-permute-start(f32[256,256]{1,0:T(8,128)S(1)} %pad_maximum_fusion.4), channel_id=1, source_target_pairs={{0,0},{2,8},{4,16},{6,24},{8,1},{10,9},{12,17},{14,25},{16,2},{18,... | collective-permute-start | bytes 786440 | tf_op jit(solution)/shard_map/ppermute | solution.py:258
  120.5 25.1 %collective-permute-start.30 = (f32[256,256]{1,0:T(8,128)S(1)}, f32[256,256]{1,0:T(8,128)S(1)}, u32[]{:S(2)}, u32[]{:S(2)}) collective-permute-start(f32[256,256]{1,0:T(8,128)S(1)} %pad_maximum_fusion.4), channel_id=1, source_target_pairs={{1,0},{3,8},{5,16},{7,24},{9,1},{11,9},{13,17},{15,25},{17,2},{19,... | collective-permute-start | bytes 786440 | tf_op jit(solution)/shard_map/ppermute | solution.py:258
  121.9 23.8 %collective-permute-start.24 = (f32[256,256]{1,0:T(8,128)S(1)}, f32[256,256]{1,0:T(8,128)S(1)}, u32[]{:S(2)}, u32[]{:S(2)}) collective-permute-start(f32[256,256]{1,0:T(8,128)S(1)} %slice_add_fusion.3), channel_id=1, source_target_pairs={{0,16},{8,24},{16,0},{24,8},{1,17},{9,25},{17,1},{25,9},{2,18},{10... | collective-permute-start | bytes 786440 | tf_op jit(solution)/shard_map/ppermute | solution.py:261
  123.6 22.2 %collective-permute-start.26 = (f32[256,256]{1,0:T(8,128)S(1)}, f32[256,256]{1,0:T(8,128)S(1)}, u32[]{:S(2)}, u32[]{:S(2)}) collective-permute-start(f32[256,256]{1,0:T(8,128)S(1)} %slice_add_fusion.2), channel_id=1, source_target_pairs={{0,8},{8,0},{16,24},{24,16},{1,9},{9,1},{17,25},{25,17},{2,10},{10... | collective-permute-start | bytes 786440 | tf_op jit(solution)/shard_map/ppermute | solution.py:261
  (2 other events, 47.9 us)

commit v4 on v1

--- a/solution.py
+++ b/solution.py
@@ -320,12 +320,11 @@
     place = jnp.stack([g, chip, core]).astype(jnp.int32)
 
     def from_line(outs):
-        summed = total = outs[0] + across(outs[1])
-        step = 1
-        while step < groups:
-            kept = total.shape[0] // 2
-            total = total[:kept] + swapped(total[kept:], "col", 2 * step)
-            step *= 2
+        summed = outs[0] + across(outs[1])
+        parts = {d: summed[j * quarter : (j + 1) * quarter] for j, d in enumerate(order_of(groups))}
+        total = parts[0]
+        for d in range(1, groups):
+            total = total + swapped(parts[d], "col", 2 * d)
         return summed, total
 
     def to_home(total):
@@ -345,14 +344,12 @@
     outs = grads(1, tiles=tiles[:-1], vectors=vectors, held=[*columns, outs[2]], row_in=None, ready=[first_summed])
     outs = grads(1, tiles=tiles[-1:], vectors=vectors, held=[*columns, outs[1]], row_in=outs[0], ready=[first_total])
     second_summed, second_total = from_line(outs)
-    first_quarters = to_home(first_total)
-    quarters = first_quarters + to_home(second_total)
-
     halves = outs[2:]
     if groups == 4:
         spare = second_summed[:PAD]
         first_x = row_swapped(jnp.concatenate([halves[2], halves[6], spare], axis=0), 1)[: 2 * half]
         first_y = row_swapped(jnp.concatenate([halves[5], halves[7], spare], axis=0), 2)[: 2 * half]
+        waited = [first_x[:PAD], first_y[:PAD]]
         second_x = row_swapped(halves[3] + first_y[half:], 1)
         second_y = row_swapped(halves[4] + first_x[half:], 2)
         top = halves[0] + first_x[:half] + second_y
@@ -362,6 +359,9 @@
         for m in range(1, groups):
             top = top + row_swapped(halves[2 * m], m)
             bottom = bottom + row_swapped(halves[2 * m + 1], m)
+        waited = []
+    homes = to_home(jnp.concatenate([first_total, second_total, *waited], axis=0))
+    quarters = [home[at : at + quarter] for at in (0, quarter) for home in homes]
     gradients = (jnp.concatenate([top, bottom], axis=0) + jnp.concatenate(quarters, axis=0)) / BLOCK
     new_accum = accum + gradients * gradients
     new_embed = embed - LEARN_RATE * gradients / jnp.sqrt(new_accum)

time: 144 us -> 153 us (1.062)
  starting transfers between devices: 37 us -> 66 us
  Pallas kernels: 38.5 us -> 14.2 us
  waiting for transfers between devices: 56.3 us -> 62 us
    ppermute x24 -> x26, starting transfers between devices: 15.1 us -> 50.5 us  [swapped(): lax.ppermute(value, axis, [(r, r ^ m) for r in range(lax.axis_size(axis))])]
    pallas_call x4, Pallas kernels: 38.5 us -> 14.2 us  [half_grads(): pl.pallas_call(functools.partial(half_kernel, k, groups, share, layout, t...]
    ppermute x8 -> x6, waiting for transfers between devices: 11.9 us -> 21.6 us  [permute(): return lax.ppermute(value, both, pairs)]
    ppermute x8 -> x6, starting transfers between devices: 22 us -> 15.6 us  [permute(): return lax.ppermute(value, both, pairs)]
    ppermute x24 -> x26, waiting for transfers between devices: 44.5 us -> 40.4 us  [swapped(): lax.ppermute(value, axis, [(r, r ^ m) for r in range(lax.axis_size(axis))])]
  transfers between devices with their start and end apart: 32 -> 32, of which waited for: 15 -> 15; matrix products, arithmetic and copies ran while one was open for 4% -> 3% of each run, Pallas kernels for 18% -> 8%
where the time goes in v4:
time: 153 us; the launch traced here: 152 us
  starting transfers between devices  66 us (43%)
  waiting for transfers between devices  62 us (41%)
  Pallas kernels  14.2 us (9%)
  other arithmetic  6.34 us (4%)
  local copies, waits for them, and re-layouts  2.46 us (2%)
    ppermute x26, starting transfers between devices, swapped(): lax.ppermute(value, axis, [(r, r ^ m) for r in range(lax.axis_size(axis))])  50.5 us
    ppermute x26, waiting for transfers between devices, swapped(): lax.ppermute(value, axis, [(r, r ^ m) for r in range(lax.axis_size(axis))])  40.4 us
    ppermute x6, waiting for transfers between devices, permute(): return lax.ppermute(value, both, pairs)  21.6 us
    ppermute x6, starting transfers between devices, permute(): return lax.ppermute(value, both, pairs)  15.6 us
    pallas_call x4, Pallas kernels, half_grads(): pl.pallas_call(functools.partial(half_kernel, k, groups, share, layout, t...  14.2 us
  transfers between devices with their start and end apart: 32, of which 15 were waited for; matrix products, arithmetic and copies ran while one was open for 3% of the time, Pallas kernels for 8%

profile of v4, /device:TPU:2, one launch (start us, length us, event | category | flops | bytes accessed | tf_op | source)
XLA Modules:
  0.0 152.1 jit_solution(17991708403098098402)
XLA Ops:
  3.0 1.6 %collective-permute-start.6 = (f32[520,256]{1,0:T(8,128)S(1)}, f32[520,256]{1,0:T(8,128)S(1)}, u32[]{:S(2)}, u32[]{:S(2)}) collective-permute-start(f32[520,256]{1,0:T(8,128)S(1)} %select_maximum_fusion.refs_7_), channel_id=1, source_target_pairs={{0,16},{8,24},{16,0},{24,8},{1,17},{9,25},{17,1},{25,9},{2,18},{10... | collective-permute-start | bytes 1597448 | tf_op jit(solution)/shard_map/ppermute | solution.py:261
  5.8 1.6 %collective-permute-start.8 = (f32[8,128]{1,0:T(8,128)S(1)}, f32[8,128]{1,0:T(8,128)S(1)}, u32[]{:S(2)}, u32[]{:S(2)}) collective-permute-start(f32[8,128]{1,0:T(8,128)S(1)} %broadcast_in_dim.8), channel_id=1, source_target_pairs={{0,8},{8,0},{16,24},{24,16},{1,9},{9,1},{17,25},{25,17},{2,10},{10... | collective-permute-start | bytes 12296 | tf_op jit(solution)/shard_map/ppermute | solution.py:261
  8.5 3.5 %collective-permute-start.10 = (f32[136,256]{1,0:T(8,128)S(1)}, f32[136,256]{1,0:T(8,128)S(1)}, u32[]{:S(2)}, u32[]{:S(2)}) collective-permute-start(f32[136,256]{1,0:T(8,128)S(1)} %select_maximum_fusion.2), channel_id=1, source_target_pairs={{0,0},{8,2},{16,4},{24,6},{1,8},{9,10},{17,12},{25,14},{2,16},{10,... | collective-permute-start | bytes 417800 | tf_op jit(solution)/shard_map/ppermute | solution.py:258
  12.0 3.0 %collective-permute-start.11 = (f32[136,256]{1,0:T(8,128)S(1)}, f32[136,256]{1,0:T(8,128)S(1)}, u32[]{:S(2)}, u32[]{:S(2)}) collective-permute-start(f32[136,256]{1,0:T(8,128)S(1)} %select_maximum_fusion.1), channel_id=1, source_target_pairs={{0,1},{8,3},{16,5},{24,7},{1,9},{9,11},{17,13},{25,15},{2,17},{10,... | collective-permute-start | bytes 417800 | tf_op jit(solution)/shard_map/ppermute | solution.py:258
  15.0 7.0 %collective-permute-done.8 = f32[8,128]{1,0:T(8,128)S(1)} collective-permute-done((f32[8,128]{1,0:T(8,128)S(1)}, f32[8,128]{1,0:T(8,128)S(1)}, u32[]{:S(2)}, u32[]{:S(2)}) %collective-permute-start.8) | collective-permute-done | bytes 4128 | tf_op jit(solution)/shard_map/ppermute | solution.py:261
  22.8 3.6 %collective-permute-done.9 = f32[8,128]{1,0:T(8,128)S(1)} collective-permute-done((f32[8,128]{1,0:T(8,128)S(1)}, f32[8,128]{1,0:T(8,128)S(1)}, u32[]{:S(2)}, u32[]{:S(2)}) %collective-permute-start.9) | collective-permute-done | bytes 4128 | tf_op jit(solution)/shard_map/ppermute | solution.py:261
  28.6 3.4 %collective-permute-start.14 = (f32[136,256]{1,0:T(8,128)S(1)}, f32[136,256]{1,0:T(8,128)S(1)}, u32[]{:S(2)}, u32[]{:S(2)}) collective-permute-start(f32[136,256]{1,0:T(8,128)S(1)} %fusion.1), channel_id=1, source_target_pairs={{0,4},{1,5},{2,6},{3,7},{4,0},{5,1},{6,2},{7,3},{8,12},{9,13},{10,... | collective-permute-start | bytes 417800 | tf_op jit(solution)/shard_map/ppermute | solution.py:261
  32.0 1.9 %collective-permute-start = (f32[136,256]{1,0:T(8,128)S(1)}, f32[136,256]{1,0:T(8,128)S(1)}, u32[]{:S(2)}, u32[]{:S(2)}) collective-permute-start(f32[136,256]{1,0:T(8,128)S(1)} %select_maximum_fusion.4), channel_id=1, source_target_pairs={{0,0},{8,2},{16,4},{24,6},{1,8},{9,10},{17,12},{25,14},{2,16},{10,... | collective-permute-start | bytes 417800 | tf_op jit(solution)/shard_map/ppermute | solution.py:258
  33.9 4.0 %collective-permute-start.1 = (f32[136,256]{1,0:T(8,128)S(1)}, f32[136,256]{1,0:T(8,128)S(1)}, u32[]{:S(2)}, u32[]{:S(2)}) collective-permute-start(f32[136,256]{1,0:T(8,128)S(1)} %select_maximum_fusion.3), channel_id=1, source_target_pairs={{0,1},{8,3},{16,5},{24,7},{1,9},{9,11},{17,13},{25,15},{2,17},{10,... | collective-permute-start | bytes 417800 | tf_op jit(solution)/shard_map/ppermute | solution.py:258
  39.9 2.2 %collective-permute-done.1 = f32[136,256]{1,0:T(8,128)S(1)} collective-permute-done((f32[136,256]{1,0:T(8,128)S(1)}, f32[136,256]{1,0:T(8,128)S(1)}, u32[]{:S(2)}, u32[]{:S(2)}) %collective-permute-start.1) | collective-permute-done | bytes 139296 | tf_op jit(solution)/shard_map/ppermute | solution.py:258
  42.2 2.0 %collective-permute-start.16 = (f32[272,256]{1,0:T(8,128)S(1)}, f32[272,256]{1,0:T(8,128)S(1)}, u32[]{:S(2)}, u32[]{:S(2)}) collective-permute-start(f32[272,256]{1,0:T(8,128)S(1)} %pad_maximum_fusion.3.refs_3_), channel_id=1, source_target_pairs={{0,1},{1,0},{2,3},{3,2},{4,5},{5,4},{6,7},{7,6},{8,9},{9,8},{10,11... | collective-permute-start | bytes 835592 | tf_op jit(solution)/shard_map/ppermute | solution.py:261
  44.2 3.8 %collective-permute-done.15.refs_4_ = f32[272,256]{1,0:T(8,128)S(1)} collective-permute-done((f32[272,256]{1,0:T(8,128)S(1)}, f32[272,256]{1,0:T(8,128)S(1)}, u32[]{:S(2)}, u32[]{:S(2)}) %collective-permute-start.15) | collective-permute-done | bytes 278560 | tf_op jit(solution)/shard_map/ppermute | solution.py:261
  48.2 3.3 %collective-permute-done.2 = f32[136,256]{1,0:T(8,128)S(1)} collective-permute-done((f32[136,256]{1,0:T(8,128)S(1)}, f32[136,256]{1,0:T(8,128)S(1)}, u32[]{:S(2)}, u32[]{:S(2)}) %collective-permute-start.2) | collective-permute-done | bytes 139296 | tf_op jit(solution)/shard_map/ppermute | solution.py:261
  51.7 5.8 %half_grads.4 = (f32[1024,256]{1,0:T(8,128)S(1)}, bf16[2048,256]{1,0:T(8,128)(2,1)S(1)}, bf16[2048,256]{1,0:T(8,128)(2,1)S(1)}, f32[32,256]{1,0:T(8,128)S(1)}, f32[256,2048]{1,0:T(8,128)S(1)}) custom-call(s32[3]{0:T(128)S(1)} %pad_add_fusion.refs_0_, s32[4]{0:T(128)S(1)} %convert_reduce_fusion.1.refs_1_, s32[2048,2048]{1,0:T(8,128)} %refs_2_.7, ...), custom_call_target="tpu_custom_call" | custom-call | flops 7247757312 | bytes 10485760 | tf_op jit(solution)/shard_map/half_grads/pallas_call | solution.py:228
  57.5 2.7 %collective-permute-done.3.refs_12_.refs_4_ = f32[272,256]{1,0:T(8,128)S(1)} collective-permute-done((f32[272,256]{1,0:T(8,128)S(1)}, f32[272,256]{1,0:T(8,128)S(1)}, u32[]{:S(2)}, u32[]{:S(2)}) %collective-permute-start.3) | collective-permute-done | bytes 278560 | tf_op jit(solution)/shard_map/ppermute | solution.py:261
  64.0 4.6 %collective-permute-start.19 = (f32[128,256]{1,0:T(8,128)S(1)}, f32[128,256]{1,0:T(8,128)S(1)}, u32[]{:S(2)}, u32[]{:S(2)}) collective-permute-start(f32[128,256]{1,0:T(8,128)S(1)} %get-tuple-element.47), channel_id=1, source_target_pairs={{0,2},{1,3},{2,0},{3,1},{4,6},{5,7},{6,4},{7,5},{8,10},{9,11},{10,... | collective-permute-start | bytes 393224 | tf_op jit(solution)/shard_map/ppermute | solution.py:261
  68.6 1.7 %collective-permute-start.20 = (f32[128,256]{1,0:T(8,128)S(1)}, f32[128,256]{1,0:T(8,128)S(1)}, u32[]{:S(2)}, u32[]{:S(2)}) collective-permute-start(f32[128,256]{1,0:T(8,128)S(1)} %get-tuple-element.49), channel_id=1, source_target_pairs={{0,4},{1,5},{2,6},{3,7},{4,0},{5,1},{6,2},{7,3},{8,12},{9,13},{10,... | collective-permute-start | bytes 393224 | tf_op jit(solution)/shard_map/ppermute | solution.py:261
  71.0 5.8 %half_grads.6 = (f32[1024,256]{1,0:T(8,128)S(1)}, f32[256,2048]{1,0:T(8,128)S(1)}) custom-call(s32[3]{0:T(128)S(1)} %pad_add_fusion.refs_0_, s32[4]{0:T(128)S(1)} %convert_reduce_fusion.1.refs_1_, s32[2048,2048]{1,0:T(8,128)} %refs_2_.7, f32[272,256]{1,0:T(8,128)S(1)} %pad_maximum_fusion.2.refs_12_.refs_3_, ...), custom_call_target="tpu_custom_call" | custom-call | flops 7247757312 | bytes 10485760 | tf_op jit(solution)/shard_map/half_grads/pallas_call | solution.py:228
  76.9 4.6 %collective-permute-done.20 = f32[128,256]{1,0:T(8,128)S(1)} collective-permute-done((f32[128,256]{1,0:T(8,128)S(1)}, f32[128,256]{1,0:T(8,128)S(1)}, u32[]{:S(2)}, u32[]{:S(2)}) %collective-permute-start.20) | collective-permute-done | bytes 131104 | tf_op jit(solution)/shard_map/ppermute | solution.py:261
  81.5 1.5 %half_grads.7 = (f32[512,256]{1,0:T(8,128)S(1)}, f32[512,256]{1,0:T(8,128)S(1)}, f32[256,256]{1,0:T(8,128)S(1)}, f32[256,256]{1,0:T(8,128)S(1)}, f32[256,256]{1,...) custom-call(s32[3]{0:T(128)S(1)} %pad_add_fusion.refs_0_, ...), custom_call_target="tpu_custom_call" | custom-call | flops 2415919104 | bytes 6291456 | tf_op jit(solution)/shard_map/half_grads/pallas_call | solution.py:228
  83.2 1.9 %collective-permute-done.22 = f32[512,256]{1,0:T(8,128)S(1)} collective-permute-done((f32[512,256]{1,0:T(8,128)S(1)}, f32[512,256]{1,0:T(8,128)S(1)}, u32[]{:S(2)}, u32[]{:S(2)}) %collective-permute-start.22) | collective-permute-done | bytes 524320 | tf_op jit(solution)/shard_map/ppermute | solution.py:261
  85.2 15.8 %collective-permute-start.23 = (f32[520,256]{1,0:T(8,128)S(1)}, f32[520,256]{1,0:T(8,128)S(1)}, u32[]{:S(2)}, u32[]{:S(2)}) collective-permute-start(f32[520,256]{1,0:T(8,128)S(1)} %get-tuple-element.58), channel_id=1, source_target_pairs={{0,8},{8,0},{16,24},{24,16},{1,9},{9,1},{17,25},{25,17},{2,10},{10... | collective-permute-start | bytes 1597448 | tf_op jit(solution)/shard_map/ppermute | solution.py:261
  102.2 3.3 %collective-permute-start.29 = (f32[128,256]{1,0:T(8,128)S(1)}, f32[128,256]{1,0:T(8,128)S(1)}, u32[]{:S(2)}, u32[]{:S(2)}) collective-permute-start(f32[128,256]{1,0:T(8,128)S(1)} %get-tuple-element.45), channel_id=1, source_target_pairs={{0,6},{1,7},{2,4},{3,5},{4,2},{5,3},{6,0},{7,1},{8,14},{9,15},{10,... | collective-permute-start | bytes 393224 | tf_op jit(solution)/shard_map/ppermute | solution.py:261
  105.5 3.9 %collective-permute-start.25 = (f32[520,256]{1,0:T(8,128)S(1)}, f32[520,256]{1,0:T(8,128)S(1)}, u32[]{:S(2)}, u32[]{:S(2)}) collective-permute-start(f32[520,256]{1,0:T(8,128)S(1)} %get-tuple-element.59), channel_id=1, source_target_pairs={{0,16},{8,24},{16,0},{24,8},{1,17},{9,25},{17,1},{25,9},{2,18},{10... | collective-permute-start | bytes 1597448 | tf_op jit(solution)/shard_map/ppermute | solution.py:261
  109.4 4.7 %collective-permute-done.28 = f32[128,256]{1,0:T(8,128)S(1)} collective-permute-done((f32[128,256]{1,0:T(8,128)S(1)}, f32[128,256]{1,0:T(8,128)S(1)}, u32[]{:S(2)}, u32[]{:S(2)}) %collective-permute-start.28) | collective-permute-done | bytes 131104 | tf_op jit(solution)/shard_map/ppermute | solution.py:261
  114.2 5.3 %collective-permute-start.24 = (f32[256,256]{1,0:T(8,128)S(1)}, f32[256,256]{1,0:T(8,128)S(1)}, u32[]{:S(2)}, u32[]{:S(2)}) collective-permute-start(f32[256,256]{1,0:T(8,128)S(1)} %slice_add_fusion.2), channel_id=1, source_target_pairs={{0,16},{8,24},{16,0},{24,8},{1,17},{9,25},{17,1},{25,9},{2,18},{10... | collective-permute-start | bytes 786440 | tf_op jit(solution)/shard_map/ppermute | solution.py:261
  119.5 2.9 %collective-permute-done.25 = f32[520,256]{1,0:T(8,128)S(1)} collective-permute-done((f32[520,256]{1,0:T(8,128)S(1)}, f32[520,256]{1,0:T(8,128)S(1)}, u32[]{:S(2)}, u32[]{:S(2)}) %collective-permute-start.25) | collective-permute-done | bytes 532512 | tf_op jit(solution)/shard_map/ppermute | solution.py:261
  122.4 2.1 %collective-permute-start.26 = (f32[256,256]{1,0:T(8,128)S(1)}, f32[256,256]{1,0:T(8,128)S(1)}, u32[]{:S(2)}, u32[]{:S(2)}) collective-permute-start(f32[256,256]{1,0:T(8,128)S(1)} %slice_add_fusion.1), channel_id=1, source_target_pairs={{0,8},{8,0},{16,24},{24,16},{1,9},{9,1},{17,25},{25,17},{2,10},{10... | collective-permute-start | bytes 786440 | tf_op jit(solution)/shard_map/ppermute | solution.py:261
  124.5 1.9 %collective-permute-start.30 = (f32[272,256]{1,0:T(8,128)S(1)}, f32[272,256]{1,0:T(8,128)S(1)}, u32[]{:S(2)}, u32[]{:S(2)}) collective-permute-start(f32[272,256]{1,0:T(8,128)S(1)} %pad_maximum_fusion.4), channel_id=1, source_target_pairs={{0,0},{2,8},{4,16},{6,24},{8,1},{10,9},{12,17},{14,25},{16,2},{18,... | collective-permute-start | bytes 835592 | tf_op jit(solution)/shard_map/ppermute | solution.py:258
  126.5 1.3 collective-permute-start.31
  127.8 4.7 %collective-permute-done.26 = f32[256,256]{1,0:T(8,128)S(1)} collective-permute-done((f32[256,256]{1,0:T(8,128)S(1)}, f32[256,256]{1,0:T(8,128)S(1)}, u32[]{:S(2)}, u32[]{:S(2)}) %collective-permute-start.26) | collective-permute-done | bytes 262176 | tf_op jit(solution)/shard_map/ppermute | solution.py:261
  132.6 17.1 %collective-permute-done.30 = f32[272,256]{1,0:T(8,128)S(1)} collective-permute-done((f32[272,256]{1,0:T(8,128)S(1)}, f32[272,256]{1,0:T(8,128)S(1)}, u32[]{:S(2)}, u32[]{:S(2)}) %collective-permute-start.30) | collective-permute-done | bytes 278560 | tf_op jit(solution)/shard_map/ppermute | solution.py:258
  (85 shorter events, 18.4 us)
Async XLA Ops:
  3.0 24.6 %collective-permute-start.6 = (f32[520,256]{1,0:T(8,128)S(1)}, f32[520,256]{1,0:T(8,128)S(1)}, u32[]{:S(2)}, u32[]{:S(2)}) collective-permute-start(f32[520,256]{1,0:T(8,128)S(1)} %select_maximum_fusion.refs_7_), channel_id=1, source_target_pairs={{0,16},{8,24},{16,0},{24,8},{1,17},{9,25},{17,1},{25,9},{2,18},{10... | collective-permute-start | bytes 1597448 | tf_op jit(solution)/shard_map/ppermute | solution.py:261
  4.6 22.9 %collective-permute-start.7 = (f32[520,256]{1,0:T(8,128)S(1)}, f32[520,256]{1,0:T(8,128)S(1)}, u32[]{:S(2)}, u32[]{:S(2)}) collective-permute-start(f32[520,256]{1,0:T(8,128)S(1)} %select_maximum_fusion.refs_7_), channel_id=1, source_target_pairs={{0,8},{8,0},{16,24},{24,16},{1,9},{9,1},{17,25},{25,17},{2,10},{10... | collective-permute-start | bytes 1597448 | tf_op jit(solution)/shard_map/ppermute | solution.py:261
  5.8 16.2 %collective-permute-start.8 = (f32[8,128]{1,0:T(8,128)S(1)}, f32[8,128]{1,0:T(8,128)S(1)}, u32[]{:S(2)}, u32[]{:S(2)}) collective-permute-start(f32[8,128]{1,0:T(8,128)S(1)} %broadcast_in_dim.8), channel_id=1, source_target_pairs={{0,8},{8,0},{16,24},{24,16},{1,9},{9,1},{17,25},{25,17},{2,10},{10... | collective-permute-start | bytes 12296 | tf_op jit(solution)/shard_map/ppermute | solution.py:261
  8.5 19.2 %collective-permute-start.10 = (f32[136,256]{1,0:T(8,128)S(1)}, f32[136,256]{1,0:T(8,128)S(1)}, u32[]{:S(2)}, u32[]{:S(2)}) collective-permute-start(f32[136,256]{1,0:T(8,128)S(1)} %select_maximum_fusion.2), channel_id=1, source_target_pairs={{0,0},{8,2},{16,4},{24,6},{1,8},{9,10},{17,12},{25,14},{2,16},{10,... | collective-permute-start | bytes 417800 | tf_op jit(solution)/shard_map/ppermute | solution.py:258
  12.0 15.8 %collective-permute-start.11 = (f32[136,256]{1,0:T(8,128)S(1)}, f32[136,256]{1,0:T(8,128)S(1)}, u32[]{:S(2)}, u32[]{:S(2)}) collective-permute-start(f32[136,256]{1,0:T(8,128)S(1)} %select_maximum_fusion.1), channel_id=1, source_target_pairs={{0,1},{8,3},{16,5},{24,7},{1,9},{9,11},{17,13},{25,15},{2,17},{10,... | collective-permute-start | bytes 417800 | tf_op jit(solution)/shard_map/ppermute | solution.py:258
  22.7 3.7 %collective-permute-start.9 = (f32[8,128]{1,0:T(8,128)S(1)}, f32[8,128]{1,0:T(8,128)S(1)}, u32[]{:S(2)}, u32[]{:S(2)}) collective-permute-start(f32[8,128]{1,0:T(8,128)S(1)} %broadcast_add_fusion), channel_id=1, source_target_pairs={{0,16},{8,24},{16,0},{24,8},{1,17},{9,25},{17,1},{25,9},{2,18},{10... | collective-permute-start | bytes 12296 | tf_op jit(solution)/shard_map/ppermute | solution.py:261
  27.6 10.4 %collective-permute-start.13 = (f32[264,256]{1,0:T(8,128)S(1)}, f32[264,256]{1,0:T(8,128)S(1)}, u32[]{:S(2)}, u32[]{:S(2)}) collective-permute-start(f32[264,256]{1,0:T(8,128)S(1)} %slice.153), channel_id=1, source_target_pairs={{0,16},{8,24},{16,0},{24,8},{1,17},{9,25},{17,1},{25,9},{2,18},{10... | collective-permute-start | bytes 811016 | tf_op jit(solution)/shard_map/ppermute | solution.py:261
  27.7 10.3 %collective-permute-start.12 = (f32[256,256]{1,0:T(8,128)S(1)}, f32[256,256]{1,0:T(8,128)S(1)}, u32[]{:S(2)}, u32[]{:S(2)}) collective-permute-start(f32[256,256]{1,0:T(8,128)S(1)} %slice.151), channel_id=1, source_target_pairs={{0,8},{8,0},{16,24},{24,16},{1,9},{9,1},{17,25},{25,17},{2,10},{10... | collective-permute-start | bytes 786440 | tf_op jit(solution)/shard_map/ppermute | solution.py:261
  28.6 9.4 %collective-permute-start.14 = (f32[136,256]{1,0:T(8,128)S(1)}, f32[136,256]{1,0:T(8,128)S(1)}, u32[]{:S(2)}, u32[]{:S(2)}) collective-permute-start(f32[136,256]{1,0:T(8,128)S(1)} %fusion.1), channel_id=1, source_target_pairs={{0,4},{1,5},{2,6},{3,7},{4,0},{5,1},{6,2},{7,3},{8,12},{9,13},{10,... | collective-permute-start | bytes 417800 | tf_op jit(solution)/shard_map/ppermute | solution.py:261
  32.0 7.9 %collective-permute-start = (f32[136,256]{1,0:T(8,128)S(1)}, f32[136,256]{1,0:T(8,128)S(1)}, u32[]{:S(2)}, u32[]{:S(2)}) collective-permute-start(f32[136,256]{1,0:T(8,128)S(1)} %select_maximum_fusion.4), channel_id=1, source_target_pairs={{0,0},{8,2},{16,4},{24,6},{1,8},{9,10},{17,12},{25,14},{2,16},{10,... | collective-permute-start | bytes 417800 | tf_op jit(solution)/shard_map/ppermute | solution.py:258
  33.9 8.1 %collective-permute-start.1 = (f32[136,256]{1,0:T(8,128)S(1)}, f32[136,256]{1,0:T(8,128)S(1)}, u32[]{:S(2)}, u32[]{:S(2)}) collective-permute-start(f32[136,256]{1,0:T(8,128)S(1)} %select_maximum_fusion.3), channel_id=1, source_target_pairs={{0,1},{8,3},{16,5},{24,7},{1,9},{9,11},{17,13},{25,15},{2,17},{10,... | collective-permute-start | bytes 417800 | tf_op jit(solution)/shard_map/ppermute | solution.py:258
  38.0 10.0 %collective-permute-start.15 = (f32[272,256]{1,0:T(8,128)S(1)}, f32[272,256]{1,0:T(8,128)S(1)}, u32[]{:S(2)}, u32[]{:S(2)}) collective-permute-start(f32[272,256]{1,0:T(8,128)S(1)} %pad_maximum_fusion.3.refs_3_), channel_id=1, source_target_pairs={{0,2},{1,3},{2,0},{3,1},{4,6},{5,7},{6,4},{7,5},{8,10},{9,11},{10,... | collective-permute-start | bytes 835592 | tf_op jit(solution)/shard_map/ppermute | solution.py:261
  42.1 9.5 %collective-permute-start.2 = (f32[136,256]{1,0:T(8,128)S(1)}, f32[136,256]{1,0:T(8,128)S(1)}, u32[]{:S(2)}, u32[]{:S(2)}) collective-permute-start(f32[136,256]{1,0:T(8,128)S(1)} %broadcast_select_fusion), channel_id=1, source_target_pairs={{0,4},{1,5},{2,6},{3,7},{4,0},{5,1},{6,2},{7,3},{8,12},{9,13},{10,... | collective-permute-start | bytes 417800 | tf_op jit(solution)/shard_map/ppermute | solution.py:261
  42.2 9.5 %collective-permute-start.16 = (f32[272,256]{1,0:T(8,128)S(1)}, f32[272,256]{1,0:T(8,128)S(1)}, u32[]{:S(2)}, u32[]{:S(2)}) collective-permute-start(f32[272,256]{1,0:T(8,128)S(1)} %pad_maximum_fusion.3.refs_3_), channel_id=1, source_target_pairs={{0,1},{1,0},{2,3},{3,2},{4,5},{5,4},{6,7},{7,6},{8,9},{9,8},{10,11... | collective-permute-start | bytes 835592 | tf_op jit(solution)/shard_map/ppermute | solution.py:261
  48.0 3.7 %collective-permute-start.17 = (f32[272,256]{1,0:T(8,128)S(1)}, f32[272,256]{1,0:T(8,128)S(1)}, u32[]{:S(2)}, u32[]{:S(2)}) collective-permute-start(f32[272,256]{1,0:T(8,128)S(1)} %collective-permute-done.15.refs_4_), channel_id=1, source_target_pairs={{0,1},{1,0},{2,3},{3,2},{4,5},{5,4},{6,7},{7,6},{8,9},{9,8},{10,11... | collective-permute-start | bytes 835592 | tf_op jit(solution)/shard_map/ppermute | solution.py:261
  51.6 8.7 %collective-permute-start.3 = (f32[272,256]{1,0:T(8,128)S(1)}, f32[272,256]{1,0:T(8,128)S(1)}, u32[]{:S(2)}, u32[]{:S(2)}) collective-permute-start(f32[272,256]{1,0:T(8,128)S(1)} %pad_maximum_fusion.2.refs_12_.refs_3_), channel_id=1, source_target_pairs={{0,2},{1,3},{2,0},{3,1},{4,6},{5,7},{6,4},{7,5},{8,10},{9,11},{10,... | collective-permute-start | bytes 835592 | tf_op jit(solution)/shard_map/ppermute | solution.py:261
  61.2 2.6 %collective-permute-start.18 = (f32[512,256]{1,0:T(8,128)S(1)}, f32[512,256]{1,0:T(8,128)S(1)}, u32[]{:S(2)}, u32[]{:S(2)}) collective-permute-start(f32[512,256]{1,0:T(8,128)S(1)} %get-tuple-element.29), channel_id=1, source_target_pairs={{0,1},{1,0},{2,3},{3,2},{4,5},{5,4},{6,7},{7,6},{8,9},{9,8},{10,11... | collective-permute-start | bytes 1572872 | tf_op jit(solution)/shard_map/ppermute | solution.py:261
  62.4 8.7 %collective-permute-start.4 = (f32[272,256]{1,0:T(8,128)S(1)}, f32[272,256]{1,0:T(8,128)S(1)}, u32[]{:S(2)}, u32[]{:S(2)}) collective-permute-start(f32[272,256]{1,0:T(8,128)S(1)} %pad_maximum_fusion.2.refs_12_.refs_3_), channel_id=1, source_target_pairs={{0,1},{1,0},{2,3},{3,2},{4,5},{5,4},{6,7},{7,6},{8,9},{9,8},{10,11... | collective-permute-start | bytes 835592 | tf_op jit(solution)/shard_map/ppermute | solution.py:261
  62.4 8.6 %collective-permute-start.5 = (f32[272,256]{1,0:T(8,128)S(1)}, f32[272,256]{1,0:T(8,128)S(1)}, u32[]{:S(2)}, u32[]{:S(2)}) collective-permute-start(f32[272,256]{1,0:T(8,128)S(1)} %collective-permute-done.3.refs_12_.refs_4_), channel_id=1, source_target_pairs={{0,1},{1,0},{2,3},{3,2},{4,5},{5,4},{6,7},{7,6},{8,9},{9,8},{10,11... | collective-permute-start | bytes 835592 | tf_op jit(solution)/shard_map/ppermute | solution.py:261
  64.0 12.9 %collective-permute-start.19 = (f32[128,256]{1,0:T(8,128)S(1)}, f32[128,256]{1,0:T(8,128)S(1)}, u32[]{:S(2)}, u32[]{:S(2)}) collective-permute-start(f32[128,256]{1,0:T(8,128)S(1)} %get-tuple-element.47), channel_id=1, source_target_pairs={{0,2},{1,3},{2,0},{3,1},{4,6},{5,7},{6,4},{7,5},{8,10},{9,11},{10,... | collective-permute-start | bytes 393224 | tf_op jit(solution)/shard_map/ppermute | solution.py:261
  68.6 12.9 %collective-permute-start.20 = (f32[128,256]{1,0:T(8,128)S(1)}, f32[128,256]{1,0:T(8,128)S(1)}, u32[]{:S(2)}, u32[]{:S(2)}) collective-permute-start(f32[128,256]{1,0:T(8,128)S(1)} %get-tuple-element.49), channel_id=1, source_target_pairs={{0,4},{1,5},{2,6},{3,7},{4,0},{5,1},{6,2},{7,3},{8,12},{9,13},{10,... | collective-permute-start | bytes 393224 | tf_op jit(solution)/shard_map/ppermute | solution.py:261
  70.3 11.2 %collective-permute-start.21 = (f32[128,256]{1,0:T(8,128)S(1)}, f32[128,256]{1,0:T(8,128)S(1)}, u32[]{:S(2)}, u32[]{:S(2)}) collective-permute-start(f32[128,256]{1,0:T(8,128)S(1)} %get-tuple-element.48), channel_id=1, source_target_pairs={{0,6},{1,7},{2,4},{3,5},{4,2},{5,3},{6,0},{7,1},{8,14},{9,15},{10,... | collective-permute-start | bytes 393224 | tf_op jit(solution)/shard_map/ppermute | solution.py:261
  83.1 2.0 %collective-permute-start.22 = (f32[512,256]{1,0:T(8,128)S(1)}, f32[512,256]{1,0:T(8,128)S(1)}, u32[]{:S(2)}, u32[]{:S(2)}) collective-permute-start(f32[512,256]{1,0:T(8,128)S(1)} %get-tuple-element.36), channel_id=1, source_target_pairs={{0,1},{1,0},{2,3},{3,2},{4,5},{5,4},{6,7},{7,6},{8,9},{9,8},{10,11... | collective-permute-start | bytes 1572872 | tf_op jit(solution)/shard_map/ppermute | solution.py:261
  85.2 29.0 %collective-permute-start.23 = (f32[520,256]{1,0:T(8,128)S(1)}, f32[520,256]{1,0:T(8,128)S(1)}, u32[]{:S(2)}, u32[]{:S(2)}) collective-permute-start(f32[520,256]{1,0:T(8,128)S(1)} %get-tuple-element.58), channel_id=1, source_target_pairs={{0,8},{8,0},{16,24},{24,16},{1,9},{9,1},{17,25},{25,17},{2,10},{10... | collective-permute-start | bytes 1597448 | tf_op jit(solution)/shard_map/ppermute | solution.py:261
  101.1 8.3 %collective-permute-start.27 = (f32[128,256]{1,0:T(8,128)S(1)}, f32[128,256]{1,0:T(8,128)S(1)}, u32[]{:S(2)}, u32[]{:S(2)}) collective-permute-start(f32[128,256]{1,0:T(8,128)S(1)} %get-tuple-element.44), channel_id=1, source_target_pairs={{0,2},{1,3},{2,0},{3,1},{4,6},{5,7},{6,4},{7,5},{8,10},{9,11},{10,... | collective-permute-start | bytes 393224 | tf_op jit(solution)/shard_map/ppermute | solution.py:261
  101.2 13.0 %collective-permute-start.28 = (f32[128,256]{1,0:T(8,128)S(1)}, f32[128,256]{1,0:T(8,128)S(1)}, u32[]{:S(2)}, u32[]{:S(2)}) collective-permute-start(f32[128,256]{1,0:T(8,128)S(1)} %get-tuple-element.46), channel_id=1, source_target_pairs={{0,4},{1,5},{2,6},{3,7},{4,0},{5,1},{6,2},{7,3},{8,12},{9,13},{10,... | collective-permute-start | bytes 393224 | tf_op jit(solution)/shard_map/ppermute | solution.py:261
  102.2 12.0 %collective-permute-start.29 = (f32[128,256]{1,0:T(8,128)S(1)}, f32[128,256]{1,0:T(8,128)S(1)}, u32[]{:S(2)}, u32[]{:S(2)}) collective-permute-start(f32[128,256]{1,0:T(8,128)S(1)} %get-tuple-element.45), channel_id=1, source_target_pairs={{0,6},{1,7},{2,4},{3,5},{4,2},{5,3},{6,0},{7,1},{8,14},{9,15},{10,... | collective-permute-start | bytes 393224 | tf_op jit(solution)/shard_map/ppermute | solution.py:261
  105.5 16.8 %collective-permute-start.25 = (f32[520,256]{1,0:T(8,128)S(1)}, f32[520,256]{1,0:T(8,128)S(1)}, u32[]{:S(2)}, u32[]{:S(2)}) collective-permute-start(f32[520,256]{1,0:T(8,128)S(1)} %get-tuple-element.59), channel_id=1, source_target_pairs={{0,16},{8,24},{16,0},{24,8},{1,17},{9,25},{17,1},{25,9},{2,18},{10... | collective-permute-start | bytes 1597448 | tf_op jit(solution)/shard_map/ppermute | solution.py:261
  114.2 13.5 %collective-permute-start.24 = (f32[256,256]{1,0:T(8,128)S(1)}, f32[256,256]{1,0:T(8,128)S(1)}, u32[]{:S(2)}, u32[]{:S(2)}) collective-permute-start(f32[256,256]{1,0:T(8,128)S(1)} %slice_add_fusion.2), channel_id=1, source_target_pairs={{0,16},{8,24},{16,0},{24,8},{1,17},{9,25},{17,1},{25,9},{2,18},{10... | collective-permute-start | bytes 786440 | tf_op jit(solution)/shard_map/ppermute | solution.py:261
  122.4 10.1 %collective-permute-start.26 = (f32[256,256]{1,0:T(8,128)S(1)}, f32[256,256]{1,0:T(8,128)S(1)}, u32[]{:S(2)}, u32[]{:S(2)}) collective-permute-start(f32[256,256]{1,0:T(8,128)S(1)} %slice_add_fusion.1), channel_id=1, source_target_pairs={{0,8},{8,0},{16,24},{24,16},{1,9},{9,1},{17,25},{25,17},{2,10},{10... | collective-permute-start | bytes 786440 | tf_op jit(solution)/shard_map/ppermute | solution.py:261
  124.5 25.1 %collective-permute-start.30 = (f32[272,256]{1,0:T(8,128)S(1)}, f32[272,256]{1,0:T(8,128)S(1)}, u32[]{:S(2)}, u32[]{:S(2)}) collective-permute-start(f32[272,256]{1,0:T(8,128)S(1)} %pad_maximum_fusion.4), channel_id=1, source_target_pairs={{0,0},{2,8},{4,16},{6,24},{8,1},{10,9},{12,17},{14,25},{16,2},{18,... | collective-permute-start | bytes 835592 | tf_op jit(solution)/shard_map/ppermute | solution.py:258
  126.5 24.4 %collective-permute-start.31 = (f32[272,256]{1,0:T(8,128)S(1)}, f32[272,256]{1,0:T(8,128)S(1)}, u32[]{:S(2)}, u32[]{:S(2)}) collective-permute-start(f32[272,256]{1,0:T(8,128)S(1)} %pad_maximum_fusion.4), channel_id=1, source_target_pairs={{1,0},{3,8},{5,16},{7,24},{9,1},{11,9},{13,17},{15,25},{17,2},{19,... | collective-permute-start | bytes 835592 | tf_op jit(solution)/shard_map/ppermute | solution.py:258
  (3 other events, 96.8 us)

commit v5 on v3

--- a/solution.py
+++ b/solution.py
@@ -353,12 +353,12 @@
     outs = grads(1, tiles=tiles[:-1], vectors=vectors, held=[*columns, outs[2]], row_in=None, ready=[first_summed])
     outs = grads(1, tiles=tiles[-1:], vectors=vectors, held=[*columns, outs[1]], row_in=outs[0], ready=[first_total])
     second_summed, second_total = from_line(outs)
-    homes = to_home(jnp.concatenate([first_total, second_total], axis=0))
-    quarters = [home[at : at + quarter] for at in (0, quarter) for home in homes]
+    first_quarters = to_home(first_total)
+    quarters = first_quarters + to_home(second_total)
 
     halves = outs[2:]
     if groups == 4:
-        spare = second_summed[:PAD]
+        spare = second_summed[:PAD] + first_quarters[0][:PAD] + first_quarters[1][:PAD]
         first_x = row_swapped(jnp.concatenate([halves[2], halves[6], spare], axis=0), 1)[: 2 * half]
         first_y = row_swapped(jnp.concatenate([halves[5], halves[7], spare], axis=0), 2)[: 2 * half]
         second_x = row_swapped(halves[3] + first_y[half:], 1)

time: 145 us -> 149 us (1.028)
  the two profiles are of different devices: /device:TPU:4 before, /device:TPU:2 now
where the time goes in v5:
time: 149 us
  starting transfers between devices  76.8 us (52%)
  waiting for transfers between devices  47.9 us (32%)
  Pallas kernels  14.3 us (10%)
  other arithmetic  6.33 us (4%)
  local copies, waits for them, and re-layouts  2.43 us (2%)
    ppermute x25, starting transfers between devices, swapped(): lax.ppermute(value, axis, [(r, r ^ m) for r in range(lax.axis_size(axis))])  53.9 us
    ppermute x25, waiting for transfers between devices, swapped(): lax.ppermute(value, axis, [(r, r ^ m) for r in range(lax.axis_size(axis))])  29.9 us
    ppermute x8, starting transfers between devices, permute(): return lax.ppermute(value, both, pairs)  22.9 us
    ppermute x8, waiting for transfers between devices, permute(): return lax.ppermute(value, both, pairs)  18 us
    pallas_call x4, Pallas kernels, half_grads(): pl.pallas_call(functools.partial(half_kernel, k, groups, share, layout, t...  14.3 us
  transfers between devices with their start and end apart: 33, of which 16 were waited for; matrix products, arithmetic and copies ran while one was open for 3% of the time, Pallas kernels for 8%

profile of v5, /device:TPU:2, one launch (start us, length us, event | category | flops | bytes accessed | tf_op | source)
XLA Modules:
  0.0 148.9 jit_solution(16793691120792890954)
XLA Ops:
  3.0 1.6 %collective-permute-start.6 = (f32[520,256]{1,0:T(8,128)S(1)}, f32[520,256]{1,0:T(8,128)S(1)}, u32[]{:S(2)}, u32[]{:S(2)}) collective-permute-start(f32[520,256]{1,0:T(8,128)S(1)} %select_maximum_fusion.refs_7_), channel_id=1, source_target_pairs={{0,16},{8,24},{16,0},{24,8},{1,17},{9,25},{17,1},{25,9},{2,18},{10... | collective-permute-start | bytes 1597448 | tf_op jit(solution)/shard_map/ppermute | solution.py:261
  5.8 1.6 %collective-permute-start.8 = (f32[8,128]{1,0:T(8,128)S(1)}, f32[8,128]{1,0:T(8,128)S(1)}, u32[]{:S(2)}, u32[]{:S(2)}) collective-permute-start(f32[8,128]{1,0:T(8,128)S(1)} %broadcast_in_dim.8), channel_id=1, source_target_pairs={{0,8},{8,0},{16,24},{24,16},{1,9},{9,1},{17,25},{25,17},{2,10},{10... | collective-permute-start | bytes 12296 | tf_op jit(solution)/shard_map/ppermute | solution.py:261
  8.5 3.5 %collective-permute-start.10 = (f32[136,256]{1,0:T(8,128)S(1)}, f32[136,256]{1,0:T(8,128)S(1)}, u32[]{:S(2)}, u32[]{:S(2)}) collective-permute-start(f32[136,256]{1,0:T(8,128)S(1)} %select_maximum_fusion.2), channel_id=1, source_target_pairs={{0,0},{8,2},{16,4},{24,6},{1,8},{9,10},{17,12},{25,14},{2,16},{10,... | collective-permute-start | bytes 417800 | tf_op jit(solution)/shard_map/ppermute | solution.py:258
  12.0 3.0 %collective-permute-start.11 = (f32[136,256]{1,0:T(8,128)S(1)}, f32[136,256]{1,0:T(8,128)S(1)}, u32[]{:S(2)}, u32[]{:S(2)}) collective-permute-start(f32[136,256]{1,0:T(8,128)S(1)} %select_maximum_fusion.1), channel_id=1, source_target_pairs={{0,1},{8,3},{16,5},{24,7},{1,9},{9,11},{17,13},{25,15},{2,17},{10,... | collective-permute-start | bytes 417800 | tf_op jit(solution)/shard_map/ppermute | solution.py:258
  15.0 7.0 %collective-permute-done.8 = f32[8,128]{1,0:T(8,128)S(1)} collective-permute-done((f32[8,128]{1,0:T(8,128)S(1)}, f32[8,128]{1,0:T(8,128)S(1)}, u32[]{:S(2)}, u32[]{:S(2)}) %collective-permute-start.8) | collective-permute-done | bytes 4128 | tf_op jit(solution)/shard_map/ppermute | solution.py:261
  22.8 3.6 %collective-permute-done.9 = f32[8,128]{1,0:T(8,128)S(1)} collective-permute-done((f32[8,128]{1,0:T(8,128)S(1)}, f32[8,128]{1,0:T(8,128)S(1)}, u32[]{:S(2)}, u32[]{:S(2)}) %collective-permute-start.9) | collective-permute-done | bytes 4128 | tf_op jit(solution)/shard_map/ppermute | solution.py:261
  28.6 3.4 %collective-permute-start.14 = (f32[136,256]{1,0:T(8,128)S(1)}, f32[136,256]{1,0:T(8,128)S(1)}, u32[]{:S(2)}, u32[]{:S(2)}) collective-permute-start(f32[136,256]{1,0:T(8,128)S(1)} %fusion.1), channel_id=1, source_target_pairs={{0,4},{1,5},{2,6},{3,7},{4,0},{5,1},{6,2},{7,3},{8,12},{9,13},{10,... | collective-permute-start | bytes 417800 | tf_op jit(solution)/shard_map/ppermute | solution.py:261
  32.0 1.9 %collective-permute-start = (f32[136,256]{1,0:T(8,128)S(1)}, f32[136,256]{1,0:T(8,128)S(1)}, u32[]{:S(2)}, u32[]{:S(2)}) collective-permute-start(f32[136,256]{1,0:T(8,128)S(1)} %select_maximum_fusion.4), channel_id=1, source_target_pairs={{0,0},{8,2},{16,4},{24,6},{1,8},{9,10},{17,12},{25,14},{2,16},{10,... | collective-permute-start | bytes 417800 | tf_op jit(solution)/shard_map/ppermute | solution.py:258
  33.9 4.0 %collective-permute-start.1 = (f32[136,256]{1,0:T(8,128)S(1)}, f32[136,256]{1,0:T(8,128)S(1)}, u32[]{:S(2)}, u32[]{:S(2)}) collective-permute-start(f32[136,256]{1,0:T(8,128)S(1)} %select_maximum_fusion.3), channel_id=1, source_target_pairs={{0,1},{8,3},{16,5},{24,7},{1,9},{9,11},{17,13},{25,15},{2,17},{10,... | collective-permute-start | bytes 417800 | tf_op jit(solution)/shard_map/ppermute | solution.py:258
  39.9 2.2 %collective-permute-done.1 = f32[136,256]{1,0:T(8,128)S(1)} collective-permute-done((f32[136,256]{1,0:T(8,128)S(1)}, f32[136,256]{1,0:T(8,128)S(1)}, u32[]{:S(2)}, u32[]{:S(2)}) %collective-permute-start.1) | collective-permute-done | bytes 139296 | tf_op jit(solution)/shard_map/ppermute | solution.py:258
  42.2 2.0 %collective-permute-start.16 = (f32[272,256]{1,0:T(8,128)S(1)}, f32[272,256]{1,0:T(8,128)S(1)}, u32[]{:S(2)}, u32[]{:S(2)}) collective-permute-start(f32[272,256]{1,0:T(8,128)S(1)} %pad_maximum_fusion.3.refs_3_), channel_id=1, source_target_pairs={{0,1},{1,0},{2,3},{3,2},{4,5},{5,4},{6,7},{7,6},{8,9},{9,8},{10,11... | collective-permute-start | bytes 835592 | tf_op jit(solution)/shard_map/ppermute | solution.py:261
  44.2 3.8 %collective-permute-done.15.refs_4_ = f32[272,256]{1,0:T(8,128)S(1)} collective-permute-done((f32[272,256]{1,0:T(8,128)S(1)}, f32[272,256]{1,0:T(8,128)S(1)}, u32[]{:S(2)}, u32[]{:S(2)}) %collective-permute-start.15) | collective-permute-done | bytes 278560 | tf_op jit(solution)/shard_map/ppermute | solution.py:261
  48.2 3.3 %collective-permute-done.2 = f32[136,256]{1,0:T(8,128)S(1)} collective-permute-done((f32[136,256]{1,0:T(8,128)S(1)}, f32[136,256]{1,0:T(8,128)S(1)}, u32[]{:S(2)}, u32[]{:S(2)}) %collective-permute-start.2) | collective-permute-done | bytes 139296 | tf_op jit(solution)/shard_map/ppermute | solution.py:261
  51.7 5.9 %half_grads.4 = (f32[1024,256]{1,0:T(8,128)S(1)}, bf16[2048,256]{1,0:T(8,128)(2,1)S(1)}, bf16[2048,256]{1,0:T(8,128)(2,1)S(1)}, f32[32,256]{1,0:T(8,128)S(1)}, f32[256,2048]{1,0:T(8,128)S(1)}) custom-call(s32[3]{0:T(128)S(1)} %pad_add_fusion.refs_0_, s32[4]{0:T(128)S(1)} %convert_reduce_fusion.1.refs_1_, s32[2048,2048]{1,0:T(8,128)} %refs_2_.7, ...), custom_call_target="tpu_custom_call" | custom-call | flops 7247757312 | bytes 10485760 | tf_op jit(solution)/shard_map/half_grads/pallas_call | solution.py:228
  57.6 2.7 %collective-permute-done.3.refs_12_.refs_4_ = f32[272,256]{1,0:T(8,128)S(1)} collective-permute-done((f32[272,256]{1,0:T(8,128)S(1)}, f32[272,256]{1,0:T(8,128)S(1)}, u32[]{:S(2)}, u32[]{:S(2)}) %collective-permute-start.3) | collective-permute-done | bytes 278560 | tf_op jit(solution)/shard_map/ppermute | solution.py:261
  63.7 10.1 %collective-permute-start.20 = (f32[128,256]{1,0:T(8,128)S(1)}, f32[128,256]{1,0:T(8,128)S(1)}, u32[]{:S(2)}, u32[]{:S(2)}) collective-permute-start(f32[128,256]{1,0:T(8,128)S(1)} %get-tuple-element.46), channel_id=1, source_target_pairs={{0,4},{1,5},{2,6},{3,7},{4,0},{5,1},{6,2},{7,3},{8,12},{9,13},{10,... | collective-permute-start | bytes 393224 | tf_op jit(solution)/shard_map/ppermute | solution.py:261
  75.2 5.9 %half_grads.6 = (f32[1024,256]{1,0:T(8,128)S(1)}, f32[256,2048]{1,0:T(8,128)S(1)}) custom-call(s32[3]{0:T(128)S(1)} %pad_add_fusion.refs_0_, s32[4]{0:T(128)S(1)} %convert_reduce_fusion.1.refs_1_, s32[2048,2048]{1,0:T(8,128)} %refs_2_.7, f32[272,256]{1,0:T(8,128)S(1)} %pad_maximum_fusion.2.refs_12_.refs_3_, ...), custom_call_target="tpu_custom_call" | custom-call | flops 7247757312 | bytes 10485760 | tf_op jit(solution)/shard_map/half_grads/pallas_call | solution.py:228
  81.1 3.3 %collective-permute-done.21 = f32[128,256]{1,0:T(8,128)S(1)} collective-permute-done((f32[128,256]{1,0:T(8,128)S(1)}, f32[128,256]{1,0:T(8,128)S(1)}, u32[]{:S(2)}, u32[]{:S(2)}) %collective-permute-start.21) | collective-permute-done | bytes 131104 | tf_op jit(solution)/shard_map/ppermute | solution.py:261
  84.5 1.5 %half_grads.7 = (f32[512,256]{1,0:T(8,128)S(1)}, f32[512,256]{1,0:T(8,128)S(1)}, f32[256,256]{1,0:T(8,128)S(1)}, f32[256,256]{1,0:T(8,128)S(1)}, f32[256,256]{1,...) custom-call(s32[3]{0:T(128)S(1)} %pad_add_fusion.refs_0_, ...), custom_call_target="tpu_custom_call" | custom-call | flops 2415919104 | bytes 6291456 | tf_op jit(solution)/shard_map/half_grads/pallas_call | solution.py:228
  86.1 6.0 %collective-permute-start.23 = (f32[128,256]{1,0:T(8,128)S(1)}, f32[128,256]{1,0:T(8,128)S(1)}, u32[]{:S(2)}, u32[]{:S(2)}) collective-permute-start(f32[128,256]{1,0:T(8,128)S(1)} %fusion.3.refs_12_), channel_id=1, source_target_pairs={{0,0},{2,8},{4,16},{6,24},{8,1},{10,9},{12,17},{14,25},{16,2},{18,... | collective-permute-start | bytes 393224 | tf_op jit(solution)/shard_map/ppermute | solution.py:258
  93.5 3.3 %collective-permute-done.23 = f32[128,256]{1,0:T(8,128)S(1)} collective-permute-done((f32[128,256]{1,0:T(8,128)S(1)}, f32[128,256]{1,0:T(8,128)S(1)}, u32[]{:S(2)}, u32[]{:S(2)}) %collective-permute-start.23) | collective-permute-done | bytes 131104 | tf_op jit(solution)/shard_map/ppermute | solution.py:258
  96.8 2.5 %collective-permute-done.24 = f32[128,256]{1,0:T(8,128)S(1)} collective-permute-done((f32[128,256]{1,0:T(8,128)S(1)}, f32[128,256]{1,0:T(8,128)S(1)}, u32[]{:S(2)}, u32[]{:S(2)}) %collective-permute-start.24) | collective-permute-done | bytes 131104 | tf_op jit(solution)/shard_map/ppermute | solution.py:258
  99.5 13.3 %collective-permute-start.29 = (f32[256,256]{1,0:T(8,128)S(1)}, f32[256,256]{1,0:T(8,128)S(1)}, u32[]{:S(2)}, u32[]{:S(2)}) collective-permute-start(f32[256,256]{1,0:T(8,128)S(1)} %slice.149), channel_id=1, source_target_pairs={{0,2},{1,3},{2,0},{3,1},{4,6},{5,7},{6,4},{7,5},{8,10},{9,11},{10,... | collective-permute-start | bytes 786440 | tf_op jit(solution)/shard_map/ppermute | solution.py:261
  112.8 4.9 %collective-permute-start.27 = (f32[520,256]{1,0:T(8,128)S(1)}, f32[520,256]{1,0:T(8,128)S(1)}, u32[]{:S(2)}, u32[]{:S(2)}) collective-permute-start(f32[520,256]{1,0:T(8,128)S(1)} %get-tuple-element.52), channel_id=1, source_target_pairs={{0,16},{8,24},{16,0},{24,8},{1,17},{9,25},{17,1},{25,9},{2,18},{10... | collective-permute-start | bytes 1597448 | tf_op jit(solution)/shard_map/ppermute | solution.py:261
  117.7 1.5 %collective-permute-done.29 = f32[256,256]{1,0:T(8,128)S(1)} collective-permute-done((f32[256,256]{1,0:T(8,128)S(1)}, f32[256,256]{1,0:T(8,128)S(1)}, u32[]{:S(2)}, u32[]{:S(2)}) %collective-permute-start.29) | collective-permute-done | bytes 262176 | tf_op jit(solution)/shard_map/ppermute | solution.py:261
  119.3 2.9 %collective-permute-start.30 = (f32[128,256]{1,0:T(8,128)S(1)}, f32[128,256]{1,0:T(8,128)S(1)}, u32[]{:S(2)}, u32[]{:S(2)}) collective-permute-start(f32[128,256]{1,0:T(8,128)S(1)} %slice.151), channel_id=1, source_target_pairs={{0,4},{1,5},{2,6},{3,7},{4,0},{5,1},{6,2},{7,3},{8,12},{9,13},{10,... | collective-permute-start | bytes 393224 | tf_op jit(solution)/shard_map/ppermute | solution.py:261
  122.2 8.1 %collective-permute-start.26 = (f32[256,256]{1,0:T(8,128)S(1)}, f32[256,256]{1,0:T(8,128)S(1)}, u32[]{:S(2)}, u32[]{:S(2)}) collective-permute-start(f32[256,256]{1,0:T(8,128)S(1)} %slice_add_fusion.3), channel_id=1, source_target_pairs={{0,16},{8,24},{16,0},{24,8},{1,17},{9,25},{17,1},{25,9},{2,18},{10... | collective-permute-start | bytes 786440 | tf_op jit(solution)/shard_map/ppermute | solution.py:261
  130.4 1.8 %collective-permute-start.28 = (f32[256,256]{1,0:T(8,128)S(1)}, f32[256,256]{1,0:T(8,128)S(1)}, u32[]{:S(2)}, u32[]{:S(2)}) collective-permute-start(f32[256,256]{1,0:T(8,128)S(1)} %slice_add_fusion.2), channel_id=1, source_target_pairs={{0,8},{8,0},{16,24},{24,16},{1,9},{9,1},{17,25},{25,17},{2,10},{10... | collective-permute-start | bytes 786440 | tf_op jit(solution)/shard_map/ppermute | solution.py:261
  132.2 1.9 %collective-permute-start.31 = (f32[128,256]{1,0:T(8,128)S(1)}, f32[128,256]{1,0:T(8,128)S(1)}, u32[]{:S(2)}, u32[]{:S(2)}) collective-permute-start(f32[128,256]{1,0:T(8,128)S(1)} %slice_add_fusion.5), channel_id=1, source_target_pairs={{0,0},{2,8},{4,16},{6,24},{8,1},{10,9},{12,17},{14,25},{16,2},{18,... | collective-permute-start | bytes 393224 | tf_op jit(solution)/shard_map/ppermute | solution.py:258
  136.8 2.0 %collective-permute-done.28 = f32[256,256]{1,0:T(8,128)S(1)} collective-permute-done((f32[256,256]{1,0:T(8,128)S(1)}, f32[256,256]{1,0:T(8,128)S(1)}, u32[]{:S(2)}, u32[]{:S(2)}) %collective-permute-start.28) | collective-permute-done | bytes 262176 | tf_op jit(solution)/shard_map/ppermute | solution.py:261
  138.8 2.3 %collective-permute-done.31 = f32[128,256]{1,0:T(8,128)S(1)} collective-permute-done((f32[128,256]{1,0:T(8,128)S(1)}, f32[128,256]{1,0:T(8,128)S(1)}, u32[]{:S(2)}, u32[]{:S(2)}) %collective-permute-start.31) | collective-permute-done | bytes 131104 | tf_op jit(solution)/shard_map/ppermute | solution.py:258
  141.2 6.6 %collective-permute-done.32 = f32[128,256]{1,0:T(8,128)S(1)} collective-permute-done((f32[128,256]{1,0:T(8,128)S(1)}, f32[128,256]{1,0:T(8,128)S(1)}, u32[]{:S(2)}, u32[]{:S(2)}) %collective-permute-start.32) | collective-permute-done | bytes 131104 | tf_op jit(solution)/shard_map/ppermute | solution.py:258
  (84 shorter events, 20.2 us)
Async XLA Ops:
  3.0 24.6 %collective-permute-start.6 = (f32[520,256]{1,0:T(8,128)S(1)}, f32[520,256]{1,0:T(8,128)S(1)}, u32[]{:S(2)}, u32[]{:S(2)}) collective-permute-start(f32[520,256]{1,0:T(8,128)S(1)} %select_maximum_fusion.refs_7_), channel_id=1, source_target_pairs={{0,16},{8,24},{16,0},{24,8},{1,17},{9,25},{17,1},{25,9},{2,18},{10... | collective-permute-start | bytes 1597448 | tf_op jit(solution)/shard_map/ppermute | solution.py:261
  4.6 22.9 %collective-permute-start.7 = (f32[520,256]{1,0:T(8,128)S(1)}, f32[520,256]{1,0:T(8,128)S(1)}, u32[]{:S(2)}, u32[]{:S(2)}) collective-permute-start(f32[520,256]{1,0:T(8,128)S(1)} %select_maximum_fusion.refs_7_), channel_id=1, source_target_pairs={{0,8},{8,0},{16,24},{24,16},{1,9},{9,1},{17,25},{25,17},{2,10},{10... | collective-permute-start | bytes 1597448 | tf_op jit(solution)/shard_map/ppermute | solution.py:261
  5.8 16.2 %collective-permute-start.8 = (f32[8,128]{1,0:T(8,128)S(1)}, f32[8,128]{1,0:T(8,128)S(1)}, u32[]{:S(2)}, u32[]{:S(2)}) collective-permute-start(f32[8,128]{1,0:T(8,128)S(1)} %broadcast_in_dim.8), channel_id=1, source_target_pairs={{0,8},{8,0},{16,24},{24,16},{1,9},{9,1},{17,25},{25,17},{2,10},{10... | collective-permute-start | bytes 12296 | tf_op jit(solution)/shard_map/ppermute | solution.py:261
  8.5 19.2 %collective-permute-start.10 = (f32[136,256]{1,0:T(8,128)S(1)}, f32[136,256]{1,0:T(8,128)S(1)}, u32[]{:S(2)}, u32[]{:S(2)}) collective-permute-start(f32[136,256]{1,0:T(8,128)S(1)} %select_maximum_fusion.2), channel_id=1, source_target_pairs={{0,0},{8,2},{16,4},{24,6},{1,8},{9,10},{17,12},{25,14},{2,16},{10,... | collective-permute-start | bytes 417800 | tf_op jit(solution)/shard_map/ppermute | solution.py:258
  12.0 15.8 %collective-permute-start.11 = (f32[136,256]{1,0:T(8,128)S(1)}, f32[136,256]{1,0:T(8,128)S(1)}, u32[]{:S(2)}, u32[]{:S(2)}) collective-permute-start(f32[136,256]{1,0:T(8,128)S(1)} %select_maximum_fusion.1), channel_id=1, source_target_pairs={{0,1},{8,3},{16,5},{24,7},{1,9},{9,11},{17,13},{25,15},{2,17},{10,... | collective-permute-start | bytes 417800 | tf_op jit(solution)/shard_map/ppermute | solution.py:258
  22.7 3.7 %collective-permute-start.9 = (f32[8,128]{1,0:T(8,128)S(1)}, f32[8,128]{1,0:T(8,128)S(1)}, u32[]{:S(2)}, u32[]{:S(2)}) collective-permute-start(f32[8,128]{1,0:T(8,128)S(1)} %broadcast_add_fusion), channel_id=1, source_target_pairs={{0,16},{8,24},{16,0},{24,8},{1,17},{9,25},{17,1},{25,9},{2,18},{10... | collective-permute-start | bytes 12296 | tf_op jit(solution)/shard_map/ppermute | solution.py:261
  27.6 10.4 %collective-permute-start.13 = (f32[264,256]{1,0:T(8,128)S(1)}, f32[264,256]{1,0:T(8,128)S(1)}, u32[]{:S(2)}, u32[]{:S(2)}) collective-permute-start(f32[264,256]{1,0:T(8,128)S(1)} %slice.135), channel_id=1, source_target_pairs={{0,16},{8,24},{16,0},{24,8},{1,17},{9,25},{17,1},{25,9},{2,18},{10... | collective-permute-start | bytes 811016 | tf_op jit(solution)/shard_map/ppermute | solution.py:261
  27.7 10.3 %collective-permute-start.12 = (f32[256,256]{1,0:T(8,128)S(1)}, f32[256,256]{1,0:T(8,128)S(1)}, u32[]{:S(2)}, u32[]{:S(2)}) collective-permute-start(f32[256,256]{1,0:T(8,128)S(1)} %slice.133), channel_id=1, source_target_pairs={{0,8},{8,0},{16,24},{24,16},{1,9},{9,1},{17,25},{25,17},{2,10},{10... | collective-permute-start | bytes 786440 | tf_op jit(solution)/shard_map/ppermute | solution.py:261
  28.6 9.4 %collective-permute-start.14 = (f32[136,256]{1,0:T(8,128)S(1)}, f32[136,256]{1,0:T(8,128)S(1)}, u32[]{:S(2)}, u32[]{:S(2)}) collective-permute-start(f32[136,256]{1,0:T(8,128)S(1)} %fusion.1), channel_id=1, source_target_pairs={{0,4},{1,5},{2,6},{3,7},{4,0},{5,1},{6,2},{7,3},{8,12},{9,13},{10,... | collective-permute-start | bytes 417800 | tf_op jit(solution)/shard_map/ppermute | solution.py:261
  32.0 7.9 %collective-permute-start = (f32[136,256]{1,0:T(8,128)S(1)}, f32[136,256]{1,0:T(8,128)S(1)}, u32[]{:S(2)}, u32[]{:S(2)}) collective-permute-start(f32[136,256]{1,0:T(8,128)S(1)} %select_maximum_fusion.4), channel_id=1, source_target_pairs={{0,0},{8,2},{16,4},{24,6},{1,8},{9,10},{17,12},{25,14},{2,16},{10,... | collective-permute-start | bytes 417800 | tf_op jit(solution)/shard_map/ppermute | solution.py:258
  33.9 8.1 %collective-permute-start.1 = (f32[136,256]{1,0:T(8,128)S(1)}, f32[136,256]{1,0:T(8,128)S(1)}, u32[]{:S(2)}, u32[]{:S(2)}) collective-permute-start(f32[136,256]{1,0:T(8,128)S(1)} %select_maximum_fusion.3), channel_id=1, source_target_pairs={{0,1},{8,3},{16,5},{24,7},{1,9},{9,11},{17,13},{25,15},{2,17},{10,... | collective-permute-start | bytes 417800 | tf_op jit(solution)/shard_map/ppermute | solution.py:258
  38.0 10.0 %collective-permute-start.15 = (f32[272,256]{1,0:T(8,128)S(1)}, f32[272,256]{1,0:T(8,128)S(1)}, u32[]{:S(2)}, u32[]{:S(2)}) collective-permute-start(f32[272,256]{1,0:T(8,128)S(1)} %pad_maximum_fusion.3.refs_3_), channel_id=1, source_target_pairs={{0,2},{1,3},{2,0},{3,1},{4,6},{5,7},{6,4},{7,5},{8,10},{9,11},{10,... | collective-permute-start | bytes 835592 | tf_op jit(solution)/shard_map/ppermute | solution.py:261
  42.1 9.5 %collective-permute-start.2 = (f32[136,256]{1,0:T(8,128)S(1)}, f32[136,256]{1,0:T(8,128)S(1)}, u32[]{:S(2)}, u32[]{:S(2)}) collective-permute-start(f32[136,256]{1,0:T(8,128)S(1)} %broadcast_select_fusion), channel_id=1, source_target_pairs={{0,4},{1,5},{2,6},{3,7},{4,0},{5,1},{6,2},{7,3},{8,12},{9,13},{10,... | collective-permute-start | bytes 417800 | tf_op jit(solution)/shard_map/ppermute | solution.py:261
  42.2 9.5 %collective-permute-start.16 = (f32[272,256]{1,0:T(8,128)S(1)}, f32[272,256]{1,0:T(8,128)S(1)}, u32[]{:S(2)}, u32[]{:S(2)}) collective-permute-start(f32[272,256]{1,0:T(8,128)S(1)} %pad_maximum_fusion.3.refs_3_), channel_id=1, source_target_pairs={{0,1},{1,0},{2,3},{3,2},{4,5},{5,4},{6,7},{7,6},{8,9},{9,8},{10,11... | collective-permute-start | bytes 835592 | tf_op jit(solution)/shard_map/ppermute | solution.py:261
  48.0 3.7 %collective-permute-start.17 = (f32[272,256]{1,0:T(8,128)S(1)}, f32[272,256]{1,0:T(8,128)S(1)}, u32[]{:S(2)}, u32[]{:S(2)}) collective-permute-start(f32[272,256]{1,0:T(8,128)S(1)} %collective-permute-done.15.refs_4_), channel_id=1, source_target_pairs={{0,1},{1,0},{2,3},{3,2},{4,5},{5,4},{6,7},{7,6},{8,9},{9,8},{10,11... | collective-permute-start | bytes 835592 | tf_op jit(solution)/shard_map/ppermute | solution.py:261
  51.6 8.7 %collective-permute-start.3 = (f32[272,256]{1,0:T(8,128)S(1)}, f32[272,256]{1,0:T(8,128)S(1)}, u32[]{:S(2)}, u32[]{:S(2)}) collective-permute-start(f32[272,256]{1,0:T(8,128)S(1)} %pad_maximum_fusion.2.refs_12_.refs_3_), channel_id=1, source_target_pairs={{0,2},{1,3},{2,0},{3,1},{4,6},{5,7},{6,4},{7,5},{8,10},{9,11},{10,... | collective-permute-start | bytes 835592 | tf_op jit(solution)/shard_map/ppermute | solution.py:261
  61.3 13.9 %collective-permute-start.4 = (f32[272,256]{1,0:T(8,128)S(1)}, f32[272,256]{1,0:T(8,128)S(1)}, u32[]{:S(2)}, u32[]{:S(2)}) collective-permute-start(f32[272,256]{1,0:T(8,128)S(1)} %pad_maximum_fusion.2.refs_12_.refs_3_), channel_id=1, source_target_pairs={{0,1},{1,0},{2,3},{3,2},{4,5},{5,4},{6,7},{7,6},{8,9},{9,8},{10,11... | collective-permute-start | bytes 835592 | tf_op jit(solution)/shard_map/ppermute | solution.py:261
  61.8 13.4 %collective-permute-start.5 = (f32[272,256]{1,0:T(8,128)S(1)}, f32[272,256]{1,0:T(8,128)S(1)}, u32[]{:S(2)}, u32[]{:S(2)}) collective-permute-start(f32[272,256]{1,0:T(8,128)S(1)} %collective-permute-done.3.refs_12_.refs_4_), channel_id=1, source_target_pairs={{0,1},{1,0},{2,3},{3,2},{4,5},{5,4},{6,7},{7,6},{8,9},{9,8},{10,11... | collective-permute-start | bytes 835592 | tf_op jit(solution)/shard_map/ppermute | solution.py:261
  63.3 17.8 %collective-permute-start.19 = (f32[128,256]{1,0:T(8,128)S(1)}, f32[128,256]{1,0:T(8,128)S(1)}, u32[]{:S(2)}, u32[]{:S(2)}) collective-permute-start(f32[128,256]{1,0:T(8,128)S(1)} %get-tuple-element.44), channel_id=1, source_target_pairs={{0,2},{1,3},{2,0},{3,1},{4,6},{5,7},{6,4},{7,5},{8,10},{9,11},{10,... | collective-permute-start | bytes 393224 | tf_op jit(solution)/shard_map/ppermute | solution.py:261
  63.7 17.4 %collective-permute-start.20 = (f32[128,256]{1,0:T(8,128)S(1)}, f32[128,256]{1,0:T(8,128)S(1)}, u32[]{:S(2)}, u32[]{:S(2)}) collective-permute-start(f32[128,256]{1,0:T(8,128)S(1)} %get-tuple-element.46), channel_id=1, source_target_pairs={{0,4},{1,5},{2,6},{3,7},{4,0},{5,1},{6,2},{7,3},{8,12},{9,13},{10,... | collective-permute-start | bytes 393224 | tf_op jit(solution)/shard_map/ppermute | solution.py:261
  73.8 10.6 %collective-permute-start.21 = (f32[128,256]{1,0:T(8,128)S(1)}, f32[128,256]{1,0:T(8,128)S(1)}, u32[]{:S(2)}, u32[]{:S(2)}) collective-permute-start(f32[128,256]{1,0:T(8,128)S(1)} %get-tuple-element.45), channel_id=1, source_target_pairs={{0,6},{1,7},{2,4},{3,5},{4,2},{5,3},{6,0},{7,1},{8,14},{9,15},{10,... | collective-permute-start | bytes 393224 | tf_op jit(solution)/shard_map/ppermute | solution.py:261
  86.0 7.4 %collective-permute-start.22 = (f32[512,256]{1,0:T(8,128)S(1)}, f32[512,256]{1,0:T(8,128)S(1)}, u32[]{:S(2)}, u32[]{:S(2)}) collective-permute-start(f32[512,256]{1,0:T(8,128)S(1)} %get-tuple-element.36), channel_id=1, source_target_pairs={{0,1},{1,0},{2,3},{3,2},{4,5},{5,4},{6,7},{7,6},{8,9},{9,8},{10,11... | collective-permute-start | bytes 1572872 | tf_op jit(solution)/shard_map/ppermute | solution.py:261
  86.1 10.7 %collective-permute-start.23 = (f32[128,256]{1,0:T(8,128)S(1)}, f32[128,256]{1,0:T(8,128)S(1)}, u32[]{:S(2)}, u32[]{:S(2)}) collective-permute-start(f32[128,256]{1,0:T(8,128)S(1)} %fusion.3.refs_12_), channel_id=1, source_target_pairs={{0,0},{2,8},{4,16},{6,24},{8,1},{10,9},{12,17},{14,25},{16,2},{18,... | collective-permute-start | bytes 393224 | tf_op jit(solution)/shard_map/ppermute | solution.py:258
  92.1 7.2 %collective-permute-start.24 = (f32[128,256]{1,0:T(8,128)S(1)}, f32[128,256]{1,0:T(8,128)S(1)}, u32[]{:S(2)}, u32[]{:S(2)}) collective-permute-start(f32[128,256]{1,0:T(8,128)S(1)} %fusion.3.refs_12_), channel_id=1, source_target_pairs={{1,0},{3,8},{5,16},{7,24},{9,1},{11,9},{13,17},{15,25},{17,2},{19,... | collective-permute-start | bytes 393224 | tf_op jit(solution)/shard_map/ppermute | solution.py:258
  99.4 22.8 %collective-permute-start.25 = (f32[520,256]{1,0:T(8,128)S(1)}, f32[520,256]{1,0:T(8,128)S(1)}, u32[]{:S(2)}, u32[]{:S(2)}) collective-permute-start(f32[520,256]{1,0:T(8,128)S(1)} %get-tuple-element.51), channel_id=1, source_target_pairs={{0,8},{8,0},{16,24},{24,16},{1,9},{9,1},{17,25},{25,17},{2,10},{10... | collective-permute-start | bytes 1597448 | tf_op jit(solution)/shard_map/ppermute | solution.py:261
  99.5 19.7 %collective-permute-start.29 = (f32[256,256]{1,0:T(8,128)S(1)}, f32[256,256]{1,0:T(8,128)S(1)}, u32[]{:S(2)}, u32[]{:S(2)}) collective-permute-start(f32[256,256]{1,0:T(8,128)S(1)} %slice.149), channel_id=1, source_target_pairs={{0,2},{1,3},{2,0},{3,1},{4,6},{5,7},{6,4},{7,5},{8,10},{9,11},{10,... | collective-permute-start | bytes 786440 | tf_op jit(solution)/shard_map/ppermute | solution.py:261
  112.8 17.6 %collective-permute-start.27 = (f32[520,256]{1,0:T(8,128)S(1)}, f32[520,256]{1,0:T(8,128)S(1)}, u32[]{:S(2)}, u32[]{:S(2)}) collective-permute-start(f32[520,256]{1,0:T(8,128)S(1)} %get-tuple-element.52), channel_id=1, source_target_pairs={{0,16},{8,24},{16,0},{24,8},{1,17},{9,25},{17,1},{25,9},{2,18},{10... | collective-permute-start | bytes 1597448 | tf_op jit(solution)/shard_map/ppermute | solution.py:261
  119.3 13.0 %collective-permute-start.30 = (f32[128,256]{1,0:T(8,128)S(1)}, f32[128,256]{1,0:T(8,128)S(1)}, u32[]{:S(2)}, u32[]{:S(2)}) collective-permute-start(f32[128,256]{1,0:T(8,128)S(1)} %slice.151), channel_id=1, source_target_pairs={{0,4},{1,5},{2,6},{3,7},{4,0},{5,1},{6,2},{7,3},{8,12},{9,13},{10,... | collective-permute-start | bytes 393224 | tf_op jit(solution)/shard_map/ppermute | solution.py:261
  122.2 14.5 %collective-permute-start.26 = (f32[256,256]{1,0:T(8,128)S(1)}, f32[256,256]{1,0:T(8,128)S(1)}, u32[]{:S(2)}, u32[]{:S(2)}) collective-permute-start(f32[256,256]{1,0:T(8,128)S(1)} %slice_add_fusion.3), channel_id=1, source_target_pairs={{0,16},{8,24},{16,0},{24,8},{1,17},{9,25},{17,1},{25,9},{2,18},{10... | collective-permute-start | bytes 786440 | tf_op jit(solution)/shard_map/ppermute | solution.py:261
  130.4 8.4 %collective-permute-start.28 = (f32[256,256]{1,0:T(8,128)S(1)}, f32[256,256]{1,0:T(8,128)S(1)}, u32[]{:S(2)}, u32[]{:S(2)}) collective-permute-start(f32[256,256]{1,0:T(8,128)S(1)} %slice_add_fusion.2), channel_id=1, source_target_pairs={{0,8},{8,0},{16,24},{24,16},{1,9},{9,1},{17,25},{25,17},{2,10},{10... | collective-permute-start | bytes 786440 | tf_op jit(solution)/shard_map/ppermute | solution.py:261
  132.2 8.9 %collective-permute-start.31 = (f32[128,256]{1,0:T(8,128)S(1)}, f32[128,256]{1,0:T(8,128)S(1)}, u32[]{:S(2)}, u32[]{:S(2)}) collective-permute-start(f32[128,256]{1,0:T(8,128)S(1)} %slice_add_fusion.5), channel_id=1, source_target_pairs={{0,0},{2,8},{4,16},{6,24},{8,1},{10,9},{12,17},{14,25},{16,2},{18,... | collective-permute-start | bytes 393224 | tf_op jit(solution)/shard_map/ppermute | solution.py:258
  134.2 13.6 %collective-permute-start.32 = (f32[128,256]{1,0:T(8,128)S(1)}, f32[128,256]{1,0:T(8,128)S(1)}, u32[]{:S(2)}, u32[]{:S(2)}) collective-permute-start(f32[128,256]{1,0:T(8,128)S(1)} %slice_add_fusion.5), channel_id=1, source_target_pairs={{1,0},{3,8},{5,16},{7,24},{9,1},{11,9},{13,17},{15,25},{17,2},{19,... | collective-permute-start | bytes 393224 | tf_op jit(solution)/shard_map/ppermute | solution.py:258
  (4 other events, 98.7 us)

commit v6 on v5

--- a/solution.py
+++ b/solution.py
@@ -328,13 +328,15 @@
         return summed, total
 
     def from_line(outs):
-        summed = total = outs[0] + across(outs[1])
+        total = outs[0] + across(outs[1])
         step = 1
         while step < groups:
             kept = total.shape[0] // 2
-            total = total[:kept] + swapped(total[kept:], "col", 2 * step)
+            came = swapped(total[kept:], "col", 2 * step)
+            first_came = came if step == 1 else first_came
+            total = total[:kept] + came
             step *= 2
-        return summed, total
+        return first_came, total
 
     def to_home(total):
         homes = []
@@ -352,13 +354,13 @@
     vectors = [lower, upper, across(lower), across(upper)]
     outs = grads(1, tiles=tiles[:-1], vectors=vectors, held=[*columns, outs[2]], row_in=None, ready=[first_summed])
     outs = grads(1, tiles=tiles[-1:], vectors=vectors, held=[*columns, outs[1]], row_in=outs[0], ready=[first_total])
-    second_summed, second_total = from_line(outs)
+    second_came, second_total = from_line(outs)
     first_quarters = to_home(first_total)
     quarters = first_quarters + to_home(second_total)
 
     halves = outs[2:]
     if groups == 4:
-        spare = second_summed[:PAD] + first_quarters[0][:PAD] + first_quarters[1][:PAD]
+        spare = second_came[:PAD] + first_quarters[0][:PAD] + first_quarters[1][:PAD]
         first_x = row_swapped(jnp.concatenate([halves[2], halves[6], spare], axis=0), 1)[: 2 * half]
         first_y = row_swapped(jnp.concatenate([halves[5], halves[7], spare], axis=0), 2)[: 2 * half]
         second_x = row_swapped(halves[3] + first_y[half:], 1)

time: 149 us -> 148 us (level); the launches traced: 149 us -> 150 us
  waiting for transfers between devices: 47.9 us -> 50.2 us
    ppermute x25, waiting for transfers between devices: 29.9 us -> 32 us  [swapped(): lax.ppermute(value, axis, [(r, r ^ m) for r in range(lax.axis_size(axis))])]
    ppermute x25, starting transfers between devices: 53.9 us -> 52.1 us  [swapped(): lax.ppermute(value, axis, [(r, r ^ m) for r in range(lax.axis_size(axis))])]
  transfers between devices with their start and end apart: 33 -> 33, of which waited for: 16 -> 17; matrix products, arithmetic and copies ran while one was open for 3% -> 3% of each run, Pallas kernels for 8% -> 8%
where the time goes in v6:
time: 148 us; the launch traced here: 150 us
  starting transfers between devices  75.7 us (51%)
  waiting for transfers between devices  50.2 us (34%)
  Pallas kernels  14.1 us (10%)
  other arithmetic  6.33 us (4%)
  local copies, waits for them, and re-layouts  2.43 us (2%)
    ppermute x25, starting transfers between devices, swapped(): lax.ppermute(value, axis, [(r, r ^ m) for r in range(lax.axis_size(axis))])  52.1 us
    ppermute x25, waiting for transfers between devices, swapped(): lax.ppermute(value, axis, [(r, r ^ m) for r in range(lax.axis_size(axis))])  32 us
    ppermute x8, starting transfers between devices, permute(): return lax.ppermute(value, both, pairs)  23.6 us
    ppermute x8, waiting for transfers between devices, permute(): return lax.ppermute(value, both, pairs)  18.3 us
    pallas_call x4, Pallas kernels, half_grads(): pl.pallas_call(functools.partial(half_kernel, k, groups, share, layout, t...  14.1 us
  transfers between devices with their start and end apart: 33, of which 17 were waited for; matrix products, arithmetic and copies ran while one was open for 3% of the time, Pallas kernels for 8%

profile of v6, /device:TPU:2, one launch (start us, length us, event | category | flops | bytes accessed | tf_op | source)
XLA Modules:
  0.0 149.8 jit_solution(9998712861480407378)
XLA Ops:
  3.0 1.6 %collective-permute-start.6 = (f32[520,256]{1,0:T(8,128)S(1)}, f32[520,256]{1,0:T(8,128)S(1)}, u32[]{:S(2)}, u32[]{:S(2)}) collective-permute-start(f32[520,256]{1,0:T(8,128)S(1)} %select_maximum_fusion.refs_7_), channel_id=1, source_target_pairs={{0,16},{8,24},{16,0},{24,8},{1,17},{9,25},{17,1},{25,9},{2,18},{10... | collective-permute-start | bytes 1597448 | tf_op jit(solution)/shard_map/ppermute | solution.py:261
  5.8 1.6 %collective-permute-start.8 = (f32[8,128]{1,0:T(8,128)S(1)}, f32[8,128]{1,0:T(8,128)S(1)}, u32[]{:S(2)}, u32[]{:S(2)}) collective-permute-start(f32[8,128]{1,0:T(8,128)S(1)} %broadcast_in_dim.8), channel_id=1, source_target_pairs={{0,8},{8,0},{16,24},{24,16},{1,9},{9,1},{17,25},{25,17},{2,10},{10... | collective-permute-start | bytes 12296 | tf_op jit(solution)/shard_map/ppermute | solution.py:261
  8.5 3.5 %collective-permute-start.10 = (f32[136,256]{1,0:T(8,128)S(1)}, f32[136,256]{1,0:T(8,128)S(1)}, u32[]{:S(2)}, u32[]{:S(2)}) collective-permute-start(f32[136,256]{1,0:T(8,128)S(1)} %select_maximum_fusion.2), channel_id=1, source_target_pairs={{0,0},{8,2},{16,4},{24,6},{1,8},{9,10},{17,12},{25,14},{2,16},{10,... | collective-permute-start | bytes 417800 | tf_op jit(solution)/shard_map/ppermute | solution.py:258
  12.0 3.0 %collective-permute-start.11 = (f32[136,256]{1,0:T(8,128)S(1)}, f32[136,256]{1,0:T(8,128)S(1)}, u32[]{:S(2)}, u32[]{:S(2)}) collective-permute-start(f32[136,256]{1,0:T(8,128)S(1)} %select_maximum_fusion.1), channel_id=1, source_target_pairs={{0,1},{8,3},{16,5},{24,7},{1,9},{9,11},{17,13},{25,15},{2,17},{10,... | collective-permute-start | bytes 417800 | tf_op jit(solution)/shard_map/ppermute | solution.py:258
  15.0 7.0 %collective-permute-done.8 = f32[8,128]{1,0:T(8,128)S(1)} collective-permute-done((f32[8,128]{1,0:T(8,128)S(1)}, f32[8,128]{1,0:T(8,128)S(1)}, u32[]{:S(2)}, u32[]{:S(2)}) %collective-permute-start.8) | collective-permute-done | bytes 4128 | tf_op jit(solution)/shard_map/ppermute | solution.py:261
  22.8 3.6 %collective-permute-done.9 = f32[8,128]{1,0:T(8,128)S(1)} collective-permute-done((f32[8,128]{1,0:T(8,128)S(1)}, f32[8,128]{1,0:T(8,128)S(1)}, u32[]{:S(2)}, u32[]{:S(2)}) %collective-permute-start.9) | collective-permute-done | bytes 4128 | tf_op jit(solution)/shard_map/ppermute | solution.py:261
  28.6 3.4 %collective-permute-start.14 = (f32[136,256]{1,0:T(8,128)S(1)}, f32[136,256]{1,0:T(8,128)S(1)}, u32[]{:S(2)}, u32[]{:S(2)}) collective-permute-start(f32[136,256]{1,0:T(8,128)S(1)} %fusion.1), channel_id=1, source_target_pairs={{0,4},{1,5},{2,6},{3,7},{4,0},{5,1},{6,2},{7,3},{8,12},{9,13},{10,... | collective-permute-start | bytes 417800 | tf_op jit(solution)/shard_map/ppermute | solution.py:261
  32.0 1.9 %collective-permute-start = (f32[136,256]{1,0:T(8,128)S(1)}, f32[136,256]{1,0:T(8,128)S(1)}, u32[]{:S(2)}, u32[]{:S(2)}) collective-permute-start(f32[136,256]{1,0:T(8,128)S(1)} %select_maximum_fusion.4), channel_id=1, source_target_pairs={{0,0},{8,2},{16,4},{24,6},{1,8},{9,10},{17,12},{25,14},{2,16},{10,... | collective-permute-start | bytes 417800 | tf_op jit(solution)/shard_map/ppermute | solution.py:258
  33.9 4.0 %collective-permute-start.1 = (f32[136,256]{1,0:T(8,128)S(1)}, f32[136,256]{1,0:T(8,128)S(1)}, u32[]{:S(2)}, u32[]{:S(2)}) collective-permute-start(f32[136,256]{1,0:T(8,128)S(1)} %select_maximum_fusion.3), channel_id=1, source_target_pairs={{0,1},{8,3},{16,5},{24,7},{1,9},{9,11},{17,13},{25,15},{2,17},{10,... | collective-permute-start | bytes 417800 | tf_op jit(solution)/shard_map/ppermute | solution.py:258
  39.9 2.2 %collective-permute-done.1 = f32[136,256]{1,0:T(8,128)S(1)} collective-permute-done((f32[136,256]{1,0:T(8,128)S(1)}, f32[136,256]{1,0:T(8,128)S(1)}, u32[]{:S(2)}, u32[]{:S(2)}) %collective-permute-start.1) | collective-permute-done | bytes 139296 | tf_op jit(solution)/shard_map/ppermute | solution.py:258
  42.2 2.0 %collective-permute-start.16 = (f32[272,256]{1,0:T(8,128)S(1)}, f32[272,256]{1,0:T(8,128)S(1)}, u32[]{:S(2)}, u32[]{:S(2)}) collective-permute-start(f32[272,256]{1,0:T(8,128)S(1)} %pad_maximum_fusion.3.refs_3_), channel_id=1, source_target_pairs={{0,1},{1,0},{2,3},{3,2},{4,5},{5,4},{6,7},{7,6},{8,9},{9,8},{10,11... | collective-permute-start | bytes 835592 | tf_op jit(solution)/shard_map/ppermute | solution.py:261
  44.2 3.8 %collective-permute-done.15.refs_4_ = f32[272,256]{1,0:T(8,128)S(1)} collective-permute-done((f32[272,256]{1,0:T(8,128)S(1)}, f32[272,256]{1,0:T(8,128)S(1)}, u32[]{:S(2)}, u32[]{:S(2)}) %collective-permute-start.15) | collective-permute-done | bytes 278560 | tf_op jit(solution)/shard_map/ppermute | solution.py:261
  48.2 3.3 %collective-permute-done.2 = f32[136,256]{1,0:T(8,128)S(1)} collective-permute-done((f32[136,256]{1,0:T(8,128)S(1)}, f32[136,256]{1,0:T(8,128)S(1)}, u32[]{:S(2)}, u32[]{:S(2)}) %collective-permute-start.2) | collective-permute-done | bytes 139296 | tf_op jit(solution)/shard_map/ppermute | solution.py:261
  51.7 5.9 %half_grads.4 = (f32[1024,256]{1,0:T(8,128)S(1)}, bf16[2048,256]{1,0:T(8,128)(2,1)S(1)}, bf16[2048,256]{1,0:T(8,128)(2,1)S(1)}, f32[32,256]{1,0:T(8,128)S(1)}, f32[256,2048]{1,0:T(8,128)S(1)}) custom-call(s32[3]{0:T(128)S(1)} %pad_add_fusion.refs_0_, s32[4]{0:T(128)S(1)} %convert_reduce_fusion.1.refs_1_, s32[2048,2048]{1,0:T(8,128)} %refs_2_.7, ...), custom_call_target="tpu_custom_call" | custom-call | flops 7247757312 | bytes 10485760 | tf_op jit(solution)/shard_map/half_grads/pallas_call | solution.py:228
  57.6 2.7 %collective-permute-done.3.refs_12_.refs_4_ = f32[272,256]{1,0:T(8,128)S(1)} collective-permute-done((f32[272,256]{1,0:T(8,128)S(1)}, f32[272,256]{1,0:T(8,128)S(1)}, u32[]{:S(2)}, u32[]{:S(2)}) %collective-permute-start.3) | collective-permute-done | bytes 278560 | tf_op jit(solution)/shard_map/ppermute | solution.py:261
  61.9 1.3 collective-permute-done.18
  63.3 5.1 %collective-permute-start.19 = (f32[128,256]{1,0:T(8,128)S(1)}, f32[128,256]{1,0:T(8,128)S(1)}, u32[]{:S(2)}, u32[]{:S(2)}) collective-permute-start(f32[128,256]{1,0:T(8,128)S(1)} %get-tuple-element.44), channel_id=1, source_target_pairs={{0,2},{1,3},{2,0},{3,1},{4,6},{5,7},{6,4},{7,5},{8,10},{9,11},{10,... | collective-permute-start | bytes 393224 | tf_op jit(solution)/shard_map/ppermute | solution.py:261
  68.5 2.4 %collective-permute-start.21 = (f32[128,256]{1,0:T(8,128)S(1)}, f32[128,256]{1,0:T(8,128)S(1)}, u32[]{:S(2)}, u32[]{:S(2)}) collective-permute-start(f32[128,256]{1,0:T(8,128)S(1)} %get-tuple-element.45), channel_id=1, source_target_pairs={{0,6},{1,7},{2,4},{3,5},{4,2},{5,3},{6,0},{7,1},{8,14},{9,15},{10,... | collective-permute-start | bytes 393224 | tf_op jit(solution)/shard_map/ppermute | solution.py:261
  70.9 5.7 %half_grads.6 = (f32[1024,256]{1,0:T(8,128)S(1)}, f32[256,2048]{1,0:T(8,128)S(1)}) custom-call(s32[3]{0:T(128)S(1)} %pad_add_fusion.refs_0_, s32[4]{0:T(128)S(1)} %convert_reduce_fusion.1.refs_1_, s32[2048,2048]{1,0:T(8,128)} %refs_2_.7, f32[272,256]{1,0:T(8,128)S(1)} %pad_maximum_fusion.2.refs_12_.refs_3_, ...), custom_call_target="tpu_custom_call" | custom-call | flops 7247757312 | bytes 10485760 | tf_op jit(solution)/shard_map/half_grads/pallas_call | solution.py:228
  76.6 4.3 %collective-permute-done.20 = f32[128,256]{1,0:T(8,128)S(1)} collective-permute-done((f32[128,256]{1,0:T(8,128)S(1)}, f32[128,256]{1,0:T(8,128)S(1)}, u32[]{:S(2)}, u32[]{:S(2)}) %collective-permute-start.20) | collective-permute-done | bytes 131104 | tf_op jit(solution)/shard_map/ppermute | solution.py:261
  80.9 1.5 %half_grads.7 = (f32[512,256]{1,0:T(8,128)S(1)}, f32[512,256]{1,0:T(8,128)S(1)}, f32[256,256]{1,0:T(8,128)S(1)}, f32[256,256]{1,0:T(8,128)S(1)}, f32[256,256]{1,...) custom-call(s32[3]{0:T(128)S(1)} %pad_add_fusion.refs_0_, ...), custom_call_target="tpu_custom_call" | custom-call | flops 2415919104 | bytes 6291456 | tf_op jit(solution)/shard_map/half_grads/pallas_call | solution.py:228
  82.5 1.9 %collective-permute-done.22 = f32[512,256]{1,0:T(8,128)S(1)} collective-permute-done((f32[512,256]{1,0:T(8,128)S(1)}, f32[512,256]{1,0:T(8,128)S(1)}, u32[]{:S(2)}, u32[]{:S(2)}) %collective-permute-start.22) | collective-permute-done | bytes 524320 | tf_op jit(solution)/shard_map/ppermute | solution.py:261
  84.5 7.5 %collective-permute-start.23 = (f32[256,256]{1,0:T(8,128)S(1)}, f32[256,256]{1,0:T(8,128)S(1)}, u32[]{:S(2)}, u32[]{:S(2)}) collective-permute-start(f32[256,256]{1,0:T(8,128)S(1)} %slice.141), channel_id=1, source_target_pairs={{0,2},{1,3},{2,0},{3,1},{4,6},{5,7},{6,4},{7,5},{8,10},{9,11},{10,... | collective-permute-start | bytes 786440 | tf_op jit(solution)/shard_map/ppermute | solution.py:261
  92.1 6.8 %collective-permute-start.24 = (f32[128,256]{1,0:T(8,128)S(1)}, f32[128,256]{1,0:T(8,128)S(1)}, u32[]{:S(2)}, u32[]{:S(2)}) collective-permute-start(f32[128,256]{1,0:T(8,128)S(1)} %fusion.3.refs_12_), channel_id=1, source_target_pairs={{0,0},{2,8},{4,16},{6,24},{8,1},{10,9},{12,17},{14,25},{16,2},{18,... | collective-permute-start | bytes 393224 | tf_op jit(solution)/shard_map/ppermute | solution.py:258
  98.8 1.3 collective-permute-start.25
  100.1 5.0 %collective-permute-done.24 = f32[128,256]{1,0:T(8,128)S(1)} collective-permute-done((f32[128,256]{1,0:T(8,128)S(1)}, f32[128,256]{1,0:T(8,128)S(1)}, u32[]{:S(2)}, u32[]{:S(2)}) %collective-permute-start.24) | collective-permute-done | bytes 131104 | tf_op jit(solution)/shard_map/ppermute | solution.py:258
  106.5 12.9 %collective-permute-start.28 = (f32[520,256]{1,0:T(8,128)S(1)}, f32[520,256]{1,0:T(8,128)S(1)}, u32[]{:S(2)}, u32[]{:S(2)}) collective-permute-start(f32[520,256]{1,0:T(8,128)S(1)} %get-tuple-element.52), channel_id=1, source_target_pairs={{0,16},{8,24},{16,0},{24,8},{1,17},{9,25},{17,1},{25,9},{2,18},{10... | collective-permute-start | bytes 1597448 | tf_op jit(solution)/shard_map/ppermute | solution.py:261
  120.6 11.2 %collective-permute-start.27 = (f32[256,256]{1,0:T(8,128)S(1)}, f32[256,256]{1,0:T(8,128)S(1)}, u32[]{:S(2)}, u32[]{:S(2)}) collective-permute-start(f32[256,256]{1,0:T(8,128)S(1)} %slice_add_fusion.3), channel_id=1, source_target_pairs={{0,16},{8,24},{16,0},{24,8},{1,17},{9,25},{17,1},{25,9},{2,18},{10... | collective-permute-start | bytes 786440 | tf_op jit(solution)/shard_map/ppermute | solution.py:261
  131.8 1.8 %collective-permute-start.29 = (f32[256,256]{1,0:T(8,128)S(1)}, f32[256,256]{1,0:T(8,128)S(1)}, u32[]{:S(2)}, u32[]{:S(2)}) collective-permute-start(f32[256,256]{1,0:T(8,128)S(1)} %slice_add_fusion.2), channel_id=1, source_target_pairs={{0,8},{8,0},{16,24},{24,16},{1,9},{9,1},{17,25},{25,17},{2,10},{10... | collective-permute-start | bytes 786440 | tf_op jit(solution)/shard_map/ppermute | solution.py:261
  133.6 1.9 %collective-permute-start.31 = (f32[128,256]{1,0:T(8,128)S(1)}, f32[128,256]{1,0:T(8,128)S(1)}, u32[]{:S(2)}, u32[]{:S(2)}) collective-permute-start(f32[128,256]{1,0:T(8,128)S(1)} %slice_add_fusion.5), channel_id=1, source_target_pairs={{0,0},{2,8},{4,16},{6,24},{8,1},{10,9},{12,17},{14,25},{16,2},{18,... | collective-permute-start | bytes 393224 | tf_op jit(solution)/shard_map/ppermute | solution.py:258
  137.8 2.1 %collective-permute-done.29 = f32[256,256]{1,0:T(8,128)S(1)} collective-permute-done((f32[256,256]{1,0:T(8,128)S(1)}, f32[256,256]{1,0:T(8,128)S(1)}, u32[]{:S(2)}, u32[]{:S(2)}) %collective-permute-start.29) | collective-permute-done | bytes 262176 | tf_op jit(solution)/shard_map/ppermute | solution.py:261
  140.0 8.1 %collective-permute-done.31 = f32[128,256]{1,0:T(8,128)S(1)} collective-permute-done((f32[128,256]{1,0:T(8,128)S(1)}, f32[128,256]{1,0:T(8,128)S(1)}, u32[]{:S(2)}, u32[]{:S(2)}) %collective-permute-start.31) | collective-permute-done | bytes 131104 | tf_op jit(solution)/shard_map/ppermute | solution.py:258
  (84 shorter events, 18.4 us)
Async XLA Ops:
  3.0 24.6 %collective-permute-start.6 = (f32[520,256]{1,0:T(8,128)S(1)}, f32[520,256]{1,0:T(8,128)S(1)}, u32[]{:S(2)}, u32[]{:S(2)}) collective-permute-start(f32[520,256]{1,0:T(8,128)S(1)} %select_maximum_fusion.refs_7_), channel_id=1, source_target_pairs={{0,16},{8,24},{16,0},{24,8},{1,17},{9,25},{17,1},{25,9},{2,18},{10... | collective-permute-start | bytes 1597448 | tf_op jit(solution)/shard_map/ppermute | solution.py:261
  4.6 22.9 %collective-permute-start.7 = (f32[520,256]{1,0:T(8,128)S(1)}, f32[520,256]{1,0:T(8,128)S(1)}, u32[]{:S(2)}, u32[]{:S(2)}) collective-permute-start(f32[520,256]{1,0:T(8,128)S(1)} %select_maximum_fusion.refs_7_), channel_id=1, source_target_pairs={{0,8},{8,0},{16,24},{24,16},{1,9},{9,1},{17,25},{25,17},{2,10},{10... | collective-permute-start | bytes 1597448 | tf_op jit(solution)/shard_map/ppermute | solution.py:261
  5.8 16.2 %collective-permute-start.8 = (f32[8,128]{1,0:T(8,128)S(1)}, f32[8,128]{1,0:T(8,128)S(1)}, u32[]{:S(2)}, u32[]{:S(2)}) collective-permute-start(f32[8,128]{1,0:T(8,128)S(1)} %broadcast_in_dim.8), channel_id=1, source_target_pairs={{0,8},{8,0},{16,24},{24,16},{1,9},{9,1},{17,25},{25,17},{2,10},{10... | collective-permute-start | bytes 12296 | tf_op jit(solution)/shard_map/ppermute | solution.py:261
  8.5 19.2 %collective-permute-start.10 = (f32[136,256]{1,0:T(8,128)S(1)}, f32[136,256]{1,0:T(8,128)S(1)}, u32[]{:S(2)}, u32[]{:S(2)}) collective-permute-start(f32[136,256]{1,0:T(8,128)S(1)} %select_maximum_fusion.2), channel_id=1, source_target_pairs={{0,0},{8,2},{16,4},{24,6},{1,8},{9,10},{17,12},{25,14},{2,16},{10,... | collective-permute-start | bytes 417800 | tf_op jit(solution)/shard_map/ppermute | solution.py:258
  12.0 15.8 %collective-permute-start.11 = (f32[136,256]{1,0:T(8,128)S(1)}, f32[136,256]{1,0:T(8,128)S(1)}, u32[]{:S(2)}, u32[]{:S(2)}) collective-permute-start(f32[136,256]{1,0:T(8,128)S(1)} %select_maximum_fusion.1), channel_id=1, source_target_pairs={{0,1},{8,3},{16,5},{24,7},{1,9},{9,11},{17,13},{25,15},{2,17},{10,... | collective-permute-start | bytes 417800 | tf_op jit(solution)/shard_map/ppermute | solution.py:258
  22.7 3.7 %collective-permute-start.9 = (f32[8,128]{1,0:T(8,128)S(1)}, f32[8,128]{1,0:T(8,128)S(1)}, u32[]{:S(2)}, u32[]{:S(2)}) collective-permute-start(f32[8,128]{1,0:T(8,128)S(1)} %broadcast_add_fusion), channel_id=1, source_target_pairs={{0,16},{8,24},{16,0},{24,8},{1,17},{9,25},{17,1},{25,9},{2,18},{10... | collective-permute-start | bytes 12296 | tf_op jit(solution)/shard_map/ppermute | solution.py:261
  27.6 10.4 %collective-permute-start.13 = (f32[264,256]{1,0:T(8,128)S(1)}, f32[264,256]{1,0:T(8,128)S(1)}, u32[]{:S(2)}, u32[]{:S(2)}) collective-permute-start(f32[264,256]{1,0:T(8,128)S(1)} %slice.135), channel_id=1, source_target_pairs={{0,16},{8,24},{16,0},{24,8},{1,17},{9,25},{17,1},{25,9},{2,18},{10... | collective-permute-start | bytes 811016 | tf_op jit(solution)/shard_map/ppermute | solution.py:261
  27.7 10.3 %collective-permute-start.12 = (f32[256,256]{1,0:T(8,128)S(1)}, f32[256,256]{1,0:T(8,128)S(1)}, u32[]{:S(2)}, u32[]{:S(2)}) collective-permute-start(f32[256,256]{1,0:T(8,128)S(1)} %slice.133), channel_id=1, source_target_pairs={{0,8},{8,0},{16,24},{24,16},{1,9},{9,1},{17,25},{25,17},{2,10},{10... | collective-permute-start | bytes 786440 | tf_op jit(solution)/shard_map/ppermute | solution.py:261
  28.6 9.4 %collective-permute-start.14 = (f32[136,256]{1,0:T(8,128)S(1)}, f32[136,256]{1,0:T(8,128)S(1)}, u32[]{:S(2)}, u32[]{:S(2)}) collective-permute-start(f32[136,256]{1,0:T(8,128)S(1)} %fusion.1), channel_id=1, source_target_pairs={{0,4},{1,5},{2,6},{3,7},{4,0},{5,1},{6,2},{7,3},{8,12},{9,13},{10,... | collective-permute-start | bytes 417800 | tf_op jit(solution)/shard_map/ppermute | solution.py:261
  32.0 7.9 %collective-permute-start = (f32[136,256]{1,0:T(8,128)S(1)}, f32[136,256]{1,0:T(8,128)S(1)}, u32[]{:S(2)}, u32[]{:S(2)}) collective-permute-start(f32[136,256]{1,0:T(8,128)S(1)} %select_maximum_fusion.4), channel_id=1, source_target_pairs={{0,0},{8,2},{16,4},{24,6},{1,8},{9,10},{17,12},{25,14},{2,16},{10,... | collective-permute-start | bytes 417800 | tf_op jit(solution)/shard_map/ppermute | solution.py:258
  33.9 8.1 %collective-permute-start.1 = (f32[136,256]{1,0:T(8,128)S(1)}, f32[136,256]{1,0:T(8,128)S(1)}, u32[]{:S(2)}, u32[]{:S(2)}) collective-permute-start(f32[136,256]{1,0:T(8,128)S(1)} %select_maximum_fusion.3), channel_id=1, source_target_pairs={{0,1},{8,3},{16,5},{24,7},{1,9},{9,11},{17,13},{25,15},{2,17},{10,... | collective-permute-start | bytes 417800 | tf_op jit(solution)/shard_map/ppermute | solution.py:258
  38.0 10.0 %collective-permute-start.15 = (f32[272,256]{1,0:T(8,128)S(1)}, f32[272,256]{1,0:T(8,128)S(1)}, u32[]{:S(2)}, u32[]{:S(2)}) collective-permute-start(f32[272,256]{1,0:T(8,128)S(1)} %pad_maximum_fusion.3.refs_3_), channel_id=1, source_target_pairs={{0,2},{1,3},{2,0},{3,1},{4,6},{5,7},{6,4},{7,5},{8,10},{9,11},{10,... | collective-permute-start | bytes 835592 | tf_op jit(solution)/shard_map/ppermute | solution.py:261
  42.1 9.5 %collective-permute-start.2 = (f32[136,256]{1,0:T(8,128)S(1)}, f32[136,256]{1,0:T(8,128)S(1)}, u32[]{:S(2)}, u32[]{:S(2)}) collective-permute-start(f32[136,256]{1,0:T(8,128)S(1)} %broadcast_select_fusion), channel_id=1, source_target_pairs={{0,4},{1,5},{2,6},{3,7},{4,0},{5,1},{6,2},{7,3},{8,12},{9,13},{10,... | collective-permute-start | bytes 417800 | tf_op jit(solution)/shard_map/ppermute | solution.py:261
  42.2 9.5 %collective-permute-start.16 = (f32[272,256]{1,0:T(8,128)S(1)}, f32[272,256]{1,0:T(8,128)S(1)}, u32[]{:S(2)}, u32[]{:S(2)}) collective-permute-start(f32[272,256]{1,0:T(8,128)S(1)} %pad_maximum_fusion.3.refs_3_), channel_id=1, source_target_pairs={{0,1},{1,0},{2,3},{3,2},{4,5},{5,4},{6,7},{7,6},{8,9},{9,8},{10,11... | collective-permute-start | bytes 835592 | tf_op jit(solution)/shard_map/ppermute | solution.py:261
  48.0 3.7 %collective-permute-start.17 = (f32[272,256]{1,0:T(8,128)S(1)}, f32[272,256]{1,0:T(8,128)S(1)}, u32[]{:S(2)}, u32[]{:S(2)}) collective-permute-start(f32[272,256]{1,0:T(8,128)S(1)} %collective-permute-done.15.refs_4_), channel_id=1, source_target_pairs={{0,1},{1,0},{2,3},{3,2},{4,5},{5,4},{6,7},{7,6},{8,9},{9,8},{10,11... | collective-permute-start | bytes 835592 | tf_op jit(solution)/shard_map/ppermute | solution.py:261
  51.6 8.7 %collective-permute-start.3 = (f32[272,256]{1,0:T(8,128)S(1)}, f32[272,256]{1,0:T(8,128)S(1)}, u32[]{:S(2)}, u32[]{:S(2)}) collective-permute-start(f32[272,256]{1,0:T(8,128)S(1)} %pad_maximum_fusion.2.refs_12_.refs_3_), channel_id=1, source_target_pairs={{0,2},{1,3},{2,0},{3,1},{4,6},{5,7},{6,4},{7,5},{8,10},{9,11},{10,... | collective-permute-start | bytes 835592 | tf_op jit(solution)/shard_map/ppermute | solution.py:261
  61.3 9.6 %collective-permute-start.4 = (f32[272,256]{1,0:T(8,128)S(1)}, f32[272,256]{1,0:T(8,128)S(1)}, u32[]{:S(2)}, u32[]{:S(2)}) collective-permute-start(f32[272,256]{1,0:T(8,128)S(1)} %pad_maximum_fusion.2.refs_12_.refs_3_), channel_id=1, source_target_pairs={{0,1},{1,0},{2,3},{3,2},{4,5},{5,4},{6,7},{7,6},{8,9},{9,8},{10,11... | collective-permute-start | bytes 835592 | tf_op jit(solution)/shard_map/ppermute | solution.py:261
  61.8 9.1 %collective-permute-start.5 = (f32[272,256]{1,0:T(8,128)S(1)}, f32[272,256]{1,0:T(8,128)S(1)}, u32[]{:S(2)}, u32[]{:S(2)}) collective-permute-start(f32[272,256]{1,0:T(8,128)S(1)} %collective-permute-done.3.refs_12_.refs_4_), channel_id=1, source_target_pairs={{0,1},{1,0},{2,3},{3,2},{4,5},{5,4},{6,7},{7,6},{8,9},{9,8},{10,11... | collective-permute-start | bytes 835592 | tf_op jit(solution)/shard_map/ppermute | solution.py:261
  63.3 13.3 %collective-permute-start.19 = (f32[128,256]{1,0:T(8,128)S(1)}, f32[128,256]{1,0:T(8,128)S(1)}, u32[]{:S(2)}, u32[]{:S(2)}) collective-permute-start(f32[128,256]{1,0:T(8,128)S(1)} %get-tuple-element.44), channel_id=1, source_target_pairs={{0,2},{1,3},{2,0},{3,1},{4,6},{5,7},{6,4},{7,5},{8,10},{9,11},{10,... | collective-permute-start | bytes 393224 | tf_op jit(solution)/shard_map/ppermute | solution.py:261
  68.5 12.4 %collective-permute-start.20 = (f32[128,256]{1,0:T(8,128)S(1)}, f32[128,256]{1,0:T(8,128)S(1)}, u32[]{:S(2)}, u32[]{:S(2)}) collective-permute-start(f32[128,256]{1,0:T(8,128)S(1)} %get-tuple-element.46), channel_id=1, source_target_pairs={{0,4},{1,5},{2,6},{3,7},{4,0},{5,1},{6,2},{7,3},{8,12},{9,13},{10,... | collective-permute-start | bytes 393224 | tf_op jit(solution)/shard_map/ppermute | solution.py:261
  68.5 12.4 %collective-permute-start.21 = (f32[128,256]{1,0:T(8,128)S(1)}, f32[128,256]{1,0:T(8,128)S(1)}, u32[]{:S(2)}, u32[]{:S(2)}) collective-permute-start(f32[128,256]{1,0:T(8,128)S(1)} %get-tuple-element.45), channel_id=1, source_target_pairs={{0,6},{1,7},{2,4},{3,5},{4,2},{5,3},{6,0},{7,1},{8,14},{9,15},{10,... | collective-permute-start | bytes 393224 | tf_op jit(solution)/shard_map/ppermute | solution.py:261
  82.5 2.0 %collective-permute-start.22 = (f32[512,256]{1,0:T(8,128)S(1)}, f32[512,256]{1,0:T(8,128)S(1)}, u32[]{:S(2)}, u32[]{:S(2)}) collective-permute-start(f32[512,256]{1,0:T(8,128)S(1)} %get-tuple-element.36), channel_id=1, source_target_pairs={{0,1},{1,0},{2,3},{3,2},{4,5},{5,4},{6,7},{7,6},{8,9},{9,8},{10,11... | collective-permute-start | bytes 1572872 | tf_op jit(solution)/shard_map/ppermute | solution.py:261
  84.5 21.8 %collective-permute-start.23 = (f32[256,256]{1,0:T(8,128)S(1)}, f32[256,256]{1,0:T(8,128)S(1)}, u32[]{:S(2)}, u32[]{:S(2)}) collective-permute-start(f32[256,256]{1,0:T(8,128)S(1)} %slice.141), channel_id=1, source_target_pairs={{0,2},{1,3},{2,0},{3,1},{4,6},{5,7},{6,4},{7,5},{8,10},{9,11},{10,... | collective-permute-start | bytes 786440 | tf_op jit(solution)/shard_map/ppermute | solution.py:261
  92.1 13.1 %collective-permute-start.24 = (f32[128,256]{1,0:T(8,128)S(1)}, f32[128,256]{1,0:T(8,128)S(1)}, u32[]{:S(2)}, u32[]{:S(2)}) collective-permute-start(f32[128,256]{1,0:T(8,128)S(1)} %fusion.3.refs_12_), channel_id=1, source_target_pairs={{0,0},{2,8},{4,16},{6,24},{8,1},{10,9},{12,17},{14,25},{16,2},{18,... | collective-permute-start | bytes 393224 | tf_op jit(solution)/shard_map/ppermute | solution.py:258
  98.8 7.5 %collective-permute-start.25 = (f32[128,256]{1,0:T(8,128)S(1)}, f32[128,256]{1,0:T(8,128)S(1)}, u32[]{:S(2)}, u32[]{:S(2)}) collective-permute-start(f32[128,256]{1,0:T(8,128)S(1)} %fusion.3.refs_12_), channel_id=1, source_target_pairs={{1,0},{3,8},{5,16},{7,24},{9,1},{11,9},{13,17},{15,25},{17,2},{19,... | collective-permute-start | bytes 393224 | tf_op jit(solution)/shard_map/ppermute | solution.py:258
  106.4 14.1 %collective-permute-start.26 = (f32[520,256]{1,0:T(8,128)S(1)}, f32[520,256]{1,0:T(8,128)S(1)}, u32[]{:S(2)}, u32[]{:S(2)}) collective-permute-start(f32[520,256]{1,0:T(8,128)S(1)} %get-tuple-element.51), channel_id=1, source_target_pairs={{0,8},{8,0},{16,24},{24,16},{1,9},{9,1},{17,25},{25,17},{2,10},{10... | collective-permute-start | bytes 1597448 | tf_op jit(solution)/shard_map/ppermute | solution.py:261
  106.5 25.3 %collective-permute-start.28 = (f32[520,256]{1,0:T(8,128)S(1)}, f32[520,256]{1,0:T(8,128)S(1)}, u32[]{:S(2)}, u32[]{:S(2)}) collective-permute-start(f32[520,256]{1,0:T(8,128)S(1)} %get-tuple-element.52), channel_id=1, source_target_pairs={{0,16},{8,24},{16,0},{24,8},{1,17},{9,25},{17,1},{25,9},{2,18},{10... | collective-permute-start | bytes 1597448 | tf_op jit(solution)/shard_map/ppermute | solution.py:261
  119.5 14.2 %collective-permute-start.30 = (f32[128,256]{1,0:T(8,128)S(1)}, f32[128,256]{1,0:T(8,128)S(1)}, u32[]{:S(2)}, u32[]{:S(2)}) collective-permute-start(f32[128,256]{1,0:T(8,128)S(1)} %slice.151), channel_id=1, source_target_pairs={{0,4},{1,5},{2,6},{3,7},{4,0},{5,1},{6,2},{7,3},{8,12},{9,13},{10,... | collective-permute-start | bytes 393224 | tf_op jit(solution)/shard_map/ppermute | solution.py:261
  120.6 17.2 %collective-permute-start.27 = (f32[256,256]{1,0:T(8,128)S(1)}, f32[256,256]{1,0:T(8,128)S(1)}, u32[]{:S(2)}, u32[]{:S(2)}) collective-permute-start(f32[256,256]{1,0:T(8,128)S(1)} %slice_add_fusion.3), channel_id=1, source_target_pairs={{0,16},{8,24},{16,0},{24,8},{1,17},{9,25},{17,1},{25,9},{2,18},{10... | collective-permute-start | bytes 786440 | tf_op jit(solution)/shard_map/ppermute | solution.py:261
  131.8 8.1 %collective-permute-start.29 = (f32[256,256]{1,0:T(8,128)S(1)}, f32[256,256]{1,0:T(8,128)S(1)}, u32[]{:S(2)}, u32[]{:S(2)}) collective-permute-start(f32[256,256]{1,0:T(8,128)S(1)} %slice_add_fusion.2), channel_id=1, source_target_pairs={{0,8},{8,0},{16,24},{24,16},{1,9},{9,1},{17,25},{25,17},{2,10},{10... | collective-permute-start | bytes 786440 | tf_op jit(solution)/shard_map/ppermute | solution.py:261
  133.6 14.4 %collective-permute-start.31 = (f32[128,256]{1,0:T(8,128)S(1)}, f32[128,256]{1,0:T(8,128)S(1)}, u32[]{:S(2)}, u32[]{:S(2)}) collective-permute-start(f32[128,256]{1,0:T(8,128)S(1)} %slice_add_fusion.5), channel_id=1, source_target_pairs={{0,0},{2,8},{4,16},{6,24},{8,1},{10,9},{12,17},{14,25},{16,2},{18,... | collective-permute-start | bytes 393224 | tf_op jit(solution)/shard_map/ppermute | solution.py:258
  135.6 13.2 %collective-permute-start.32 = (f32[128,256]{1,0:T(8,128)S(1)}, f32[128,256]{1,0:T(8,128)S(1)}, u32[]{:S(2)}, u32[]{:S(2)}) collective-permute-start(f32[128,256]{1,0:T(8,128)S(1)} %slice_add_fusion.5), channel_id=1, source_target_pairs={{1,0},{3,8},{5,16},{7,24},{9,1},{11,9},{13,17},{15,25},{17,2},{19,... | collective-permute-start | bytes 393224 | tf_op jit(solution)/shard_map/ppermute | solution.py:258
  (4 other events, 100.2 us)

commit v7 on v4

--- a/solution.py
+++ b/solution.py
@@ -344,12 +344,14 @@
     outs = grads(1, tiles=tiles[:-1], vectors=vectors, held=[*columns, outs[2]], row_in=None, ready=[first_summed])
     outs = grads(1, tiles=tiles[-1:], vectors=vectors, held=[*columns, outs[1]], row_in=outs[0], ready=[first_total])
     second_summed, second_total = from_line(outs)
+    first_quarters = to_home(first_total)
+    quarters = first_quarters + to_home(second_total)
+
     halves = outs[2:]
     if groups == 4:
-        spare = second_summed[:PAD]
+        spare = second_summed[:PAD] + first_quarters[0][:PAD] + first_quarters[1][:PAD]
         first_x = row_swapped(jnp.concatenate([halves[2], halves[6], spare], axis=0), 1)[: 2 * half]
         first_y = row_swapped(jnp.concatenate([halves[5], halves[7], spare], axis=0), 2)[: 2 * half]
-        waited = [first_x[:PAD], first_y[:PAD]]
         second_x = row_swapped(halves[3] + first_y[half:], 1)
         second_y = row_swapped(halves[4] + first_x[half:], 2)
         top = halves[0] + first_x[:half] + second_y
@@ -359,9 +361,6 @@
         for m in range(1, groups):
             top = top + row_swapped(halves[2 * m], m)
             bottom = bottom + row_swapped(halves[2 * m + 1], m)
-        waited = []
-    homes = to_home(jnp.concatenate([first_total, second_total, *waited], axis=0))
-    quarters = [home[at : at + quarter] for at in (0, quarter) for home in homes]
     gradients = (jnp.concatenate([top, bottom], axis=0) + jnp.concatenate(quarters, axis=0)) / BLOCK
     new_accum = accum + gradients * gradients
     new_embed = embed - LEARN_RATE * gradients / jnp.sqrt(new_accum)

time: 153 us -> 147 us (0.961)
  waiting for transfers between devices: 62 us -> 45.4 us
  starting transfers between devices: 66 us -> 75.3 us
    ppermute x26, waiting for transfers between devices: 40.4 us -> 27.6 us  [swapped(): lax.ppermute(value, axis, [(r, r ^ m) for r in range(lax.axis_size(axis))])]
    ppermute x6 -> x8, starting transfers between devices: 15.6 us -> 23.6 us  [permute(): return lax.ppermute(value, both, pairs)]
    ppermute x6 -> x8, waiting for transfers between devices: 21.6 us -> 17.8 us  [permute(): return lax.ppermute(value, both, pairs)]
  transfers between devices with their start and end apart: 32 -> 34, of which waited for: 15 -> 15; matrix products, arithmetic and copies ran while one was open for 3% -> 4% of each run, Pallas kernels for 8% -> 8%
where the time goes in v7:
time: 147 us; the launch traced here: 145 us
  starting transfers between devices  75.3 us (51%)
  waiting for transfers between devices  45.4 us (31%)
  Pallas kernels  14.5 us (10%)
  other arithmetic  6.32 us (4%)
  local copies, waits for them, and re-layouts  2.42 us (2%)
    ppermute x26, starting transfers between devices, swapped(): lax.ppermute(value, axis, [(r, r ^ m) for r in range(lax.axis_size(axis))])  51.6 us
    ppermute x26, waiting for transfers between devices, swapped(): lax.ppermute(value, axis, [(r, r ^ m) for r in range(lax.axis_size(axis))])  27.6 us
    ppermute x8, starting transfers between devices, permute(): return lax.ppermute(value, both, pairs)  23.6 us
    ppermute x8, waiting for transfers between devices, permute(): return lax.ppermute(value, both, pairs)  17.8 us
    pallas_call x4, Pallas kernels, half_grads(): pl.pallas_call(functools.partial(half_kernel, k, groups, share, layout, t...  14.5 us
  transfers between devices with their start and end apart: 34, of which 15 were waited for; matrix products, arithmetic and copies ran while one was open for 4% of the time, Pallas kernels for 8%

profile of v7, /device:TPU:2, one launch (start us, length us, event | category | flops | bytes accessed | tf_op | source)
XLA Modules:
  0.0 145.1 jit_solution(10066893607909436024)
XLA Ops:
  3.0 1.6 %collective-permute-start.6 = (f32[520,256]{1,0:T(8,128)S(1)}, f32[520,256]{1,0:T(8,128)S(1)}, u32[]{:S(2)}, u32[]{:S(2)}) collective-permute-start(f32[520,256]{1,0:T(8,128)S(1)} %select_maximum_fusion.refs_7_), channel_id=1, source_target_pairs={{0,16},{8,24},{16,0},{24,8},{1,17},{9,25},{17,1},{25,9},{2,18},{10... | collective-permute-start | bytes 1597448 | tf_op jit(solution)/shard_map/ppermute | solution.py:261
  5.8 1.6 %collective-permute-start.8 = (f32[8,128]{1,0:T(8,128)S(1)}, f32[8,128]{1,0:T(8,128)S(1)}, u32[]{:S(2)}, u32[]{:S(2)}) collective-permute-start(f32[8,128]{1,0:T(8,128)S(1)} %broadcast_in_dim.8), channel_id=1, source_target_pairs={{0,8},{8,0},{16,24},{24,16},{1,9},{9,1},{17,25},{25,17},{2,10},{10... | collective-permute-start | bytes 12296 | tf_op jit(solution)/shard_map/ppermute | solution.py:261
  8.5 3.5 %collective-permute-start.10 = (f32[136,256]{1,0:T(8,128)S(1)}, f32[136,256]{1,0:T(8,128)S(1)}, u32[]{:S(2)}, u32[]{:S(2)}) collective-permute-start(f32[136,256]{1,0:T(8,128)S(1)} %select_maximum_fusion.2), channel_id=1, source_target_pairs={{0,0},{8,2},{16,4},{24,6},{1,8},{9,10},{17,12},{25,14},{2,16},{10,... | collective-permute-start | bytes 417800 | tf_op jit(solution)/shard_map/ppermute | solution.py:258
  12.0 3.0 %collective-permute-start.11 = (f32[136,256]{1,0:T(8,128)S(1)}, f32[136,256]{1,0:T(8,128)S(1)}, u32[]{:S(2)}, u32[]{:S(2)}) collective-permute-start(f32[136,256]{1,0:T(8,128)S(1)} %select_maximum_fusion.1), channel_id=1, source_target_pairs={{0,1},{8,3},{16,5},{24,7},{1,9},{9,11},{17,13},{25,15},{2,17},{10,... | collective-permute-start | bytes 417800 | tf_op jit(solution)/shard_map/ppermute | solution.py:258
  15.0 7.0 %collective-permute-done.8 = f32[8,128]{1,0:T(8,128)S(1)} collective-permute-done((f32[8,128]{1,0:T(8,128)S(1)}, f32[8,128]{1,0:T(8,128)S(1)}, u32[]{:S(2)}, u32[]{:S(2)}) %collective-permute-start.8) | collective-permute-done | bytes 4128 | tf_op jit(solution)/shard_map/ppermute | solution.py:261
  22.8 3.6 %collective-permute-done.9 = f32[8,128]{1,0:T(8,128)S(1)} collective-permute-done((f32[8,128]{1,0:T(8,128)S(1)}, f32[8,128]{1,0:T(8,128)S(1)}, u32[]{:S(2)}, u32[]{:S(2)}) %collective-permute-start.9) | collective-permute-done | bytes 4128 | tf_op jit(solution)/shard_map/ppermute | solution.py:261
  28.6 3.4 %collective-permute-start.14 = (f32[136,256]{1,0:T(8,128)S(1)}, f32[136,256]{1,0:T(8,128)S(1)}, u32[]{:S(2)}, u32[]{:S(2)}) collective-permute-start(f32[136,256]{1,0:T(8,128)S(1)} %fusion.1), channel_id=1, source_target_pairs={{0,4},{1,5},{2,6},{3,7},{4,0},{5,1},{6,2},{7,3},{8,12},{9,13},{10,... | collective-permute-start | bytes 417800 | tf_op jit(solution)/shard_map/ppermute | solution.py:261
  32.0 1.9 %collective-permute-start = (f32[136,256]{1,0:T(8,128)S(1)}, f32[136,256]{1,0:T(8,128)S(1)}, u32[]{:S(2)}, u32[]{:S(2)}) collective-permute-start(f32[136,256]{1,0:T(8,128)S(1)} %select_maximum_fusion.4), channel_id=1, source_target_pairs={{0,0},{8,2},{16,4},{24,6},{1,8},{9,10},{17,12},{25,14},{2,16},{10,... | collective-permute-start | bytes 417800 | tf_op jit(solution)/shard_map/ppermute | solution.py:258
  33.9 4.0 %collective-permute-start.1 = (f32[136,256]{1,0:T(8,128)S(1)}, f32[136,256]{1,0:T(8,128)S(1)}, u32[]{:S(2)}, u32[]{:S(2)}) collective-permute-start(f32[136,256]{1,0:T(8,128)S(1)} %select_maximum_fusion.3), channel_id=1, source_target_pairs={{0,1},{8,3},{16,5},{24,7},{1,9},{9,11},{17,13},{25,15},{2,17},{10,... | collective-permute-start | bytes 417800 | tf_op jit(solution)/shard_map/ppermute | solution.py:258
  39.9 2.2 %collective-permute-done.1 = f32[136,256]{1,0:T(8,128)S(1)} collective-permute-done((f32[136,256]{1,0:T(8,128)S(1)}, f32[136,256]{1,0:T(8,128)S(1)}, u32[]{:S(2)}, u32[]{:S(2)}) %collective-permute-start.1) | collective-permute-done | bytes 139296 | tf_op jit(solution)/shard_map/ppermute | solution.py:258
  42.2 2.0 %collective-permute-start.16 = (f32[272,256]{1,0:T(8,128)S(1)}, f32[272,256]{1,0:T(8,128)S(1)}, u32[]{:S(2)}, u32[]{:S(2)}) collective-permute-start(f32[272,256]{1,0:T(8,128)S(1)} %pad_maximum_fusion.3.refs_3_), channel_id=1, source_target_pairs={{0,1},{1,0},{2,3},{3,2},{4,5},{5,4},{6,7},{7,6},{8,9},{9,8},{10,11... | collective-permute-start | bytes 835592 | tf_op jit(solution)/shard_map/ppermute | solution.py:261
  44.2 3.8 %collective-permute-done.15.refs_4_ = f32[272,256]{1,0:T(8,128)S(1)} collective-permute-done((f32[272,256]{1,0:T(8,128)S(1)}, f32[272,256]{1,0:T(8,128)S(1)}, u32[]{:S(2)}, u32[]{:S(2)}) %collective-permute-start.15) | collective-permute-done | bytes 278560 | tf_op jit(solution)/shard_map/ppermute | solution.py:261
  48.2 3.3 %collective-permute-done.2 = f32[136,256]{1,0:T(8,128)S(1)} collective-permute-done((f32[136,256]{1,0:T(8,128)S(1)}, f32[136,256]{1,0:T(8,128)S(1)}, u32[]{:S(2)}, u32[]{:S(2)}) %collective-permute-start.2) | collective-permute-done | bytes 139296 | tf_op jit(solution)/shard_map/ppermute | solution.py:261
  51.7 6.0 %half_grads.4 = (f32[1024,256]{1,0:T(8,128)S(1)}, bf16[2048,256]{1,0:T(8,128)(2,1)S(1)}, bf16[2048,256]{1,0:T(8,128)(2,1)S(1)}, f32[32,256]{1,0:T(8,128)S(1)}, f32[256,2048]{1,0:T(8,128)S(1)}) custom-call(s32[3]{0:T(128)S(1)} %pad_add_fusion.refs_0_, s32[4]{0:T(128)S(1)} %convert_reduce_fusion.1.refs_1_, s32[2048,2048]{1,0:T(8,128)} %refs_2_.7, ...), custom_call_target="tpu_custom_call" | custom-call | flops 7247757312 | bytes 10485760 | tf_op jit(solution)/shard_map/half_grads/pallas_call | solution.py:228
  57.7 2.6 %collective-permute-done.3.refs_12_.refs_4_ = f32[272,256]{1,0:T(8,128)S(1)} collective-permute-done((f32[272,256]{1,0:T(8,128)S(1)}, f32[272,256]{1,0:T(8,128)S(1)}, u32[]{:S(2)}, u32[]{:S(2)}) %collective-permute-start.3) | collective-permute-done | bytes 278560 | tf_op jit(solution)/shard_map/ppermute | solution.py:261
  61.9 1.3 collective-permute-done.18
  63.3 11.5 %collective-permute-start.19 = (f32[128,256]{1,0:T(8,128)S(1)}, f32[128,256]{1,0:T(8,128)S(1)}, u32[]{:S(2)}, u32[]{:S(2)}) collective-permute-start(f32[128,256]{1,0:T(8,128)S(1)} %get-tuple-element.47), channel_id=1, source_target_pairs={{0,2},{1,3},{2,0},{3,1},{4,6},{5,7},{6,4},{7,5},{8,10},{9,11},{10,... | collective-permute-start | bytes 393224 | tf_op jit(solution)/shard_map/ppermute | solution.py:261
  74.8 2.4 %collective-permute-start.21 = (f32[128,256]{1,0:T(8,128)S(1)}, f32[128,256]{1,0:T(8,128)S(1)}, u32[]{:S(2)}, u32[]{:S(2)}) collective-permute-start(f32[128,256]{1,0:T(8,128)S(1)} %get-tuple-element.48), channel_id=1, source_target_pairs={{0,6},{1,7},{2,4},{3,5},{4,2},{5,3},{6,0},{7,1},{8,14},{9,15},{10,... | collective-permute-start | bytes 393224 | tf_op jit(solution)/shard_map/ppermute | solution.py:261
  77.3 6.0 %half_grads.6 = (f32[1024,256]{1,0:T(8,128)S(1)}, f32[256,2048]{1,0:T(8,128)S(1)}) custom-call(s32[3]{0:T(128)S(1)} %pad_add_fusion.refs_0_, s32[4]{0:T(128)S(1)} %convert_reduce_fusion.1.refs_1_, s32[2048,2048]{1,0:T(8,128)} %refs_2_.7, f32[272,256]{1,0:T(8,128)S(1)} %pad_maximum_fusion.2.refs_12_.refs_3_, ...), custom_call_target="tpu_custom_call" | custom-call | flops 7247757312 | bytes 10485760 | tf_op jit(solution)/shard_map/half_grads/pallas_call | solution.py:228
  83.3 3.2 %collective-permute-done.20 = f32[128,256]{1,0:T(8,128)S(1)} collective-permute-done((f32[128,256]{1,0:T(8,128)S(1)}, f32[128,256]{1,0:T(8,128)S(1)}, u32[]{:S(2)}, u32[]{:S(2)}) %collective-permute-start.20) | collective-permute-done | bytes 131104 | tf_op jit(solution)/shard_map/ppermute | solution.py:261
  86.5 1.5 %half_grads.7 = (f32[512,256]{1,0:T(8,128)S(1)}, f32[512,256]{1,0:T(8,128)S(1)}, f32[256,256]{1,0:T(8,128)S(1)}, f32[256,256]{1,0:T(8,128)S(1)}, f32[256,256]{1,...) custom-call(s32[3]{0:T(128)S(1)} %pad_add_fusion.refs_0_, ...), custom_call_target="tpu_custom_call" | custom-call | flops 2415919104 | bytes 6291456 | tf_op jit(solution)/shard_map/half_grads/pallas_call | solution.py:228
  88.1 6.8 %collective-permute-start.23 = (f32[128,256]{1,0:T(8,128)S(1)}, f32[128,256]{1,0:T(8,128)S(1)}, u32[]{:S(2)}, u32[]{:S(2)}) collective-permute-start(f32[128,256]{1,0:T(8,128)S(1)} %fusion.5.refs_12_), channel_id=1, source_target_pairs={{0,0},{2,8},{4,16},{6,24},{8,1},{10,9},{12,17},{14,25},{16,2},{18,... | collective-permute-start | bytes 393224 | tf_op jit(solution)/shard_map/ppermute | solution.py:258
  94.9 1.3 collective-permute-start.24
  96.3 1.8 %collective-permute-done.23 = f32[128,256]{1,0:T(8,128)S(1)} collective-permute-done((f32[128,256]{1,0:T(8,128)S(1)}, f32[128,256]{1,0:T(8,128)S(1)}, u32[]{:S(2)}, u32[]{:S(2)}) %collective-permute-start.23) | collective-permute-done | bytes 131104 | tf_op jit(solution)/shard_map/ppermute | solution.py:258
  98.1 4.0 %collective-permute-done.24 = f32[128,256]{1,0:T(8,128)S(1)} collective-permute-done((f32[128,256]{1,0:T(8,128)S(1)}, f32[128,256]{1,0:T(8,128)S(1)}, u32[]{:S(2)}, u32[]{:S(2)}) %collective-permute-start.24) | collective-permute-done | bytes 131104 | tf_op jit(solution)/shard_map/ppermute | solution.py:258
  102.3 13.5 %collective-permute-start.27 = (f32[520,256]{1,0:T(8,128)S(1)}, f32[520,256]{1,0:T(8,128)S(1)}, u32[]{:S(2)}, u32[]{:S(2)}) collective-permute-start(f32[520,256]{1,0:T(8,128)S(1)} %get-tuple-element.55), channel_id=1, source_target_pairs={{0,16},{8,24},{16,0},{24,8},{1,17},{9,25},{17,1},{25,9},{2,18},{10... | collective-permute-start | bytes 1597448 | tf_op jit(solution)/shard_map/ppermute | solution.py:261
  115.9 4.3 %collective-permute-start.31 = (f32[128,256]{1,0:T(8,128)S(1)}, f32[128,256]{1,0:T(8,128)S(1)}, u32[]{:S(2)}, u32[]{:S(2)}) collective-permute-start(f32[128,256]{1,0:T(8,128)S(1)} %get-tuple-element.45), channel_id=1, source_target_pairs={{0,6},{1,7},{2,4},{3,5},{4,2},{5,3},{6,0},{7,1},{8,14},{9,15},{10,... | collective-permute-start | bytes 393224 | tf_op jit(solution)/shard_map/ppermute | solution.py:261
  120.3 8.5 %collective-permute-start.26 = (f32[256,256]{1,0:T(8,128)S(1)}, f32[256,256]{1,0:T(8,128)S(1)}, u32[]{:S(2)}, u32[]{:S(2)}) collective-permute-start(f32[256,256]{1,0:T(8,128)S(1)} %slice_add_fusion.2), channel_id=1, source_target_pairs={{0,16},{8,24},{16,0},{24,8},{1,17},{9,25},{17,1},{25,9},{2,18},{10... | collective-permute-start | bytes 786440 | tf_op jit(solution)/shard_map/ppermute | solution.py:261
  129.2 1.9 %collective-permute-start.32 = (f32[128,256]{1,0:T(8,128)S(1)}, f32[128,256]{1,0:T(8,128)S(1)}, u32[]{:S(2)}, u32[]{:S(2)}) collective-permute-start(f32[128,256]{1,0:T(8,128)S(1)} %fusion.3), channel_id=1, source_target_pairs={{0,0},{2,8},{4,16},{6,24},{8,1},{10,9},{12,17},{14,25},{16,2},{18,... | collective-permute-start | bytes 393224 | tf_op jit(solution)/shard_map/ppermute | solution.py:258
  131.1 1.3 collective-permute-start.33
  133.3 1.9 %collective-permute-done.28 = f32[256,256]{1,0:T(8,128)S(1)} collective-permute-done((f32[256,256]{1,0:T(8,128)S(1)}, f32[256,256]{1,0:T(8,128)S(1)}, u32[]{:S(2)}, u32[]{:S(2)}) %collective-permute-start.28) | collective-permute-done | bytes 262176 | tf_op jit(solution)/shard_map/ppermute | solution.py:261
  135.3 7.9 %collective-permute-done.32 = f32[128,256]{1,0:T(8,128)S(1)} collective-permute-done((f32[128,256]{1,0:T(8,128)S(1)}, f32[128,256]{1,0:T(8,128)S(1)}, u32[]{:S(2)}, u32[]{:S(2)}) %collective-permute-start.32) | collective-permute-done | bytes 131104 | tf_op jit(solution)/shard_map/ppermute | solution.py:258
  (84 shorter events, 15.4 us)
Async XLA Ops:
  3.0 24.6 %collective-permute-start.6 = (f32[520,256]{1,0:T(8,128)S(1)}, f32[520,256]{1,0:T(8,128)S(1)}, u32[]{:S(2)}, u32[]{:S(2)}) collective-permute-start(f32[520,256]{1,0:T(8,128)S(1)} %select_maximum_fusion.refs_7_), channel_id=1, source_target_pairs={{0,16},{8,24},{16,0},{24,8},{1,17},{9,25},{17,1},{25,9},{2,18},{10... | collective-permute-start | bytes 1597448 | tf_op jit(solution)/shard_map/ppermute | solution.py:261
  4.6 22.9 %collective-permute-start.7 = (f32[520,256]{1,0:T(8,128)S(1)}, f32[520,256]{1,0:T(8,128)S(1)}, u32[]{:S(2)}, u32[]{:S(2)}) collective-permute-start(f32[520,256]{1,0:T(8,128)S(1)} %select_maximum_fusion.refs_7_), channel_id=1, source_target_pairs={{0,8},{8,0},{16,24},{24,16},{1,9},{9,1},{17,25},{25,17},{2,10},{10... | collective-permute-start | bytes 1597448 | tf_op jit(solution)/shard_map/ppermute | solution.py:261
  5.8 16.2 %collective-permute-start.8 = (f32[8,128]{1,0:T(8,128)S(1)}, f32[8,128]{1,0:T(8,128)S(1)}, u32[]{:S(2)}, u32[]{:S(2)}) collective-permute-start(f32[8,128]{1,0:T(8,128)S(1)} %broadcast_in_dim.8), channel_id=1, source_target_pairs={{0,8},{8,0},{16,24},{24,16},{1,9},{9,1},{17,25},{25,17},{2,10},{10... | collective-permute-start | bytes 12296 | tf_op jit(solution)/shard_map/ppermute | solution.py:261
  8.5 19.2 %collective-permute-start.10 = (f32[136,256]{1,0:T(8,128)S(1)}, f32[136,256]{1,0:T(8,128)S(1)}, u32[]{:S(2)}, u32[]{:S(2)}) collective-permute-start(f32[136,256]{1,0:T(8,128)S(1)} %select_maximum_fusion.2), channel_id=1, source_target_pairs={{0,0},{8,2},{16,4},{24,6},{1,8},{9,10},{17,12},{25,14},{2,16},{10,... | collective-permute-start | bytes 417800 | tf_op jit(solution)/shard_map/ppermute | solution.py:258
  12.0 15.8 %collective-permute-start.11 = (f32[136,256]{1,0:T(8,128)S(1)}, f32[136,256]{1,0:T(8,128)S(1)}, u32[]{:S(2)}, u32[]{:S(2)}) collective-permute-start(f32[136,256]{1,0:T(8,128)S(1)} %select_maximum_fusion.1), channel_id=1, source_target_pairs={{0,1},{8,3},{16,5},{24,7},{1,9},{9,11},{17,13},{25,15},{2,17},{10,... | collective-permute-start | bytes 417800 | tf_op jit(solution)/shard_map/ppermute | solution.py:258
  22.7 3.7 %collective-permute-start.9 = (f32[8,128]{1,0:T(8,128)S(1)}, f32[8,128]{1,0:T(8,128)S(1)}, u32[]{:S(2)}, u32[]{:S(2)}) collective-permute-start(f32[8,128]{1,0:T(8,128)S(1)} %broadcast_add_fusion), channel_id=1, source_target_pairs={{0,16},{8,24},{16,0},{24,8},{1,17},{9,25},{17,1},{25,9},{2,18},{10... | collective-permute-start | bytes 12296 | tf_op jit(solution)/shard_map/ppermute | solution.py:261
  27.6 10.4 %collective-permute-start.13 = (f32[264,256]{1,0:T(8,128)S(1)}, f32[264,256]{1,0:T(8,128)S(1)}, u32[]{:S(2)}, u32[]{:S(2)}) collective-permute-start(f32[264,256]{1,0:T(8,128)S(1)} %slice.135), channel_id=1, source_target_pairs={{0,16},{8,24},{16,0},{24,8},{1,17},{9,25},{17,1},{25,9},{2,18},{10... | collective-permute-start | bytes 811016 | tf_op jit(solution)/shard_map/ppermute | solution.py:261
  27.7 10.3 %collective-permute-start.12 = (f32[256,256]{1,0:T(8,128)S(1)}, f32[256,256]{1,0:T(8,128)S(1)}, u32[]{:S(2)}, u32[]{:S(2)}) collective-permute-start(f32[256,256]{1,0:T(8,128)S(1)} %slice.133), channel_id=1, source_target_pairs={{0,8},{8,0},{16,24},{24,16},{1,9},{9,1},{17,25},{25,17},{2,10},{10... | collective-permute-start | bytes 786440 | tf_op jit(solution)/shard_map/ppermute | solution.py:261
  28.6 9.4 %collective-permute-start.14 = (f32[136,256]{1,0:T(8,128)S(1)}, f32[136,256]{1,0:T(8,128)S(1)}, u32[]{:S(2)}, u32[]{:S(2)}) collective-permute-start(f32[136,256]{1,0:T(8,128)S(1)} %fusion.1), channel_id=1, source_target_pairs={{0,4},{1,5},{2,6},{3,7},{4,0},{5,1},{6,2},{7,3},{8,12},{9,13},{10,... | collective-permute-start | bytes 417800 | tf_op jit(solution)/shard_map/ppermute | solution.py:261
  32.0 7.9 %collective-permute-start = (f32[136,256]{1,0:T(8,128)S(1)}, f32[136,256]{1,0:T(8,128)S(1)}, u32[]{:S(2)}, u32[]{:S(2)}) collective-permute-start(f32[136,256]{1,0:T(8,128)S(1)} %select_maximum_fusion.4), channel_id=1, source_target_pairs={{0,0},{8,2},{16,4},{24,6},{1,8},{9,10},{17,12},{25,14},{2,16},{10,... | collective-permute-start | bytes 417800 | tf_op jit(solution)/shard_map/ppermute | solution.py:258
  33.9 8.1 %collective-permute-start.1 = (f32[136,256]{1,0:T(8,128)S(1)}, f32[136,256]{1,0:T(8,128)S(1)}, u32[]{:S(2)}, u32[]{:S(2)}) collective-permute-start(f32[136,256]{1,0:T(8,128)S(1)} %select_maximum_fusion.3), channel_id=1, source_target_pairs={{0,1},{8,3},{16,5},{24,7},{1,9},{9,11},{17,13},{25,15},{2,17},{10,... | collective-permute-start | bytes 417800 | tf_op jit(solution)/shard_map/ppermute | solution.py:258
  38.0 10.0 %collective-permute-start.15 = (f32[272,256]{1,0:T(8,128)S(1)}, f32[272,256]{1,0:T(8,128)S(1)}, u32[]{:S(2)}, u32[]{:S(2)}) collective-permute-start(f32[272,256]{1,0:T(8,128)S(1)} %pad_maximum_fusion.3.refs_3_), channel_id=1, source_target_pairs={{0,2},{1,3},{2,0},{3,1},{4,6},{5,7},{6,4},{7,5},{8,10},{9,11},{10,... | collective-permute-start | bytes 835592 | tf_op jit(solution)/shard_map/ppermute | solution.py:261
  42.1 9.5 %collective-permute-start.2 = (f32[136,256]{1,0:T(8,128)S(1)}, f32[136,256]{1,0:T(8,128)S(1)}, u32[]{:S(2)}, u32[]{:S(2)}) collective-permute-start(f32[136,256]{1,0:T(8,128)S(1)} %broadcast_select_fusion), channel_id=1, source_target_pairs={{0,4},{1,5},{2,6},{3,7},{4,0},{5,1},{6,2},{7,3},{8,12},{9,13},{10,... | collective-permute-start | bytes 417800 | tf_op jit(solution)/shard_map/ppermute | solution.py:261
  42.2 9.5 %collective-permute-start.16 = (f32[272,256]{1,0:T(8,128)S(1)}, f32[272,256]{1,0:T(8,128)S(1)}, u32[]{:S(2)}, u32[]{:S(2)}) collective-permute-start(f32[272,256]{1,0:T(8,128)S(1)} %pad_maximum_fusion.3.refs_3_), channel_id=1, source_target_pairs={{0,1},{1,0},{2,3},{3,2},{4,5},{5,4},{6,7},{7,6},{8,9},{9,8},{10,11... | collective-permute-start | bytes 835592 | tf_op jit(solution)/shard_map/ppermute | solution.py:261
  51.6 8.7 %collective-permute-start.3 = (f32[272,256]{1,0:T(8,128)S(1)}, f32[272,256]{1,0:T(8,128)S(1)}, u32[]{:S(2)}, u32[]{:S(2)}) collective-permute-start(f32[272,256]{1,0:T(8,128)S(1)} %pad_maximum_fusion.2.refs_12_.refs_3_), channel_id=1, source_target_pairs={{0,2},{1,3},{2,0},{3,1},{4,6},{5,7},{6,4},{7,5},{8,10},{9,11},{10,... | collective-permute-start | bytes 835592 | tf_op jit(solution)/shard_map/ppermute | solution.py:261
  61.3 15.9 %collective-permute-start.4 = (f32[272,256]{1,0:T(8,128)S(1)}, f32[272,256]{1,0:T(8,128)S(1)}, u32[]{:S(2)}, u32[]{:S(2)}) collective-permute-start(f32[272,256]{1,0:T(8,128)S(1)} %pad_maximum_fusion.2.refs_12_.refs_3_), channel_id=1, source_target_pairs={{0,1},{1,0},{2,3},{3,2},{4,5},{5,4},{6,7},{7,6},{8,9},{9,8},{10,11... | collective-permute-start | bytes 835592 | tf_op jit(solution)/shard_map/ppermute | solution.py:261
  61.8 15.4 %collective-permute-start.5 = (f32[272,256]{1,0:T(8,128)S(1)}, f32[272,256]{1,0:T(8,128)S(1)}, u32[]{:S(2)}, u32[]{:S(2)}) collective-permute-start(f32[272,256]{1,0:T(8,128)S(1)} %collective-permute-done.3.refs_12_.refs_4_), channel_id=1, source_target_pairs={{0,1},{1,0},{2,3},{3,2},{4,5},{5,4},{6,7},{7,6},{8,9},{9,8},{10,11... | collective-permute-start | bytes 835592 | tf_op jit(solution)/shard_map/ppermute | solution.py:261
  63.3 20.0 %collective-permute-start.19 = (f32[128,256]{1,0:T(8,128)S(1)}, f32[128,256]{1,0:T(8,128)S(1)}, u32[]{:S(2)}, u32[]{:S(2)}) collective-permute-start(f32[128,256]{1,0:T(8,128)S(1)} %get-tuple-element.47), channel_id=1, source_target_pairs={{0,2},{1,3},{2,0},{3,1},{4,6},{5,7},{6,4},{7,5},{8,10},{9,11},{10,... | collective-permute-start | bytes 393224 | tf_op jit(solution)/shard_map/ppermute | solution.py:261
  74.8 11.7 %collective-permute-start.20 = (f32[128,256]{1,0:T(8,128)S(1)}, f32[128,256]{1,0:T(8,128)S(1)}, u32[]{:S(2)}, u32[]{:S(2)}) collective-permute-start(f32[128,256]{1,0:T(8,128)S(1)} %get-tuple-element.49), channel_id=1, source_target_pairs={{0,4},{1,5},{2,6},{3,7},{4,0},{5,1},{6,2},{7,3},{8,12},{9,13},{10,... | collective-permute-start | bytes 393224 | tf_op jit(solution)/shard_map/ppermute | solution.py:261
  74.8 11.7 %collective-permute-start.21 = (f32[128,256]{1,0:T(8,128)S(1)}, f32[128,256]{1,0:T(8,128)S(1)}, u32[]{:S(2)}, u32[]{:S(2)}) collective-permute-start(f32[128,256]{1,0:T(8,128)S(1)} %get-tuple-element.48), channel_id=1, source_target_pairs={{0,6},{1,7},{2,4},{3,5},{4,2},{5,3},{6,0},{7,1},{8,14},{9,15},{10,... | collective-permute-start | bytes 393224 | tf_op jit(solution)/shard_map/ppermute | solution.py:261
  88.1 8.2 %collective-permute-start.22 = (f32[512,256]{1,0:T(8,128)S(1)}, f32[512,256]{1,0:T(8,128)S(1)}, u32[]{:S(2)}, u32[]{:S(2)}) collective-permute-start(f32[512,256]{1,0:T(8,128)S(1)} %get-tuple-element.36), channel_id=1, source_target_pairs={{0,1},{1,0},{2,3},{3,2},{4,5},{5,4},{6,7},{7,6},{8,9},{9,8},{10,11... | collective-permute-start | bytes 1572872 | tf_op jit(solution)/shard_map/ppermute | solution.py:261
  88.1 10.0 %collective-permute-start.23 = (f32[128,256]{1,0:T(8,128)S(1)}, f32[128,256]{1,0:T(8,128)S(1)}, u32[]{:S(2)}, u32[]{:S(2)}) collective-permute-start(f32[128,256]{1,0:T(8,128)S(1)} %fusion.5.refs_12_), channel_id=1, source_target_pairs={{0,0},{2,8},{4,16},{6,24},{8,1},{10,9},{12,17},{14,25},{16,2},{18,... | collective-permute-start | bytes 393224 | tf_op jit(solution)/shard_map/ppermute | solution.py:258
  94.9 7.2 %collective-permute-start.24 = (f32[128,256]{1,0:T(8,128)S(1)}, f32[128,256]{1,0:T(8,128)S(1)}, u32[]{:S(2)}, u32[]{:S(2)}) collective-permute-start(f32[128,256]{1,0:T(8,128)S(1)} %fusion.5.refs_12_), channel_id=1, source_target_pairs={{1,0},{3,8},{5,16},{7,24},{9,1},{11,9},{13,17},{15,25},{17,2},{19,... | collective-permute-start | bytes 393224 | tf_op jit(solution)/shard_map/ppermute | solution.py:258
  102.2 18.0 %collective-permute-start.25 = (f32[520,256]{1,0:T(8,128)S(1)}, f32[520,256]{1,0:T(8,128)S(1)}, u32[]{:S(2)}, u32[]{:S(2)}) collective-permute-start(f32[520,256]{1,0:T(8,128)S(1)} %get-tuple-element.54), channel_id=1, source_target_pairs={{0,8},{8,0},{16,24},{24,16},{1,9},{9,1},{17,25},{25,17},{2,10},{10... | collective-permute-start | bytes 1597448 | tf_op jit(solution)/shard_map/ppermute | solution.py:261
  102.3 26.5 %collective-permute-start.27 = (f32[520,256]{1,0:T(8,128)S(1)}, f32[520,256]{1,0:T(8,128)S(1)}, u32[]{:S(2)}, u32[]{:S(2)}) collective-permute-start(f32[520,256]{1,0:T(8,128)S(1)} %get-tuple-element.55), channel_id=1, source_target_pairs={{0,16},{8,24},{16,0},{24,8},{1,17},{9,25},{17,1},{25,9},{2,18},{10... | collective-permute-start | bytes 1597448 | tf_op jit(solution)/shard_map/ppermute | solution.py:261
  115.8 13.4 %collective-permute-start.29 = (f32[128,256]{1,0:T(8,128)S(1)}, f32[128,256]{1,0:T(8,128)S(1)}, u32[]{:S(2)}, u32[]{:S(2)}) collective-permute-start(f32[128,256]{1,0:T(8,128)S(1)} %get-tuple-element.44), channel_id=1, source_target_pairs={{0,2},{1,3},{2,0},{3,1},{4,6},{5,7},{6,4},{7,5},{8,10},{9,11},{10,... | collective-permute-start | bytes 393224 | tf_op jit(solution)/shard_map/ppermute | solution.py:261
  115.8 13.3 %collective-permute-start.30 = (f32[128,256]{1,0:T(8,128)S(1)}, f32[128,256]{1,0:T(8,128)S(1)}, u32[]{:S(2)}, u32[]{:S(2)}) collective-permute-start(f32[128,256]{1,0:T(8,128)S(1)} %get-tuple-element.46), channel_id=1, source_target_pairs={{0,4},{1,5},{2,6},{3,7},{4,0},{5,1},{6,2},{7,3},{8,12},{9,13},{10,... | collective-permute-start | bytes 393224 | tf_op jit(solution)/shard_map/ppermute | solution.py:261
  115.9 13.2 %collective-permute-start.31 = (f32[128,256]{1,0:T(8,128)S(1)}, f32[128,256]{1,0:T(8,128)S(1)}, u32[]{:S(2)}, u32[]{:S(2)}) collective-permute-start(f32[128,256]{1,0:T(8,128)S(1)} %get-tuple-element.45), channel_id=1, source_target_pairs={{0,6},{1,7},{2,4},{3,5},{4,2},{5,3},{6,0},{7,1},{8,14},{9,15},{10,... | collective-permute-start | bytes 393224 | tf_op jit(solution)/shard_map/ppermute | solution.py:261
  120.3 13.0 %collective-permute-start.26 = (f32[256,256]{1,0:T(8,128)S(1)}, f32[256,256]{1,0:T(8,128)S(1)}, u32[]{:S(2)}, u32[]{:S(2)}) collective-permute-start(f32[256,256]{1,0:T(8,128)S(1)} %slice_add_fusion.2), channel_id=1, source_target_pairs={{0,16},{8,24},{16,0},{24,8},{1,17},{9,25},{17,1},{25,9},{2,18},{10... | collective-permute-start | bytes 786440 | tf_op jit(solution)/shard_map/ppermute | solution.py:261
  128.8 6.4 %collective-permute-start.28 = (f32[256,256]{1,0:T(8,128)S(1)}, f32[256,256]{1,0:T(8,128)S(1)}, u32[]{:S(2)}, u32[]{:S(2)}) collective-permute-start(f32[256,256]{1,0:T(8,128)S(1)} %slice_add_fusion.1), channel_id=1, source_target_pairs={{0,8},{8,0},{16,24},{24,16},{1,9},{9,1},{17,25},{25,17},{2,10},{10... | collective-permute-start | bytes 786440 | tf_op jit(solution)/shard_map/ppermute | solution.py:261
  129.2 14.0 %collective-permute-start.32 = (f32[128,256]{1,0:T(8,128)S(1)}, f32[128,256]{1,0:T(8,128)S(1)}, u32[]{:S(2)}, u32[]{:S(2)}) collective-permute-start(f32[128,256]{1,0:T(8,128)S(1)} %fusion.3), channel_id=1, source_target_pairs={{0,0},{2,8},{4,16},{6,24},{8,1},{10,9},{12,17},{14,25},{16,2},{18,... | collective-permute-start | bytes 393224 | tf_op jit(solution)/shard_map/ppermute | solution.py:258
  131.1 12.9 %collective-permute-start.33 = (f32[128,256]{1,0:T(8,128)S(1)}, f32[128,256]{1,0:T(8,128)S(1)}, u32[]{:S(2)}, u32[]{:S(2)}) collective-permute-start(f32[128,256]{1,0:T(8,128)S(1)} %fusion.3), channel_id=1, source_target_pairs={{1,0},{3,8},{5,16},{7,24},{9,1},{11,9},{13,17},{15,25},{17,2},{19,... | collective-permute-start | bytes 393224 | tf_op jit(solution)/shard_map/ppermute | solution.py:258
  (5 other events, 92.8 us)

commit v8 on v7

--- a/solution.py
+++ b/solution.py
@@ -9,7 +9,7 @@
 
 BLOCK = 1024
 LEARN_RATE = 0.05
-SUB = 512
+SUB = 1024
 PAD = 8
 VMEM_LIMIT = 42 * 2**20
 

time: 147 us -> 145 us (0.986)
  starting transfers between devices: 75.3 us -> 70.8 us
  waiting for transfers between devices: 45.4 us -> 49.4 us
    ppermute x8, waiting for transfers between devices: 17.8 us -> 21.7 us  [permute(): return lax.ppermute(value, both, pairs)]
    ppermute x8, starting transfers between devices: 23.6 us -> 20.2 us  [permute(): return lax.ppermute(value, both, pairs)]
where the time goes in v8:
time: 145 us; the launch traced here: 144 us
  starting transfers between devices  70.8 us (49%)
  waiting for transfers between devices  49.4 us (34%)
  Pallas kernels  14.3 us (10%)
  other arithmetic  6.32 us (4%)
  local copies, waits for them, and re-layouts  2.42 us (2%)
    ppermute x26, starting transfers between devices, swapped(): lax.ppermute(value, axis, [(r, r ^ m) for r in range(lax.axis_size(axis))])  50.6 us
    ppermute x26, waiting for transfers between devices, swapped(): lax.ppermute(value, axis, [(r, r ^ m) for r in range(lax.axis_size(axis))])  27.7 us
    ppermute x8, waiting for transfers between devices, permute(): return lax.ppermute(value, both, pairs)  21.7 us
    ppermute x8, starting transfers between devices, permute(): return lax.ppermute(value, both, pairs)  20.2 us
    pallas_call x4, Pallas kernels, half_grads(): pl.pallas_call(functools.partial(half_kernel, k, groups, share, layout, t...  14.3 us
  transfers between devices with their start and end apart: 34, of which 15 were waited for; matrix products, arithmetic and copies ran while one was open for 4% of the time, Pallas kernels for 8%

profile of v8, /device:TPU:2, one launch (start us, length us, event | category | flops | bytes accessed | tf_op | source)
XLA Modules:
  0.0 144.3 jit_solution(540385128001910270)
XLA Ops:
  0.6 1.3 convert_reduce_fusion
  3.0 1.6 %collective-permute-start.6 = (f32[520,256]{1,0:T(8,128)S(1)}, f32[520,256]{1,0:T(8,128)S(1)}, u32[]{:S(2)}, u32[]{:S(2)}) collective-permute-start(f32[520,256]{1,0:T(8,128)S(1)} %select_maximum_fusion.refs_7_), channel_id=1, source_target_pairs={{0,16},{8,24},{16,0},{24,8},{1,17},{9,25},{17,1},{25,9},{2,18},{10... | collective-permute-start | bytes 1597448 | tf_op jit(solution)/shard_map/ppermute | solution.py:261
  5.8 1.6 %collective-permute-start.8 = (f32[8,128]{1,0:T(8,128)S(1)}, f32[8,128]{1,0:T(8,128)S(1)}, u32[]{:S(2)}, u32[]{:S(2)}) collective-permute-start(f32[8,128]{1,0:T(8,128)S(1)} %broadcast_in_dim.8), channel_id=1, source_target_pairs={{0,8},{8,0},{16,24},{24,16},{1,9},{9,1},{17,25},{25,17},{2,10},{10... | collective-permute-start | bytes 12296 | tf_op jit(solution)/shard_map/ppermute | solution.py:261
  8.5 3.5 %collective-permute-start.10 = (f32[136,256]{1,0:T(8,128)S(1)}, f32[136,256]{1,0:T(8,128)S(1)}, u32[]{:S(2)}, u32[]{:S(2)}) collective-permute-start(f32[136,256]{1,0:T(8,128)S(1)} %select_maximum_fusion.2), channel_id=1, source_target_pairs={{0,0},{8,2},{16,4},{24,6},{1,8},{9,10},{17,12},{25,14},{2,16},{10,... | collective-permute-start | bytes 417800 | tf_op jit(solution)/shard_map/ppermute | solution.py:258
  12.0 3.0 %collective-permute-start.11 = (f32[136,256]{1,0:T(8,128)S(1)}, f32[136,256]{1,0:T(8,128)S(1)}, u32[]{:S(2)}, u32[]{:S(2)}) collective-permute-start(f32[136,256]{1,0:T(8,128)S(1)} %select_maximum_fusion.1), channel_id=1, source_target_pairs={{0,1},{8,3},{16,5},{24,7},{1,9},{9,11},{17,13},{25,15},{2,17},{10,... | collective-permute-start | bytes 417800 | tf_op jit(solution)/shard_map/ppermute | solution.py:258
  15.0 7.0 %collective-permute-done.8 = f32[8,128]{1,0:T(8,128)S(1)} collective-permute-done((f32[8,128]{1,0:T(8,128)S(1)}, f32[8,128]{1,0:T(8,128)S(1)}, u32[]{:S(2)}, u32[]{:S(2)}) %collective-permute-start.8) | collective-permute-done | bytes 4128 | tf_op jit(solution)/shard_map/ppermute | solution.py:261
  22.8 3.6 %collective-permute-done.9 = f32[8,128]{1,0:T(8,128)S(1)} collective-permute-done((f32[8,128]{1,0:T(8,128)S(1)}, f32[8,128]{1,0:T(8,128)S(1)}, u32[]{:S(2)}, u32[]{:S(2)}) %collective-permute-start.9) | collective-permute-done | bytes 4128 | tf_op jit(solution)/shard_map/ppermute | solution.py:261
  28.6 3.4 %collective-permute-start.14 = (f32[136,256]{1,0:T(8,128)S(1)}, f32[136,256]{1,0:T(8,128)S(1)}, u32[]{:S(2)}, u32[]{:S(2)}) collective-permute-start(f32[136,256]{1,0:T(8,128)S(1)} %fusion.1), channel_id=1, source_target_pairs={{0,4},{1,5},{2,6},{3,7},{4,0},{5,1},{6,2},{7,3},{8,12},{9,13},{10,... | collective-permute-start | bytes 417800 | tf_op jit(solution)/shard_map/ppermute | solution.py:261
  32.0 1.9 %collective-permute-start = (f32[136,256]{1,0:T(8,128)S(1)}, f32[136,256]{1,0:T(8,128)S(1)}, u32[]{:S(2)}, u32[]{:S(2)}) collective-permute-start(f32[136,256]{1,0:T(8,128)S(1)} %select_maximum_fusion.4), channel_id=1, source_target_pairs={{0,0},{8,2},{16,4},{24,6},{1,8},{9,10},{17,12},{25,14},{2,16},{10,... | collective-permute-start | bytes 417800 | tf_op jit(solution)/shard_map/ppermute | solution.py:258
  33.9 4.0 %collective-permute-start.1 = (f32[136,256]{1,0:T(8,128)S(1)}, f32[136,256]{1,0:T(8,128)S(1)}, u32[]{:S(2)}, u32[]{:S(2)}) collective-permute-start(f32[136,256]{1,0:T(8,128)S(1)} %select_maximum_fusion.3), channel_id=1, source_target_pairs={{0,1},{8,3},{16,5},{24,7},{1,9},{9,11},{17,13},{25,15},{2,17},{10,... | collective-permute-start | bytes 417800 | tf_op jit(solution)/shard_map/ppermute | solution.py:258
  39.9 2.2 %collective-permute-done.1 = f32[136,256]{1,0:T(8,128)S(1)} collective-permute-done((f32[136,256]{1,0:T(8,128)S(1)}, f32[136,256]{1,0:T(8,128)S(1)}, u32[]{:S(2)}, u32[]{:S(2)}) %collective-permute-start.1) | collective-permute-done | bytes 139296 | tf_op jit(solution)/shard_map/ppermute | solution.py:258
  42.2 2.0 %collective-permute-start.16 = (f32[272,256]{1,0:T(8,128)S(1)}, f32[272,256]{1,0:T(8,128)S(1)}, u32[]{:S(2)}, u32[]{:S(2)}) collective-permute-start(f32[272,256]{1,0:T(8,128)S(1)} %pad_maximum_fusion.3.refs_3_), channel_id=1, source_target_pairs={{0,1},{1,0},{2,3},{3,2},{4,5},{5,4},{6,7},{7,6},{8,9},{9,8},{10,11... | collective-permute-start | bytes 835592 | tf_op jit(solution)/shard_map/ppermute | solution.py:261
  44.2 3.8 %collective-permute-done.15.refs_4_ = f32[272,256]{1,0:T(8,128)S(1)} collective-permute-done((f32[272,256]{1,0:T(8,128)S(1)}, f32[272,256]{1,0:T(8,128)S(1)}, u32[]{:S(2)}, u32[]{:S(2)}) %collective-permute-start.15) | collective-permute-done | bytes 278560 | tf_op jit(solution)/shard_map/ppermute | solution.py:261
  48.2 3.3 %collective-permute-done.2 = f32[136,256]{1,0:T(8,128)S(1)} collective-permute-done((f32[136,256]{1,0:T(8,128)S(1)}, f32[136,256]{1,0:T(8,128)S(1)}, u32[]{:S(2)}, u32[]{:S(2)}) %collective-permute-start.2) | collective-permute-done | bytes 139296 | tf_op jit(solution)/shard_map/ppermute | solution.py:261
  51.7 5.9 %half_grads.4 = (f32[1024,256]{1,0:T(8,128)S(1)}, bf16[2048,256]{1,0:T(8,128)(2,1)S(1)}, bf16[2048,256]{1,0:T(8,128)(2,1)S(1)}, f32[32,256]{1,0:T(8,128)S(1)}, f32[256,2048]{1,0:T(8,128)S(1)}) custom-call(s32[3]{0:T(128)S(1)} %pad_add_fusion.refs_0_, s32[4]{0:T(128)S(1)} %convert_reduce_fusion.1.refs_1_, s32[2048,2048]{1,0:T(8,128)} %refs_2_.7, ...), custom_call_target="tpu_custom_call" | custom-call | flops 7247757312 | bytes 10485760 | tf_op jit(solution)/shard_map/half_grads/pallas_call | solution.py:228
  57.6 2.7 %collective-permute-done.3.refs_12_.refs_4_ = f32[272,256]{1,0:T(8,128)S(1)} collective-permute-done((f32[272,256]{1,0:T(8,128)S(1)}, f32[272,256]{1,0:T(8,128)S(1)}, u32[]{:S(2)}, u32[]{:S(2)}) %collective-permute-start.3) | collective-permute-done | bytes 278560 | tf_op jit(solution)/shard_map/ppermute | solution.py:261
  61.2 4.2 %collective-permute-start.18 = (f32[512,256]{1,0:T(8,128)S(1)}, f32[512,256]{1,0:T(8,128)S(1)}, u32[]{:S(2)}, u32[]{:S(2)}) collective-permute-start(f32[512,256]{1,0:T(8,128)S(1)} %get-tuple-element.29), channel_id=1, source_target_pairs={{0,1},{1,0},{2,3},{3,2},{4,5},{5,4},{6,7},{7,6},{8,9},{9,8},{10,11... | collective-permute-start | bytes 1572872 | tf_op jit(solution)/shard_map/ppermute | solution.py:261
  67.2 3.7 %collective-permute-start.20 = (f32[128,256]{1,0:T(8,128)S(1)}, f32[128,256]{1,0:T(8,128)S(1)}, u32[]{:S(2)}, u32[]{:S(2)}) collective-permute-start(f32[128,256]{1,0:T(8,128)S(1)} %get-tuple-element.49), channel_id=1, source_target_pairs={{0,4},{1,5},{2,6},{3,7},{4,0},{5,1},{6,2},{7,3},{8,12},{9,13},{10,... | collective-permute-start | bytes 393224 | tf_op jit(solution)/shard_map/ppermute | solution.py:261
  71.6 5.9 %half_grads.6 = (f32[1024,256]{1,0:T(8,128)S(1)}, f32[256,2048]{1,0:T(8,128)S(1)}) custom-call(s32[3]{0:T(128)S(1)} %pad_add_fusion.refs_0_, s32[4]{0:T(128)S(1)} %convert_reduce_fusion.1.refs_1_, s32[2048,2048]{1,0:T(8,128)} %refs_2_.7, f32[272,256]{1,0:T(8,128)S(1)} %pad_maximum_fusion.2.refs_12_.refs_3_, ...), custom_call_target="tpu_custom_call" | custom-call | flops 7247757312 | bytes 10485760 | tf_op jit(solution)/shard_map/half_grads/pallas_call | solution.py:228
  77.5 3.4 %collective-permute-done.20 = f32[128,256]{1,0:T(8,128)S(1)} collective-permute-done((f32[128,256]{1,0:T(8,128)S(1)}, f32[128,256]{1,0:T(8,128)S(1)}, u32[]{:S(2)}, u32[]{:S(2)}) %collective-permute-start.20) | collective-permute-done | bytes 131104 | tf_op jit(solution)/shard_map/ppermute | solution.py:261
  80.9 1.5 %half_grads.7 = (f32[512,256]{1,0:T(8,128)S(1)}, f32[512,256]{1,0:T(8,128)S(1)}, f32[256,256]{1,0:T(8,128)S(1)}, f32[256,256]{1,0:T(8,128)S(1)}, f32[256,256]{1,...) custom-call(s32[3]{0:T(128)S(1)} %pad_add_fusion.refs_0_, ...), custom_call_target="tpu_custom_call" | custom-call | flops 2415919104 | bytes 6291456 | tf_op jit(solution)/shard_map/half_grads/pallas_call | solution.py:228
  82.5 3.0 %collective-permute-start.22 = (f32[512,256]{1,0:T(8,128)S(1)}, f32[512,256]{1,0:T(8,128)S(1)}, u32[]{:S(2)}, u32[]{:S(2)}) collective-permute-start(f32[512,256]{1,0:T(8,128)S(1)} %get-tuple-element.36), channel_id=1, source_target_pairs={{0,1},{1,0},{2,3},{3,2},{4,5},{5,4},{6,7},{7,6},{8,9},{9,8},{10,11... | collective-permute-start | bytes 1572872 | tf_op jit(solution)/shard_map/ppermute | solution.py:261
  85.5 3.4 %collective-permute-start.23 = (f32[128,256]{1,0:T(8,128)S(1)}, f32[128,256]{1,0:T(8,128)S(1)}, u32[]{:S(2)}, u32[]{:S(2)}) collective-permute-start(f32[128,256]{1,0:T(8,128)S(1)} %fusion.5.refs_12_), channel_id=1, source_target_pairs={{0,0},{2,8},{4,16},{6,24},{8,1},{10,9},{12,17},{14,25},{16,2},{18,... | collective-permute-start | bytes 393224 | tf_op jit(solution)/shard_map/ppermute | solution.py:258
  88.9 1.3 collective-permute-start.24
  90.3 8.6 %collective-permute-done.23 = f32[128,256]{1,0:T(8,128)S(1)} collective-permute-done((f32[128,256]{1,0:T(8,128)S(1)}, f32[128,256]{1,0:T(8,128)S(1)}, u32[]{:S(2)}, u32[]{:S(2)}) %collective-permute-start.23) | collective-permute-done | bytes 131104 | tf_op jit(solution)/shard_map/ppermute | solution.py:258
  100.1 14.8 %collective-permute-start.27 = (f32[520,256]{1,0:T(8,128)S(1)}, f32[520,256]{1,0:T(8,128)S(1)}, u32[]{:S(2)}, u32[]{:S(2)}) collective-permute-start(f32[520,256]{1,0:T(8,128)S(1)} %get-tuple-element.55), channel_id=1, source_target_pairs={{0,16},{8,24},{16,0},{24,8},{1,17},{9,25},{17,1},{25,9},{2,18},{10... | collective-permute-start | bytes 1597448 | tf_op jit(solution)/shard_map/ppermute | solution.py:261
  115.0 4.3 %collective-permute-start.31 = (f32[128,256]{1,0:T(8,128)S(1)}, f32[128,256]{1,0:T(8,128)S(1)}, u32[]{:S(2)}, u32[]{:S(2)}) collective-permute-start(f32[128,256]{1,0:T(8,128)S(1)} %get-tuple-element.45), channel_id=1, source_target_pairs={{0,6},{1,7},{2,4},{3,5},{4,2},{5,3},{6,0},{7,1},{8,14},{9,15},{10,... | collective-permute-start | bytes 393224 | tf_op jit(solution)/shard_map/ppermute | solution.py:261
  119.4 8.6 %collective-permute-start.26 = (f32[256,256]{1,0:T(8,128)S(1)}, f32[256,256]{1,0:T(8,128)S(1)}, u32[]{:S(2)}, u32[]{:S(2)}) collective-permute-start(f32[256,256]{1,0:T(8,128)S(1)} %slice_add_fusion.2), channel_id=1, source_target_pairs={{0,16},{8,24},{16,0},{24,8},{1,17},{9,25},{17,1},{25,9},{2,18},{10... | collective-permute-start | bytes 786440 | tf_op jit(solution)/shard_map/ppermute | solution.py:261
  128.4 1.9 %collective-permute-start.32 = (f32[128,256]{1,0:T(8,128)S(1)}, f32[128,256]{1,0:T(8,128)S(1)}, u32[]{:S(2)}, u32[]{:S(2)}) collective-permute-start(f32[128,256]{1,0:T(8,128)S(1)} %fusion.3), channel_id=1, source_target_pairs={{0,0},{2,8},{4,16},{6,24},{8,1},{10,9},{12,17},{14,25},{16,2},{18,... | collective-permute-start | bytes 393224 | tf_op jit(solution)/shard_map/ppermute | solution.py:258
  130.4 1.3 collective-permute-start.33
  132.7 1.8 %collective-permute-done.28 = f32[256,256]{1,0:T(8,128)S(1)} collective-permute-done((f32[256,256]{1,0:T(8,128)S(1)}, f32[256,256]{1,0:T(8,128)S(1)}, u32[]{:S(2)}, u32[]{:S(2)}) %collective-permute-start.28) | collective-permute-done | bytes 262176 | tf_op jit(solution)/shard_map/ppermute | solution.py:261
  134.5 7.9 %collective-permute-done.32 = f32[128,256]{1,0:T(8,128)S(1)} collective-permute-done((f32[128,256]{1,0:T(8,128)S(1)}, f32[128,256]{1,0:T(8,128)S(1)}, u32[]{:S(2)}, u32[]{:S(2)}) %collective-permute-start.32) | collective-permute-done | bytes 131104 | tf_op jit(solution)/shard_map/ppermute | solution.py:258
  (84 shorter events, 16.9 us)
Async XLA Ops:
  3.0 24.6 %collective-permute-start.6 = (f32[520,256]{1,0:T(8,128)S(1)}, f32[520,256]{1,0:T(8,128)S(1)}, u32[]{:S(2)}, u32[]{:S(2)}) collective-permute-start(f32[520,256]{1,0:T(8,128)S(1)} %select_maximum_fusion.refs_7_), channel_id=1, source_target_pairs={{0,16},{8,24},{16,0},{24,8},{1,17},{9,25},{17,1},{25,9},{2,18},{10... | collective-permute-start | bytes 1597448 | tf_op jit(solution)/shard_map/ppermute | solution.py:261
  4.6 22.9 %collective-permute-start.7 = (f32[520,256]{1,0:T(8,128)S(1)}, f32[520,256]{1,0:T(8,128)S(1)}, u32[]{:S(2)}, u32[]{:S(2)}) collective-permute-start(f32[520,256]{1,0:T(8,128)S(1)} %select_maximum_fusion.refs_7_), channel_id=1, source_target_pairs={{0,8},{8,0},{16,24},{24,16},{1,9},{9,1},{17,25},{25,17},{2,10},{10... | collective-permute-start | bytes 1597448 | tf_op jit(solution)/shard_map/ppermute | solution.py:261
  5.8 16.2 %collective-permute-start.8 = (f32[8,128]{1,0:T(8,128)S(1)}, f32[8,128]{1,0:T(8,128)S(1)}, u32[]{:S(2)}, u32[]{:S(2)}) collective-permute-start(f32[8,128]{1,0:T(8,128)S(1)} %broadcast_in_dim.8), channel_id=1, source_target_pairs={{0,8},{8,0},{16,24},{24,16},{1,9},{9,1},{17,25},{25,17},{2,10},{10... | collective-permute-start | bytes 12296 | tf_op jit(solution)/shard_map/ppermute | solution.py:261
  8.5 19.2 %collective-permute-start.10 = (f32[136,256]{1,0:T(8,128)S(1)}, f32[136,256]{1,0:T(8,128)S(1)}, u32[]{:S(2)}, u32[]{:S(2)}) collective-permute-start(f32[136,256]{1,0:T(8,128)S(1)} %select_maximum_fusion.2), channel_id=1, source_target_pairs={{0,0},{8,2},{16,4},{24,6},{1,8},{9,10},{17,12},{25,14},{2,16},{10,... | collective-permute-start | bytes 417800 | tf_op jit(solution)/shard_map/ppermute | solution.py:258
  12.0 15.8 %collective-permute-start.11 = (f32[136,256]{1,0:T(8,128)S(1)}, f32[136,256]{1,0:T(8,128)S(1)}, u32[]{:S(2)}, u32[]{:S(2)}) collective-permute-start(f32[136,256]{1,0:T(8,128)S(1)} %select_maximum_fusion.1), channel_id=1, source_target_pairs={{0,1},{8,3},{16,5},{24,7},{1,9},{9,11},{17,13},{25,15},{2,17},{10,... | collective-permute-start | bytes 417800 | tf_op jit(solution)/shard_map/ppermute | solution.py:258
  27.6 10.4 %collective-permute-start.13 = (f32[264,256]{1,0:T(8,128)S(1)}, f32[264,256]{1,0:T(8,128)S(1)}, u32[]{:S(2)}, u32[]{:S(2)}) collective-permute-start(f32[264,256]{1,0:T(8,128)S(1)} %slice.135), channel_id=1, source_target_pairs={{0,16},{8,24},{16,0},{24,8},{1,17},{9,25},{17,1},{25,9},{2,18},{10... | collective-permute-start | bytes 811016 | tf_op jit(solution)/shard_map/ppermute | solution.py:261
  27.7 10.3 %collective-permute-start.12 = (f32[256,256]{1,0:T(8,128)S(1)}, f32[256,256]{1,0:T(8,128)S(1)}, u32[]{:S(2)}, u32[]{:S(2)}) collective-permute-start(f32[256,256]{1,0:T(8,128)S(1)} %slice.133), channel_id=1, source_target_pairs={{0,8},{8,0},{16,24},{24,16},{1,9},{9,1},{17,25},{25,17},{2,10},{10... | collective-permute-start | bytes 786440 | tf_op jit(solution)/shard_map/ppermute | solution.py:261
  28.6 9.4 %collective-permute-start.14 = (f32[136,256]{1,0:T(8,128)S(1)}, f32[136,256]{1,0:T(8,128)S(1)}, u32[]{:S(2)}, u32[]{:S(2)}) collective-permute-start(f32[136,256]{1,0:T(8,128)S(1)} %fusion.1), channel_id=1, source_target_pairs={{0,4},{1,5},{2,6},{3,7},{4,0},{5,1},{6,2},{7,3},{8,12},{9,13},{10,... | collective-permute-start | bytes 417800 | tf_op jit(solution)/shard_map/ppermute | solution.py:261
  32.0 7.9 %collective-permute-start = (f32[136,256]{1,0:T(8,128)S(1)}, f32[136,256]{1,0:T(8,128)S(1)}, u32[]{:S(2)}, u32[]{:S(2)}) collective-permute-start(f32[136,256]{1,0:T(8,128)S(1)} %select_maximum_fusion.4), channel_id=1, source_target_pairs={{0,0},{8,2},{16,4},{24,6},{1,8},{9,10},{17,12},{25,14},{2,16},{10,... | collective-permute-start | bytes 417800 | tf_op jit(solution)/shard_map/ppermute | solution.py:258
  33.9 8.1 %collective-permute-start.1 = (f32[136,256]{1,0:T(8,128)S(1)}, f32[136,256]{1,0:T(8,128)S(1)}, u32[]{:S(2)}, u32[]{:S(2)}) collective-permute-start(f32[136,256]{1,0:T(8,128)S(1)} %select_maximum_fusion.3), channel_id=1, source_target_pairs={{0,1},{8,3},{16,5},{24,7},{1,9},{9,11},{17,13},{25,15},{2,17},{10,... | collective-permute-start | bytes 417800 | tf_op jit(solution)/shard_map/ppermute | solution.py:258
  38.0 10.0 %collective-permute-start.15 = (f32[272,256]{1,0:T(8,128)S(1)}, f32[272,256]{1,0:T(8,128)S(1)}, u32[]{:S(2)}, u32[]{:S(2)}) collective-permute-start(f32[272,256]{1,0:T(8,128)S(1)} %pad_maximum_fusion.3.refs_3_), channel_id=1, source_target_pairs={{0,2},{1,3},{2,0},{3,1},{4,6},{5,7},{6,4},{7,5},{8,10},{9,11},{10,... | collective-permute-start | bytes 835592 | tf_op jit(solution)/shard_map/ppermute | solution.py:261
  42.1 9.5 %collective-permute-start.2 = (f32[136,256]{1,0:T(8,128)S(1)}, f32[136,256]{1,0:T(8,128)S(1)}, u32[]{:S(2)}, u32[]{:S(2)}) collective-permute-start(f32[136,256]{1,0:T(8,128)S(1)} %broadcast_select_fusion), channel_id=1, source_target_pairs={{0,4},{1,5},{2,6},{3,7},{4,0},{5,1},{6,2},{7,3},{8,12},{9,13},{10,... | collective-permute-start | bytes 417800 | tf_op jit(solution)/shard_map/ppermute | solution.py:261
  42.2 9.5 %collective-permute-start.16 = (f32[272,256]{1,0:T(8,128)S(1)}, f32[272,256]{1,0:T(8,128)S(1)}, u32[]{:S(2)}, u32[]{:S(2)}) collective-permute-start(f32[272,256]{1,0:T(8,128)S(1)} %pad_maximum_fusion.3.refs_3_), channel_id=1, source_target_pairs={{0,1},{1,0},{2,3},{3,2},{4,5},{5,4},{6,7},{7,6},{8,9},{9,8},{10,11... | collective-permute-start | bytes 835592 | tf_op jit(solution)/shard_map/ppermute | solution.py:261
  51.6 8.7 %collective-permute-start.3 = (f32[272,256]{1,0:T(8,128)S(1)}, f32[272,256]{1,0:T(8,128)S(1)}, u32[]{:S(2)}, u32[]{:S(2)}) collective-permute-start(f32[272,256]{1,0:T(8,128)S(1)} %pad_maximum_fusion.2.refs_12_.refs_3_), channel_id=1, source_target_pairs={{0,2},{1,3},{2,0},{3,1},{4,6},{5,7},{6,4},{7,5},{8,10},{9,11},{10,... | collective-permute-start | bytes 835592 | tf_op jit(solution)/shard_map/ppermute | solution.py:261
  61.2 5.8 %collective-permute-start.18 = (f32[512,256]{1,0:T(8,128)S(1)}, f32[512,256]{1,0:T(8,128)S(1)}, u32[]{:S(2)}, u32[]{:S(2)}) collective-permute-start(f32[512,256]{1,0:T(8,128)S(1)} %get-tuple-element.29), channel_id=1, source_target_pairs={{0,1},{1,0},{2,3},{3,2},{4,5},{5,4},{6,7},{7,6},{8,9},{9,8},{10,11... | collective-permute-start | bytes 1572872 | tf_op jit(solution)/shard_map/ppermute | solution.py:261
  65.5 6.1 %collective-permute-start.4 = (f32[272,256]{1,0:T(8,128)S(1)}, f32[272,256]{1,0:T(8,128)S(1)}, u32[]{:S(2)}, u32[]{:S(2)}) collective-permute-start(f32[272,256]{1,0:T(8,128)S(1)} %pad_maximum_fusion.2.refs_12_.refs_3_), channel_id=1, source_target_pairs={{0,1},{1,0},{2,3},{3,2},{4,5},{5,4},{6,7},{7,6},{8,9},{9,8},{10,11... | collective-permute-start | bytes 835592 | tf_op jit(solution)/shard_map/ppermute | solution.py:261
  65.6 6.0 %collective-permute-start.5 = (f32[272,256]{1,0:T(8,128)S(1)}, f32[272,256]{1,0:T(8,128)S(1)}, u32[]{:S(2)}, u32[]{:S(2)}) collective-permute-start(f32[272,256]{1,0:T(8,128)S(1)} %collective-permute-done.3.refs_12_.refs_4_), channel_id=1, source_target_pairs={{0,1},{1,0},{2,3},{3,2},{4,5},{5,4},{6,7},{7,6},{8,9},{9,8},{10,11... | collective-permute-start | bytes 835592 | tf_op jit(solution)/shard_map/ppermute | solution.py:261
  67.1 10.4 %collective-permute-start.19 = (f32[128,256]{1,0:T(8,128)S(1)}, f32[128,256]{1,0:T(8,128)S(1)}, u32[]{:S(2)}, u32[]{:S(2)}) collective-permute-start(f32[128,256]{1,0:T(8,128)S(1)} %get-tuple-element.47), channel_id=1, source_target_pairs={{0,2},{1,3},{2,0},{3,1},{4,6},{5,7},{6,4},{7,5},{8,10},{9,11},{10,... | collective-permute-start | bytes 393224 | tf_op jit(solution)/shard_map/ppermute | solution.py:261
  67.2 13.7 %collective-permute-start.20 = (f32[128,256]{1,0:T(8,128)S(1)}, f32[128,256]{1,0:T(8,128)S(1)}, u32[]{:S(2)}, u32[]{:S(2)}) collective-permute-start(f32[128,256]{1,0:T(8,128)S(1)} %get-tuple-element.49), channel_id=1, source_target_pairs={{0,4},{1,5},{2,6},{3,7},{4,0},{5,1},{6,2},{7,3},{8,12},{9,13},{10,... | collective-permute-start | bytes 393224 | tf_op jit(solution)/shard_map/ppermute | solution.py:261
  70.9 10.0 %collective-permute-start.21 = (f32[128,256]{1,0:T(8,128)S(1)}, f32[128,256]{1,0:T(8,128)S(1)}, u32[]{:S(2)}, u32[]{:S(2)}) collective-permute-start(f32[128,256]{1,0:T(8,128)S(1)} %get-tuple-element.48), channel_id=1, source_target_pairs={{0,6},{1,7},{2,4},{3,5},{4,2},{5,3},{6,0},{7,1},{8,14},{9,15},{10,... | collective-permute-start | bytes 393224 | tf_op jit(solution)/shard_map/ppermute | solution.py:261
  82.5 7.7 %collective-permute-start.22 = (f32[512,256]{1,0:T(8,128)S(1)}, f32[512,256]{1,0:T(8,128)S(1)}, u32[]{:S(2)}, u32[]{:S(2)}) collective-permute-start(f32[512,256]{1,0:T(8,128)S(1)} %get-tuple-element.36), channel_id=1, source_target_pairs={{0,1},{1,0},{2,3},{3,2},{4,5},{5,4},{6,7},{7,6},{8,9},{9,8},{10,11... | collective-permute-start | bytes 1572872 | tf_op jit(solution)/shard_map/ppermute | solution.py:261
  85.5 13.4 %collective-permute-start.23 = (f32[128,256]{1,0:T(8,128)S(1)}, f32[128,256]{1,0:T(8,128)S(1)}, u32[]{:S(2)}, u32[]{:S(2)}) collective-permute-start(f32[128,256]{1,0:T(8,128)S(1)} %fusion.5.refs_12_), channel_id=1, source_target_pairs={{0,0},{2,8},{4,16},{6,24},{8,1},{10,9},{12,17},{14,25},{16,2},{18,... | collective-permute-start | bytes 393224 | tf_op jit(solution)/shard_map/ppermute | solution.py:258
  88.9 11.1 %collective-permute-start.24 = (f32[128,256]{1,0:T(8,128)S(1)}, f32[128,256]{1,0:T(8,128)S(1)}, u32[]{:S(2)}, u32[]{:S(2)}) collective-permute-start(f32[128,256]{1,0:T(8,128)S(1)} %fusion.5.refs_12_), channel_id=1, source_target_pairs={{1,0},{3,8},{5,16},{7,24},{9,1},{11,9},{13,17},{15,25},{17,2},{19,... | collective-permute-start | bytes 393224 | tf_op jit(solution)/shard_map/ppermute | solution.py:258
  100.0 19.3 %collective-permute-start.25 = (f32[520,256]{1,0:T(8,128)S(1)}, f32[520,256]{1,0:T(8,128)S(1)}, u32[]{:S(2)}, u32[]{:S(2)}) collective-permute-start(f32[520,256]{1,0:T(8,128)S(1)} %get-tuple-element.54), channel_id=1, source_target_pairs={{0,8},{8,0},{16,24},{24,16},{1,9},{9,1},{17,25},{25,17},{2,10},{10... | collective-permute-start | bytes 1597448 | tf_op jit(solution)/shard_map/ppermute | solution.py:261
  100.1 27.9 %collective-permute-start.27 = (f32[520,256]{1,0:T(8,128)S(1)}, f32[520,256]{1,0:T(8,128)S(1)}, u32[]{:S(2)}, u32[]{:S(2)}) collective-permute-start(f32[520,256]{1,0:T(8,128)S(1)} %get-tuple-element.55), channel_id=1, source_target_pairs={{0,16},{8,24},{16,0},{24,8},{1,17},{9,25},{17,1},{25,9},{2,18},{10... | collective-permute-start | bytes 1597448 | tf_op jit(solution)/shard_map/ppermute | solution.py:261
  114.9 13.5 %collective-permute-start.29 = (f32[128,256]{1,0:T(8,128)S(1)}, f32[128,256]{1,0:T(8,128)S(1)}, u32[]{:S(2)}, u32[]{:S(2)}) collective-permute-start(f32[128,256]{1,0:T(8,128)S(1)} %get-tuple-element.44), channel_id=1, source_target_pairs={{0,2},{1,3},{2,0},{3,1},{4,6},{5,7},{6,4},{7,5},{8,10},{9,11},{10,... | collective-permute-start | bytes 393224 | tf_op jit(solution)/shard_map/ppermute | solution.py:261
  115.0 13.4 %collective-permute-start.30 = (f32[128,256]{1,0:T(8,128)S(1)}, f32[128,256]{1,0:T(8,128)S(1)}, u32[]{:S(2)}, u32[]{:S(2)}) collective-permute-start(f32[128,256]{1,0:T(8,128)S(1)} %get-tuple-element.46), channel_id=1, source_target_pairs={{0,4},{1,5},{2,6},{3,7},{4,0},{5,1},{6,2},{7,3},{8,12},{9,13},{10,... | collective-permute-start | bytes 393224 | tf_op jit(solution)/shard_map/ppermute | solution.py:261
  115.0 13.3 %collective-permute-start.31 = (f32[128,256]{1,0:T(8,128)S(1)}, f32[128,256]{1,0:T(8,128)S(1)}, u32[]{:S(2)}, u32[]{:S(2)}) collective-permute-start(f32[128,256]{1,0:T(8,128)S(1)} %get-tuple-element.45), channel_id=1, source_target_pairs={{0,6},{1,7},{2,4},{3,5},{4,2},{5,3},{6,0},{7,1},{8,14},{9,15},{10,... | collective-permute-start | bytes 393224 | tf_op jit(solution)/shard_map/ppermute | solution.py:261
  119.4 13.2 %collective-permute-start.26 = (f32[256,256]{1,0:T(8,128)S(1)}, f32[256,256]{1,0:T(8,128)S(1)}, u32[]{:S(2)}, u32[]{:S(2)}) collective-permute-start(f32[256,256]{1,0:T(8,128)S(1)} %slice_add_fusion.2), channel_id=1, source_target_pairs={{0,16},{8,24},{16,0},{24,8},{1,17},{9,25},{17,1},{25,9},{2,18},{10... | collective-permute-start | bytes 786440 | tf_op jit(solution)/shard_map/ppermute | solution.py:261
  128.0 6.4 %collective-permute-start.28 = (f32[256,256]{1,0:T(8,128)S(1)}, f32[256,256]{1,0:T(8,128)S(1)}, u32[]{:S(2)}, u32[]{:S(2)}) collective-permute-start(f32[256,256]{1,0:T(8,128)S(1)} %slice_add_fusion.1), channel_id=1, source_target_pairs={{0,8},{8,0},{16,24},{24,16},{1,9},{9,1},{17,25},{25,17},{2,10},{10... | collective-permute-start | bytes 786440 | tf_op jit(solution)/shard_map/ppermute | solution.py:261
  128.4 14.0 %collective-permute-start.32 = (f32[128,256]{1,0:T(8,128)S(1)}, f32[128,256]{1,0:T(8,128)S(1)}, u32[]{:S(2)}, u32[]{:S(2)}) collective-permute-start(f32[128,256]{1,0:T(8,128)S(1)} %fusion.3), channel_id=1, source_target_pairs={{0,0},{2,8},{4,16},{6,24},{8,1},{10,9},{12,17},{14,25},{16,2},{18,... | collective-permute-start | bytes 393224 | tf_op jit(solution)/shard_map/ppermute | solution.py:258
  130.4 12.9 %collective-permute-start.33 = (f32[128,256]{1,0:T(8,128)S(1)}, f32[128,256]{1,0:T(8,128)S(1)}, u32[]{:S(2)}, u32[]{:S(2)}) collective-permute-start(f32[128,256]{1,0:T(8,128)S(1)} %fusion.3), channel_id=1, source_target_pairs={{1,0},{3,8},{5,16},{7,24},{9,1},{11,9},{13,17},{15,25},{17,2},{19,... | collective-permute-start | bytes 393224 | tf_op jit(solution)/shard_map/ppermute | solution.py:258
  (5 other events, 94.7 us)
